TPU v7x, 32 devices: a whole 2x2x4 slice. The times are simulated.
32 devices in a mesh: img: 2 (over y), row: 4 (over x, core), col: 4 (over z).
Axes of the slice: x: 2, y: 2, z: 4, core: 2. Of those that a mesh axis runs over, the one named last changes fastest.
Arguments:
- latents: bfloat16 [4, 64, 32, 16], P('img', 'row', 'col'), may hold values from -6 to 6
- skip: bfloat16 [4, 64, 32, 1408], P('img', 'row', 'col'), may hold values from -6 to 6
- temb: bfloat16 [4, 1408], P('img'), may hold values from -6 to 6
- text: bfloat16 [4, 333, 1024], P('img'), may hold values from -6 to 6
- text_len: int32 [4, 2], P('img'), may hold values from 1 to 256, as said below
- extent: int32 [4, 2], P('img'), may hold values from 16 to 64, as said below
- embed_weight: bfloat16 [144, 1408], P(None, ('row', 'col')), may hold values from -0.5 to 0.5
- skip_weight: bfloat16 [2816, 1408], P(('row', 'col')), may hold values from -0.109375 to 0.109375
- shift_weight: bfloat16 [1408, 1408], P(('row', 'col')), may hold values from -0.15625 to 0.15625
- qkv_weight: bfloat16 [1408, 4224], P(('row', 'col')), may hold values from -0.15625 to 0.15625
- out_weight: bfloat16 [1408, 1408], P(('row', 'col')), may hold values from -4 to 4
- cross_query: bfloat16 [1408, 1408], P(('row', 'col')), may hold values from -0.15625 to 0.15625
- cross_keys: bfloat16 [1024, 2816], P(None, ('row', 'col')), may hold values from -0.1875 to 0.1875
- cross_out: bfloat16 [1408, 1408], P(('row', 'col')), may hold values from -1.25 to 1.25
- up_weight: bfloat16 [1408, 6144], P(('row', 'col')), may hold values from -0.15625 to 0.15625
- down_weight: bfloat16 [6144, 1408], P(('row', 'col')), may hold values from -0.15625 to 0.15625
- final_weight: bfloat16 [1408, 144], P(('row', 'col')), may hold values from -0.0546875 to 0.0546875
- norm_gain: bfloat16 [3, 1408], P(None, ('row', 'col')), may hold values from 0.5 to 1.5
- norm_shift: bfloat16 [3, 1408], P(None, ('row', 'col')), may hold values from -1.75 to 1.75
- skip_gain: bfloat16 [2816], P(('row', 'col')), may hold values from 0.5 to 1.5
- skip_shift: bfloat16 [2816], P(('row', 'col')), may hold values from -1.75 to 1.75
- head_gain: bfloat16 [352], P(('row', 'col')), may hold values from 0.5 to 1.5
- head_shift: bfloat16 [352], P(('row', 'col')), may hold values from -1.75 to 1.75
- front_biases: bfloat16 [8448], P(('row', 'col')), may hold values from -1.75 to 1.75
- all_biases: bfloat16 [11776], P(('row', 'col')), may hold values from -1.75 to 1.75
- cross_bias: bfloat16 [2816], P(('row', 'col')), may hold values from -1.75 to 1.75
- cotangent: bfloat16 [4, 64, 32, 16], P('img', 'row', 'col'), may hold values from -6 to 6
Outputs:
- out_latents: float32 [4, 64, 32, 16], P('img', 'row', 'col')
- grad_latents: float32 [4, 64, 32, 16], P('img', 'row', 'col')
- grad_skip: float32 [4, 64, 32, 1408], P('img', 'row', 'col')
- grad_embed: float32 [144, 1408], P(None, ('row', 'col'))
- grad_skip_weight: float32 [2816, 1408], P(('row', 'col'))
- grad_shift: float32 [1408, 1408], P(('row', 'col'))
- grad_qkv: float32 [1408, 4224], P(('row', 'col'))
- grad_out: float32 [1408, 1408], P(('row', 'col'))
- grad_cross_query: float32 [1408, 1408], P(('row', 'col'))
- grad_cross_keys: float32 [1024, 2816], P(None, ('row', 'col'))
- grad_cross_out: float32 [1408, 1408], P(('row', 'col'))
- grad_up: float32 [1408, 6144], P(('row', 'col'))
- grad_down: float32 [6144, 1408], P(('row', 'col'))
- grad_final: float32 [1408, 144], P(('row', 'col'))
- grad_norm_gain: float32 [3, 1408], P(None, ('row', 'col'))
- grad_norm_shift: float32 [3, 1408], P(None, ('row', 'col'))
- grad_skip_gain: float32 [2816], P(('row', 'col'))
- grad_skip_shift: float32 [2816], P(('row', 'col'))
- grad_head_gain: float32 [352], P(('row', 'col'))
- grad_head_shift: float32 [352], P(('row', 'col'))
- grad_front_biases: float32 [8448], P(('row', 'col'))
- grad_biases: float32 [11776], P(('row', 'col'))
- grad_cross_bias: float32 [2816], P(('row', 'col'))
Inputs may be any that keep to these rules, and one draw needn't show every extreme that they name: `text_len`: column 0 counts live 77 slots (at most 77), column 1 live mT5 slots; some image has 77 and 256 live tokens, some image a single live 77 token. Each image's extent is either (64, 32) or (32, 16); every aligned block of 2 images holds at least one image of full extent, and some image is of half extent.
All inputs are finite; a program needn't handle non-finite values.
Results may differ from a plain program's by a relative error of at most 0.033.
Values may be sent and summed in bfloat16 or wider, within the bound.
A program may use at most 448 MiB of HBM per device.

v0:
```python
import math

import jax
import jax.numpy as jnp
from jax import lax
from jax.sharding import PartitionSpec as P

D = 1408
HEADS = 16
HD = 88
FF = 6144
CLIP = 77


NORM_EPS = 1e-06
NEG_FILL = -1e30
STEPS = ((-1, -1), (-1, 0), (-1, 1), (0, -1), (0, 0), (0, 1), (1, -1), (1, 0), (1, 1))


def with_halo(block, sides, width):
    for axis, dim in sides:
        count = lax.axis_size(axis)
        forward = [(i, i + 1) for i in range(count - 1)]
        backward = [(target, source) for source, target in forward]
        low = lax.ppermute(
            lax.slice_in_dim(block, block.shape[dim] - width, None, axis=dim), axis, forward
        )
        high = lax.ppermute(lax.slice_in_dim(block, 0, width, axis=dim), axis, backward)
        block = jnp.concatenate([low, block, high], axis=dim)
    return block


def matmul(former, latter):
    return jnp.dot(former, latter, preferred_element_type=jnp.float32)


def matmul_back(former, latter):
    return lax.dot_general(
        former, latter, (((former.ndim - 1,), (1,)), ((), ())), preferred_element_type=jnp.float32
    )


def weight_grad(inputs, grads):
    flat_in = inputs.reshape(-1, inputs.shape[-1])
    flat_grad = grads.reshape(-1, grads.shape[-1])
    return lax.dot_general(
        flat_in, flat_grad, (((0,), (0,)), ((), ())), preferred_element_type=jnp.float32
    )


def column_sum(grads):
    return jnp.sum(grads.astype(jnp.float32).reshape(-1, grads.shape[-1]), axis=0)


def layer_norm(values, scales, offsets):
    centre = values - jnp.mean(values, axis=-1, keepdims=True)
    spread = jnp.mean(centre * centre, axis=-1, keepdims=True)
    return centre * lax.rsqrt(spread + NORM_EPS) * scales + offsets


def head_norm(values, scales, offsets):
    old_shape = values.shape
    per_head = values.reshape(old_shape[:-1] + (old_shape[-1] // HD, HD))
    return layer_norm(per_head, scales, offsets).reshape(old_shape)


def rope_tables(row_place, col_place):
    quarter = HD // 4
    pair_index = jnp.arange(HD, dtype=jnp.int32) // 2
    by_row = pair_index < quarter
    within = jnp.where(by_row, pair_index, pair_index - quarter).astype(jnp.float32)
    frequency = jnp.exp(-math.log(10000.0) * within / quarter)
    places = jnp.where(by_row[None, :], row_place[:, None], col_place[:, None])
    angles = jnp.tile(places * frequency[None, :], (1, HEADS))
    return (jnp.cos(angles), jnp.sin(angles))


def rotate(values, cosine_table, sine_table):
    is_even = jnp.arange(values.shape[-1], dtype=jnp.int32) % 2 == 0
    swapped = jnp.where(is_even, -jnp.roll(values, -1, axis=-1), jnp.roll(values, 1, axis=-1))
    return values * cosine_table + swapped * sine_table


def gather_near(padded, tall, broad):
    return jnp.concatenate(
        [
            padded[..., 1 + step_row : 1 + step_row + tall, 1 + step_col : 1 + step_col + broad, :]
            for step_row, step_col in STEPS
        ],
        axis=-1,
    )


def spread_near(padded, tall, broad, channels):
    result = None
    for number, (step_row, step_col) in enumerate(STEPS):
        portion = padded[
            ...,
            1 - step_row : 1 - step_row + tall,
            1 - step_col : 1 - step_col + broad,
            number * channels : (number + 1) * channels,
        ]
        result = portion if result is None else result + portion
    return result


def split_front(vector):
    cut_points = (0, D, 2 * D, 3 * D, 6 * D)
    return tuple((vector[cut_points[number] : cut_points[number + 1]] for number in range(4)))


def split_back(vector):
    cut_points = (0, D, 2 * D, 3 * D, 3 * D + FF, 4 * D + FF)
    return tuple((vector[cut_points[number] : cut_points[number + 1]] for number in range(5)))


def open_params(full_set):
    (
        embed_full,
        skip_full,
        shift_full,
        qkv_full,
        out_full,
        cross_q_full,
        cross_o_full,
        up_full,
        down_full,
        final_full,
        gain_rows,
        offset_rows,
        skip_gains,
        skip_offsets,
        head_gains,
        head_offsets,
        front_vector,
        bias_vector,
    ) = full_set
    return (
        embed_full,
        skip_full,
        shift_full,
        qkv_full,
        out_full,
        cross_q_full,
        cross_o_full,
        up_full,
        down_full,
        final_full,
        gain_rows.astype(jnp.float32),
        offset_rows.astype(jnp.float32),
        skip_gains.astype(jnp.float32),
        skip_offsets.astype(jnp.float32),
        head_gains.astype(jnp.float32).reshape(4, HD),
        head_offsets.astype(jnp.float32).reshape(4, HD),
        split_front(front_vector.astype(jnp.float32)),
        split_back(bias_vector.astype(jnp.float32)),
    )


def fold_blocks(state_in, first_part, second_part, block_fn):
    piece_len = first_part.shape[1]
    block_len = math.gcd(piece_len, 1024)

    def loop_body(number, state_now):
        offset = number * block_len
        first_block = lax.dynamic_slice_in_dim(first_part, offset, block_len, 1)
        second_block = lax.dynamic_slice_in_dim(second_part, offset, block_len, 1)
        return block_fn(state_now, first_block, second_block, offset)

    return lax.fori_loop(0, piece_len // block_len, loop_body, state_in)


def body(
    latents,
    skip,
    temb,
    text,
    text_len,
    extent,
    embed_weight,
    skip_weight,
    shift_weight,
    qkv_weight,
    out_weight,
    cross_query,
    cross_keys,
    cross_out,
    up_weight,
    down_weight,
    final_weight,
    norm_gain,
    norm_shift,
    skip_gain,
    skip_shift,
    head_gain,
    head_shift,
    front_biases,
    all_biases,
    cross_bias,
    cotangent,
):
    img_count = latents.shape[0]
    tile_rows = latents.shape[1]
    tile_cols = latents.shape[2]
    patch_vals = latents.shape[3]
    tokens = tile_rows * tile_cols
    col_count = lax.axis_size("col")
    row_index = lax.axis_index("row")
    col_index = lax.axis_index("col")
    score_scale = 1.0 / math.sqrt(HD)
    local_rows = row_index * tile_rows + jnp.arange(tile_rows, dtype=jnp.int32)
    local_cols = col_index * tile_cols + jnp.arange(tile_cols, dtype=jnp.int32)
    inside = (
        (local_rows[None, :, None] < extent[:, 0, None, None])
        & (local_cols[None, None, :] < extent[:, 1, None, None])
    ).astype(jnp.float32)
    token_inside = inside.reshape(img_count, tokens, 1)
    own_usable = (inside.reshape(img_count, tokens) > 0.5)[:, None, None, :]
    row_place = jnp.repeat(local_rows, tile_cols).astype(jnp.float32)
    col_place = jnp.tile(local_cols, tile_rows).astype(jnp.float32)
    cosine_table, sine_table = rope_tables(row_place, col_place)

    def rope_norm(values, scales, offsets):
        return rotate(head_norm(values, scales, offsets), cosine_table, sine_table)

    def gelu_tanh(values):
        return jax.nn.gelu(values, approximate=True)

    def key_usable(index_vec):
        device = index_vec // tokens
        within = index_vec % tokens
        grid_row = device // col_count * tile_rows + within // tile_cols
        grid_col = device % col_count * tile_cols + within % tile_cols
        return (grid_row[None, :] < extent[:, 0:1]) & (grid_col[None, :] < extent[:, 1:2])

    full_set = (
        lax.all_gather(embed_weight, ("row", "col"), axis=1, tiled=True),
        lax.all_gather(skip_weight, ("row", "col"), axis=0, tiled=True),
        lax.all_gather(shift_weight, ("row", "col"), axis=0, tiled=True),
        lax.all_gather(qkv_weight, ("row", "col"), axis=0, tiled=True),
        lax.all_gather(out_weight, ("row", "col"), axis=0, tiled=True),
        lax.all_gather(cross_query, ("row", "col"), axis=0, tiled=True),
        lax.all_gather(cross_out, ("row", "col"), axis=0, tiled=True),
        lax.all_gather(up_weight, ("row", "col"), axis=0, tiled=True),
        lax.all_gather(down_weight, ("row", "col"), axis=0, tiled=True),
        lax.all_gather(final_weight, ("row", "col"), axis=0, tiled=True),
        lax.all_gather(norm_gain, ("row", "col"), axis=1, tiled=True),
        lax.all_gather(norm_shift, ("row", "col"), axis=1, tiled=True),
        lax.all_gather(skip_gain, ("row", "col"), axis=0, tiled=True),
        lax.all_gather(skip_shift, ("row", "col"), axis=0, tiled=True),
        lax.all_gather(head_gain, ("row", "col"), axis=0, tiled=True),
        lax.all_gather(head_shift, ("row", "col"), axis=0, tiled=True),
        lax.all_gather(front_biases, ("row", "col"), axis=0, tiled=True),
        lax.all_gather(all_biases, ("row", "col"), axis=0, tiled=True),
    )
    (
        embed_full,
        skip_full,
        shift_full,
        qkv_full,
        out_full,
        cross_q_full,
        cross_o_full,
        up_full,
        down_full,
        final_full,
        gain_rows,
        offset_rows,
        skip_gains,
        skip_offsets,
        head_gains,
        head_offsets,
        front_parts,
        bias_parts,
    ) = open_params(full_set)
    bias_embed, bias_skip, bias_shift, bias_qkv = front_parts
    bias_out, bias_cross_q, bias_cross_o, bias_up, bias_down = bias_parts
    lat_masked = (latents * inside[..., None]).astype(jnp.bfloat16)
    cot_masked = (cotangent * inside[..., None]).astype(jnp.bfloat16)
    rims = with_halo(
        jnp.concatenate([lat_masked, cot_masked], axis=-1), (("row", 1), ("col", 2)), 1
    )
    near = gather_near(rims[..., :patch_vals], tile_rows, tile_cols).reshape(
        img_count, tokens, 9 * patch_vals
    )
    cot_near = gather_near(rims[..., patch_vals:], tile_rows, tile_cols).reshape(
        img_count, tokens, 9 * patch_vals
    )
    embedded = matmul(near, embed_full) + bias_embed
    joined_full = jnp.concatenate(
        [embedded, skip.reshape(img_count, tokens, D).astype(jnp.float32)], axis=-1
    )
    skip_normed, skip_norm_pull = jax.vjp(layer_norm, joined_full, skip_gains, skip_offsets)
    skip_in = skip_normed.astype(jnp.bfloat16)
    resid_in = matmul(skip_in, skip_full) + bias_skip
    time_act = jax.nn.silu(temb.astype(jnp.float32)).astype(jnp.bfloat16)
    shift_rows = matmul(time_act, shift_full) + bias_shift
    self_norm, self_norm_pull = jax.vjp(layer_norm, resid_in, gain_rows[0], offset_rows[0])
    normed = (self_norm + shift_rows[:, None, :]).astype(jnp.bfloat16)
    qkv_rows = matmul(normed, qkv_full) + bias_qkv
    query_rope, query_pull = jax.vjp(rope_norm, qkv_rows[..., :D], head_gains[0], head_offsets[0])
    key_rope, key_pull = jax.vjp(
        rope_norm, qkv_rows[..., D : 2 * D], head_gains[1], head_offsets[1]
    )
    queries = query_rope.astype(jnp.bfloat16)
    key_rows = key_rope.astype(jnp.bfloat16)
    value_rows = qkv_rows[..., 2 * D :].astype(jnp.bfloat16)
    query_heads = queries.reshape(img_count, tokens, HEADS, HD)

    def attend_block(state_in, key_block, value_block, first_index):
        run_max, run_sum, run_acc = state_in
        block_len = key_block.shape[1]
        usable = key_usable(first_index + jnp.arange(block_len, dtype=jnp.int32))[:, None, None, :]
        scores = (
            jnp.einsum(
                "gqhd,gkhd->ghqk",
                query_heads,
                key_block.reshape(img_count, block_len, HEADS, HD),
                preferred_element_type=jnp.float32,
            )
            * score_scale
        )
        new_max = jnp.maximum(run_max, jnp.max(jnp.where(usable, scores, NEG_FILL), axis=-1))
        prob_rows = jnp.where(usable, jnp.exp(scores - new_max[..., None]), 0.0)
        factor = jnp.exp(run_max - new_max)
        run_sum = run_sum * factor + jnp.sum(prob_rows, axis=-1)
        run_acc = run_acc * factor[..., None] + jnp.einsum(
            "ghqk,gkhd->ghqd",
            prob_rows.astype(jnp.bfloat16),
            value_block.reshape(img_count, block_len, HEADS, HD),
            preferred_element_type=jnp.float32,
        )
        return (new_max, run_sum, run_acc)

    start_state = (
        jnp.full((img_count, HEADS, tokens), NEG_FILL, jnp.float32),
        jnp.zeros((img_count, HEADS, tokens), jnp.float32),
        jnp.zeros((img_count, HEADS, tokens, HD), jnp.float32),
    )
    portion = (
        lax.all_gather(key_rows, ("row", "col"), axis=1, tiled=True),
        lax.all_gather(value_rows, ("row", "col"), axis=1, tiled=True),
    )
    run_max, run_sum, run_acc = fold_blocks(start_state, portion[0], portion[1], attend_block)
    log_total = run_max + jnp.log(run_sum)
    attended_heads = jnp.transpose(run_acc / run_sum[..., None], (0, 2, 1, 3))
    attended_low = attended_heads.reshape(img_count, tokens, D).astype(jnp.bfloat16)
    resid_self = resid_in + matmul(attended_low, out_full) + bias_out
    cross_norm, cross_norm_pull = jax.vjp(layer_norm, resid_self, gain_rows[1], offset_rows[1])
    cross_in = cross_norm.astype(jnp.bfloat16)
    cross_rows = matmul(cross_in, cross_q_full) + bias_cross_q
    cross_rope, cross_query_pull = jax.vjp(rope_norm, cross_rows, head_gains[2], head_offsets[2])
    cross_queries = cross_rope.astype(jnp.bfloat16)
    part_width = cross_keys.shape[1]
    part_start = lax.axis_index(("row", "col")) * part_width
    is_key = part_start + jnp.arange(part_width, dtype=jnp.int32) < D

    def text_norm(values, scales, offsets):
        return jnp.where(is_key, head_norm(values, scales, offsets), values)

    text_part = matmul(text, cross_keys) + cross_bias.astype(jnp.float32)
    text_normed, text_pull = jax.vjp(text_norm, text_part, head_gains[3], head_offsets[3])
    text_both = lax.all_gather(text_normed.astype(jnp.bfloat16), ("row", "col"), axis=2, tiled=True)
    text_keys = text_both[..., :D]
    text_values = text_both[..., D:]
    text_count = text.shape[1]
    text_key_heads = text_keys.reshape(img_count, text_count, HEADS, HD)
    text_value_heads = text_values.reshape(img_count, text_count, HEADS, HD)
    places = jnp.arange(text_count, dtype=jnp.int32)
    live = (
        (places[None, :] < text_len[:, 0:1])
        | (places[None, :] >= CLIP) & (places[None, :] < CLIP + text_len[:, 1:2])
    )[:, None, None, :]
    cross_query_heads = cross_queries.reshape(img_count, tokens, HEADS, HD)
    cross_scores = (
        jnp.einsum(
            "gqhd,gkhd->ghqk", cross_query_heads, text_key_heads, preferred_element_type=jnp.float32
        )
        * score_scale
    )
    cross_masked = jnp.where(live, cross_scores, NEG_FILL)
    cross_shifted = jnp.exp(cross_masked - jnp.max(cross_masked, axis=-1, keepdims=True))
    cross_probs = cross_shifted / jnp.sum(cross_shifted, axis=-1, keepdims=True)
    cross_probs_low = cross_probs.astype(jnp.bfloat16)
    cross_mixed = jnp.einsum(
        "ghqk,gkhd->gqhd", cross_probs_low, text_value_heads, preferred_element_type=jnp.float32
    )
    cross_low = cross_mixed.reshape(img_count, tokens, D).astype(jnp.bfloat16)
    resid_cross = resid_self + matmul(cross_low, cross_o_full) + bias_cross_o
    mlp_norm, mlp_norm_pull = jax.vjp(layer_norm, resid_cross, gain_rows[2], offset_rows[2])
    mlp_in = mlp_norm.astype(jnp.bfloat16)
    hidden = matmul(mlp_in, up_full) + bias_up
    gelu_out, gelu_pull = jax.vjp(gelu_tanh, hidden)
    activated = gelu_out.astype(jnp.bfloat16)
    resid_out = resid_cross + matmul(activated, down_full) + bias_down
    resid_low = resid_out.astype(jnp.bfloat16)
    emitted = matmul(resid_low, final_full) * token_inside
    emit_rim = with_halo(
        emitted.reshape(img_count, tile_rows, tile_cols, 9 * patch_vals),
        (("row", 1), ("col", 2)),
        1,
    )
    out_latents = spread_near(emit_rim, tile_rows, tile_cols, patch_vals) * inside[..., None]
    full_set = (
        lax.all_gather(embed_weight, ("row", "col"), axis=1, tiled=True),
        lax.all_gather(skip_weight, ("row", "col"), axis=0, tiled=True),
        lax.all_gather(shift_weight, ("row", "col"), axis=0, tiled=True),
        lax.all_gather(qkv_weight, ("row", "col"), axis=0, tiled=True),
        lax.all_gather(out_weight, ("row", "col"), axis=0, tiled=True),
        lax.all_gather(cross_query, ("row", "col"), axis=0, tiled=True),
        lax.all_gather(cross_out, ("row", "col"), axis=0, tiled=True),
        lax.all_gather(up_weight, ("row", "col"), axis=0, tiled=True),
        lax.all_gather(down_weight, ("row", "col"), axis=0, tiled=True),
        lax.all_gather(final_weight, ("row", "col"), axis=0, tiled=True),
        lax.all_gather(norm_gain, ("row", "col"), axis=1, tiled=True),
        lax.all_gather(norm_shift, ("row", "col"), axis=1, tiled=True),
        lax.all_gather(skip_gain, ("row", "col"), axis=0, tiled=True),
        lax.all_gather(skip_shift, ("row", "col"), axis=0, tiled=True),
        lax.all_gather(head_gain, ("row", "col"), axis=0, tiled=True),
        lax.all_gather(head_shift, ("row", "col"), axis=0, tiled=True),
        lax.all_gather(front_biases, ("row", "col"), axis=0, tiled=True),
        lax.all_gather(all_biases, ("row", "col"), axis=0, tiled=True),
    )
    (
        embed_full,
        skip_full,
        shift_full,
        qkv_full,
        out_full,
        cross_q_full,
        cross_o_full,
        up_full,
        down_full,
        final_full,
        gain_rows,
        offset_rows,
        skip_gains,
        skip_offsets,
        head_gains,
        head_offsets,
        front_parts,
        bias_parts,
    ) = open_params(full_set)
    grad_emitted = (cot_near.astype(jnp.float32) * token_inside).astype(jnp.bfloat16)
    grad_final = weight_grad(resid_low, grad_emitted)
    grad_resid_out = matmul_back(grad_emitted, final_full)
    grad_down_rows = grad_resid_out.astype(jnp.bfloat16)
    grad_down = weight_grad(activated, grad_down_rows)
    bias_down_grad = column_sum(grad_down_rows)
    grad_hidden = gelu_pull(matmul_back(grad_down_rows, down_full))[0].astype(jnp.bfloat16)
    grad_up = weight_grad(mlp_in, grad_hidden)
    bias_up_grad = column_sum(grad_hidden)
    grad_from_mlp, gain_mlp_grad, shift_mlp_grad = mlp_norm_pull(matmul_back(grad_hidden, up_full))
    grad_resid_cross = grad_resid_out + grad_from_mlp
    grad_cross_low = grad_resid_cross.astype(jnp.bfloat16)
    grad_cross_out = weight_grad(cross_low, grad_cross_low)
    bias_cross_o_grad = column_sum(grad_cross_low)
    grad_cross_mixed = matmul_back(grad_cross_low, cross_o_full).astype(jnp.bfloat16)
    grad_mixed_heads = grad_cross_mixed.reshape(img_count, tokens, HEADS, HD)
    grad_text_values = jnp.einsum(
        "ghqk,gqhd->gkhd", cross_probs_low, grad_mixed_heads, preferred_element_type=jnp.float32
    )
    grad_cross_prob = jnp.einsum(
        "gqhd,gkhd->ghqk", grad_mixed_heads, text_value_heads, preferred_element_type=jnp.float32
    )
    grad_cross_scores = (
        cross_probs
        * (grad_cross_prob - jnp.sum(cross_probs * grad_cross_prob, axis=-1, keepdims=True))
    ).astype(jnp.bfloat16)
    grad_cross_queries = (
        jnp.einsum(
            "ghqk,gkhd->gqhd", grad_cross_scores, text_key_heads, preferred_element_type=jnp.float32
        )
        * score_scale
    )
    grad_text_keys = (
        jnp.einsum(
            "ghqk,gqhd->gkhd",
            grad_cross_scores,
            cross_query_heads,
            preferred_element_type=jnp.float32,
        )
        * score_scale
    )
    grad_text_both = jnp.concatenate(
        [
            grad_text_keys.reshape(img_count, text_count, D),
            grad_text_values.reshape(img_count, text_count, D),
        ],
        axis=-1,
    )
    grad_text_part = lax.psum_scatter(
        grad_text_both, ("row", "col"), scatter_dimension=2, tiled=True
    )
    grad_text_lin, head_gain_ck_grad, head_shift_ck_grad = text_pull(grad_text_part)
    grad_text_low = grad_text_lin.astype(jnp.bfloat16)
    grad_keys_local = weight_grad(text, grad_text_low)
    grad_bias_local = column_sum(grad_text_low)
    grad_cross_lin, head_gain_cq_grad, head_shift_cq_grad = cross_query_pull(
        grad_cross_queries.reshape(img_count, tokens, D)
    )
    grad_cross_rows = grad_cross_lin.astype(jnp.bfloat16)
    grad_cross_query = weight_grad(cross_in, grad_cross_rows)
    bias_cross_q_grad = column_sum(grad_cross_rows)
    grad_from_cross, gain_cross_grad, shift_cross_grad = cross_norm_pull(
        matmul_back(grad_cross_rows, cross_q_full)
    )
    grad_resid_self = grad_resid_cross + grad_from_cross
    grad_out_rows = grad_resid_self.astype(jnp.bfloat16)
    grad_out = weight_grad(attended_low, grad_out_rows)
    bias_out_grad = column_sum(grad_out_rows)
    grad_attended = matmul_back(grad_out_rows, out_full).astype(jnp.bfloat16)
    grad_heads = grad_attended.reshape(img_count, tokens, HEADS, HD)
    row_delta = jnp.transpose(
        jnp.sum(grad_heads.astype(jnp.float32) * attended_heads, axis=-1), (0, 2, 1)
    )
    total_all, delta_all = (
        lax.all_gather(log_total, ("row", "col"), axis=2, tiled=True),
        lax.all_gather(row_delta, ("row", "col"), axis=2, tiled=True),
    )

    def query_grad_block(state_in, key_block, value_block, first_index):
        block_len = key_block.shape[1]
        usable = key_usable(first_index + jnp.arange(block_len, dtype=jnp.int32))[:, None, None, :]
        key_heads = key_block.reshape(img_count, block_len, HEADS, HD)
        scores = (
            jnp.einsum(
                "gqhd,gkhd->ghqk", query_heads, key_heads, preferred_element_type=jnp.float32
            )
            * score_scale
        )
        prob_rows = jnp.where(usable, jnp.exp(scores - log_total[..., None]), 0.0)
        grad_prob = jnp.einsum(
            "gqhd,gkhd->ghqk",
            grad_heads,
            value_block.reshape(img_count, block_len, HEADS, HD),
            preferred_element_type=jnp.float32,
        )
        grad_scores = (prob_rows * (grad_prob - row_delta[..., None])).astype(jnp.bfloat16)
        return (
            state_in
            + jnp.einsum(
                "ghqk,gkhd->ghqd", grad_scores, key_heads, preferred_element_type=jnp.float32
            )
            * score_scale
        )

    portion = (
        lax.all_gather(key_rows, ("row", "col"), axis=1, tiled=True),
        lax.all_gather(value_rows, ("row", "col"), axis=1, tiled=True),
    )
    grad_query_heads = fold_blocks(
        jnp.zeros((img_count, HEADS, tokens, HD), jnp.float32),
        portion[0],
        portion[1],
        query_grad_block,
    )
    own_keys = key_rows.reshape(img_count, tokens, HEADS, HD)
    own_values = value_rows.reshape(img_count, tokens, HEADS, HD)

    def key_grad_block(state_in, query_block, grad_block, first_index):
        grad_keys_acc, grad_values_acc = state_in
        block_len = query_block.shape[1]
        total_rows = lax.dynamic_slice_in_dim(total_all, first_index, block_len, 2)
        delta_rows = lax.dynamic_slice_in_dim(delta_all, first_index, block_len, 2)
        query_part = query_block.reshape(img_count, block_len, HEADS, HD)
        grad_part = grad_block.reshape(img_count, block_len, HEADS, HD)
        scores = (
            jnp.einsum("gqhd,gkhd->ghqk", query_part, own_keys, preferred_element_type=jnp.float32)
            * score_scale
        )
        prob_rows = jnp.where(own_usable, jnp.exp(scores - total_rows[..., None]), 0.0)
        grad_values_acc = grad_values_acc + jnp.einsum(
            "ghqk,gqhd->ghkd",
            prob_rows.astype(jnp.bfloat16),
            grad_part,
            preferred_element_type=jnp.float32,
        )
        grad_prob = jnp.einsum(
            "gqhd,gkhd->ghqk", grad_part, own_values, preferred_element_type=jnp.float32
        )
        grad_scores = (prob_rows * (grad_prob - delta_rows[..., None])).astype(jnp.bfloat16)
        grad_keys_acc = (
            grad_keys_acc
            + jnp.einsum(
                "ghqk,gqhd->ghkd", grad_scores, query_part, preferred_element_type=jnp.float32
            )
            * score_scale
        )
        return (grad_keys_acc, grad_values_acc)

    zero_heads = jnp.zeros((img_count, HEADS, tokens, HD), jnp.float32)
    portion = (
        lax.all_gather(queries, ("row", "col"), axis=1, tiled=True),
        lax.all_gather(grad_attended, ("row", "col"), axis=1, tiled=True),
    )
    grad_key_heads, grad_value_heads = fold_blocks(
        (zero_heads, zero_heads), portion[0], portion[1], key_grad_block
    )

    def heads_to_rows(head_major):
        return jnp.transpose(head_major, (0, 2, 1, 3)).reshape(img_count, tokens, D)

    grad_query_lin, head_gain_q_grad, head_shift_q_grad = query_pull(
        heads_to_rows(grad_query_heads)
    )
    grad_key_lin, head_gain_k_grad, head_shift_k_grad = key_pull(heads_to_rows(grad_key_heads))
    grad_qkv_rows = jnp.concatenate(
        [grad_query_lin, grad_key_lin, heads_to_rows(grad_value_heads)], axis=-1
    ).astype(jnp.bfloat16)
    grad_qkv = weight_grad(normed, grad_qkv_rows)
    bias_qkv_grad = column_sum(grad_qkv_rows)
    grad_normed = matmul_back(grad_qkv_rows, qkv_full)
    grad_shift_rows = jnp.sum(grad_normed, axis=1)
    grad_shift = lax.dot_general(
        time_act.astype(jnp.float32),
        grad_shift_rows,
        (((0,), (0,)), ((), ())),
        precision=lax.Precision.HIGHEST,
    )
    bias_shift_grad = jnp.sum(grad_shift_rows, axis=0)
    grad_from_self, gain_self_grad, shift_self_grad = self_norm_pull(grad_normed)
    grad_resid_in = grad_resid_self + grad_from_self
    grad_merged = grad_resid_in.astype(jnp.bfloat16)
    grad_skip_weight = weight_grad(skip_in, grad_merged)
    bias_skip_grad = column_sum(grad_merged)
    grad_skip_normed = matmul_back(grad_merged, skip_full)
    grad_joined, skip_gain_grad, skip_shift_grad = skip_norm_pull(grad_skip_normed)
    grad_skip = grad_joined[..., D:].reshape(img_count, tile_rows, tile_cols, D)
    grad_embedded = grad_joined[..., :D].astype(jnp.bfloat16)
    grad_embed = weight_grad(near, grad_embedded)
    bias_embed_grad = column_sum(grad_embedded)
    grad_near = matmul_back(grad_embedded, embed_full).reshape(
        img_count, tile_rows, tile_cols, 9 * patch_vals
    )
    near_rim = with_halo(grad_near, (("row", 1), ("col", 2)), 1)
    grad_latents = spread_near(near_rim, tile_rows, tile_cols, patch_vals) * inside[..., None]
    gain_grads = jnp.stack([gain_self_grad, gain_cross_grad, gain_mlp_grad])
    shift_grads = jnp.stack([shift_self_grad, shift_cross_grad, shift_mlp_grad])
    head_gain_grads = jnp.concatenate(
        [head_gain_q_grad, head_gain_k_grad, head_gain_cq_grad, head_gain_ck_grad]
    )
    head_shift_grads = jnp.concatenate(
        [head_shift_q_grad, head_shift_k_grad, head_shift_cq_grad, head_shift_ck_grad]
    )
    front_grads = jnp.concatenate([bias_embed_grad, bias_skip_grad, bias_shift_grad, bias_qkv_grad])
    bias_grads = jnp.concatenate(
        [bias_out_grad, bias_cross_q_grad, bias_cross_o_grad, bias_up_grad, bias_down_grad]
    )
    (
        shard_embed,
        shard_skip,
        shard_shift,
        shard_qkv,
        shard_out,
        shard_cross_q,
        shard_cross_o,
        shard_up,
        shard_down,
        shard_final,
        shard_gain,
        shard_offset,
        shard_skip_gain,
        shard_skip_shift,
        shard_head_gain,
        shard_head_shift,
        shard_front,
        shard_biases,
    ) = (
        lax.psum_scatter(grad_embed, ("row", "col"), scatter_dimension=1, tiled=True),
        lax.psum_scatter(grad_skip_weight, ("row", "col"), scatter_dimension=0, tiled=True),
        lax.psum_scatter(grad_shift, ("row", "col"), scatter_dimension=0, tiled=True),
        lax.psum_scatter(grad_qkv, ("row", "col"), scatter_dimension=0, tiled=True),
        lax.psum_scatter(grad_out, ("row", "col"), scatter_dimension=0, tiled=True),
        lax.psum_scatter(grad_cross_query, ("row", "col"), scatter_dimension=0, tiled=True),
        lax.psum_scatter(grad_cross_out, ("row", "col"), scatter_dimension=0, tiled=True),
        lax.psum_scatter(grad_up, ("row", "col"), scatter_dimension=0, tiled=True),
        lax.psum_scatter(grad_down, ("row", "col"), scatter_dimension=0, tiled=True),
        lax.psum_scatter(grad_final, ("row", "col"), scatter_dimension=0, tiled=True),
        lax.psum_scatter(gain_grads, ("row", "col"), scatter_dimension=1, tiled=True),
        lax.psum_scatter(shift_grads, ("row", "col"), scatter_dimension=1, tiled=True),
        lax.psum_scatter(skip_gain_grad, ("row", "col"), scatter_dimension=0, tiled=True),
        lax.psum_scatter(skip_shift_grad, ("row", "col"), scatter_dimension=0, tiled=True),
        lax.psum_scatter(head_gain_grads, ("row", "col"), scatter_dimension=0, tiled=True),
        lax.psum_scatter(head_shift_grads, ("row", "col"), scatter_dimension=0, tiled=True),
        lax.psum_scatter(front_grads, ("row", "col"), scatter_dimension=0, tiled=True),
        lax.psum_scatter(bias_grads, ("row", "col"), scatter_dimension=0, tiled=True),
    )
    (
        total_embed,
        total_skip,
        total_shift,
        total_qkv,
        total_out,
        total_cross_q,
        total_cross_o,
        total_up,
        total_down,
        total_final,
        total_gain,
        total_offset,
        total_skip_gain,
        total_skip_shift,
        total_head_gain,
        total_head_shift,
        total_front,
        total_biases,
        total_cross_keys,
        total_cross_bias,
    ) = lax.psum(
        (
            shard_embed,
            shard_skip,
            shard_shift,
            shard_qkv,
            shard_out,
            shard_cross_q,
            shard_cross_o,
            shard_up,
            shard_down,
            shard_final,
            shard_gain,
            shard_offset,
            shard_skip_gain,
            shard_skip_shift,
            shard_head_gain,
            shard_head_shift,
            shard_front,
            shard_biases,
            grad_keys_local,
            grad_bias_local,
        ),
        "img",
    )
    return (
        out_latents,
        grad_latents,
        grad_skip,
        total_embed,
        total_skip,
        total_shift,
        total_qkv,
        total_out,
        total_cross_q,
        total_cross_keys,
        total_cross_o,
        total_up,
        total_down,
        total_final,
        total_gain,
        total_offset,
        total_skip_gain,
        total_skip_shift,
        total_head_gain,
        total_head_shift,
        total_front,
        total_biases,
        total_cross_bias,
    )


def solution(mesh):
    placed = (
        P("img", "row", "col", None),
        P("img", "row", "col", None),
        P("img", None),
        P("img", None, None),
        P("img", None),
        P("img", None),
        P(None, ("row", "col")),
        P(("row", "col"), None),
        P(("row", "col"), None),
        P(("row", "col"), None),
        P(("row", "col"), None),
        P(("row", "col"), None),
        P(None, ("row", "col")),
        P(("row", "col"), None),
        P(("row", "col"), None),
        P(("row", "col"), None),
        P(("row", "col"), None),
        P(None, ("row", "col")),
        P(None, ("row", "col")),
        P(("row", "col")),
        P(("row", "col")),
        P(("row", "col")),
        P(("row", "col")),
        P(("row", "col")),
        P(("row", "col")),
        P(("row", "col")),
        P("img", "row", "col", None),
    )
    return jax.shard_map(
        body,
        mesh=mesh,
        in_specs=placed,
        out_specs=(
            P("img", "row", "col", None),
            P("img", "row", "col", None),
            P("img", "row", "col", None),
            P(None, ("row", "col")),
            P(("row", "col"), None),
            P(("row", "col"), None),
            P(("row", "col"), None),
            P(("row", "col"), None),
            P(("row", "col"), None),
            P(None, ("row", "col")),
            P(("row", "col"), None),
            P(("row", "col"), None),
            P(("row", "col"), None),
            P(("row", "col"), None),
            P(None, ("row", "col")),
            P(None, ("row", "col")),
            P(("row", "col")),
            P(("row", "col")),
            P(("row", "col")),
            P(("row", "col")),
            P(("row", "col")),
            P(("row", "col")),
            P(("row", "col")),
        ),
        check_vma=False,
    )
```

profile of v0, /device:TPU:0, one launch (start us, length us, event | category | flops | bytes accessed | tf_op | source)
XLA Modules:
  0.0 3396.0 jit_solution(2630109727015675599)
XLA Ops:
  19.3 63.9 %all-reduce.34 = (bf16[8448]{0:T(1024)(128)(2,1)S(1)}, bf16[2816]{0:T(1024)(128)(2,1)S(1)}, bf16[2816]{0:T(1024)(128)(2,1)S(1)}, bf16[352]{0:T(512)(128)(2,1)S(1...) all-reduce(bf16[8448]{0:T(1024)(128)(2,1)S(1)} %dynamic-update-slic, ...), channel_id=1, replica_groups=mesh['img'=2,'row'=4,'col'=4] {'row','col'}, use_global_device_ids=true, to_apply=%add.12 | all-reduce | flops 26560 | bytes 106240
  88.4 41.8 %all-gather = bf16[16,88,144]{1,2,0:T(8,128)(2,1)S(1)} all-gather(bf16[1,88,144]{1,2,0:T(8,128)(2,1)S(1)} %bitcast.459), channel_id=1, replica_groups=mesh['img'=2,'row'=4,'col'=4] {'row','col'}, dimensions={0}, use_global_device_ids=true | all-gather | bytes 430848 | tf_op jit(solution)/shard_map/all_gather | solution.py:237
  131.1 32.2 all-gather.2
  279.8 40.7 %all-gather.3 = bf16[16,88,144]{1,2,0:T(8,128)(2,1)S(1)} all-gather(bf16[1,88,144]{1,2,0:T(8,128)(2,1)S(1)} %bitcast.460), channel_id=1, replica_groups=mesh['img'=2,'row'=4,'col'=4] {'row','col'}, dimensions={0}, use_global_device_ids=true | all-gather | bytes 430848 | tf_op jit(solution)/shard_map/all_gather | solution.py:246
  331.7 61.8 %all-gather.24.cloned.1.call-done = bf16[2,2048,1408]{2,1,0:T(8,128)(2,1)} async-done(((bf16[2,128,1408]{2,1,0:T(8,128)(2,1)}), bf16[2,2048,1408]{2,1,0:T(8,128)(2,1)}) %all-gather.24.cloned.1.call-update) | async-done | bytes 11534352 | tf_op jit(solution)/shard_map/all_gather | solution.py:341
  409.2 79.1 %all-gather.26.cloned.1.call-done = bf16[2,2048,1408]{2,1,0:T(8,128)(2,1)} async-done(((bf16[2,128,1408]{2,1,0:T(8,128)(2,1)}), bf16[2,2048,1408]{2,1,0:T(8,128)(2,1)}) %all-gather.26.cloned.1.call-update) | async-done | bytes 11534352 | tf_op jit(solution)/shard_map/all_gather | solution.py:342
  503.4 73.0 %while.54 = (s32[]{:T(128)}, f32[2,16,128]{2,1,0:T(8,128)S(1)}, f32[2,16,128]{2,1,0:T(8,128)S(1)}, f32[2,16,128,88]{2,3,1,0:T(8,128)S(1)}, s32[2,2]{0,1:T(2,128)...) while((s32[]{:T(128)}, f32[2,16,128]{2,1,0:T(8,128)S(1)}, ...), condition=%wide.region_12.13_spmd.clone, body=%wide.region_9.12_spmd.clone.sunk | while | flops 1523703808 | bytes 111894784 | solution.py:170
  643.4 91.5 %all-gather.36.cloned.1.call-done = bf16[1408,6144]{1,0:T(8,128)(2,1)} async-done(((bf16[88,6144]{1,0:T(8,128)(2,1)}), bf16[1408,6144]{1,0:T(8,128)(2,1)}) %all-gather.36.cloned.1.call-update) | async-done | bytes 17301520 | tf_op jit(solution)/shard_map/all_gather | solution.py:244
  748.5 84.3 %all-gather.38.cloned.1.call-done = bf16[6144,1408]{1,0:T(8,128)(2,1)} async-done(((bf16[384,1408]{1,0:T(8,128)(2,1)}), bf16[6144,1408]{1,0:T(8,128)(2,1)}) %all-gather.38.cloned.1.call-update) | async-done | bytes 17301520 | tf_op jit(solution)/shard_map/all_gather | solution.py:245
  945.3 71.3 %while.55 = (s32[]{:T(128)}, f32[2,16,128,88]{2,3,1,0:T(8,128)}, s32[2,2]{0,1:T(2,128)S(1)}, bf16[2,2048,1408]{1,2,0:T(8,128)(2,1)}, bf16[2,128,16,88]{1,3,2,0:T...) while((s32[]{:T(128)}, f32[2,16,128,88]{2,3,1,0:T(8,128)}, ...), condition=%wide.region_32.33_spmd.clone, body=%wide.region_31.32_spmd.clone.sunk | while | flops 2240909312 | bytes 78303472 | solution.py:170
  1023.3 37.0 %all_gather.108 = f32[2,16,2048]{2,1,0:T(8,128)S(1)} all-gather(f32[2,16,128]{2,1,0:T(8,128)S(1)} %get-tuple-element.1765), channel_id=1, replica_groups=mesh['img'=2,'row'=4,'col'=4] {'row','col'}, dimensions={2}, use_global_device_ids=true | all-gather | bytes 278528 | tf_op jit(solution)/shard_map/all_gather | solution.py:518
  1060.3 37.2 %all_gather.110 = f32[2,16,2048]{2,1,0:T(8,128)} all-gather(f32[2,16,128]{2,1,0:T(8,128)S(1)} %get-tuple-element.1764), channel_id=1, replica_groups=mesh['img'=2,'row'=4,'col'=4] {'row','col'}, dimensions={2}, use_global_device_ids=true | all-gather | bytes 278528 | tf_op jit(solution)/shard_map/all_gather | solution.py:519
  1118.5 82.5 %all-gather.42.cloned.1.call-done = bf16[2,2048,1408]{2,1,0:T(8,128)(2,1)} async-done(((bf16[2,128,1408]{2,1,0:T(8,128)(2,1)}), bf16[2,2048,1408]{2,1,0:T(8,128)(2,1)}) %all-gather.42.cloned.1.call-update) | async-done | bytes 11534352 | tf_op jit(solution)/shard_map/all_gather | solution.py:595
  1200.9 140.1 %while.56 = (s32[]{:T(128)}, f32[2,16,128,88]{2,3,1,0:T(8,128)S(1)}, f32[2,16,128,88]{2,3,1,0:T(8,128)}, bf16[2,2048,1408]{2,1,0:T(8,128)(2,1)}, bf16[2,128,16,8...) while((s32[]{:T(128)}, ...), condition=%wide.region_36.37_spmd.clone, body=%wide.region_35.36_spmd.clone.sunk | while | flops 2996536064 | bytes 148375120 | solution.py:170
  1528.2 46.4 %reduce-scatter.36.cloned.1.call-done = f32[88,144]{1,0:T(8,128)} async-done(((f32[1408,144]{1,0:T(8,128)}), f32[88,144]{1,0:T(8,128)}) %reduce-scatter.36.cloned.1.call-update) | async-done | bytes 50704
  1577.8 103.3 %reduce-scatter.44.cloned.1.call-done = f32[88,1408]{1,0:T(8,128)} async-done(((f32[1408,1408]{1,0:T(8,128)}), f32[88,1408]{1,0:T(8,128)}) %reduce-scatter.44.cloned.1.call-update) | async-done | bytes 495632
  1681.1 107.5 %reduce-scatter.46.cloned.1.call-done = f32[88,1408]{1,0:T(8,128)} async-done(((f32[1408,1408]{1,0:T(8,128)}), f32[88,1408]{1,0:T(8,128)}) %reduce-scatter.46.cloned.1.call-update) | async-done | bytes 495632
  1788.6 106.8 %reduce-scatter.48.cloned.1.call-done = f32[88,1408]{1,0:T(8,128)} async-done(((f32[1408,1408]{1,0:T(8,128)}), f32[88,1408]{1,0:T(8,128)}) %reduce-scatter.48.cloned.1.call-update) | async-done | bytes 495632
  1895.4 107.5 %reduce-scatter.40.cloned.1.call-done = f32[88,1408]{1,0:T(8,128)} async-done(((f32[1408,1408]{1,0:T(8,128)}), f32[88,1408]{1,0:T(8,128)}) %reduce-scatter.40.cloned.1.call-update) | async-done | bytes 495632
  2002.9 174.3 %reduce-scatter.28.cloned.1.call-done = f32[176,1408]{1,0:T(8,128)} async-done(((f32[2816,1408]{1,0:T(8,128)}), f32[176,1408]{1,0:T(8,128)}) %reduce-scatter.28.cloned.1.call-update) | async-done | bytes 991248 | tf_op jit(solution)/shard_map/reduce_scatter | solution.py:671
  2177.2 349.1 %reduce-scatter.32.cloned.1.call-done = f32[88,6144]{1,0:T(8,128)} async-done(((f32[1408,6144]{1,0:T(8,128)}), f32[88,6144]{1,0:T(8,128)}) %reduce-scatter.32.cloned.1.call-update) | async-done | bytes 2162704 | tf_op jit(solution)/shard_map/reduce_scatter | solution.py:677
  2526.3 348.9 %reduce-scatter.34.cloned.1.call-done = f32[384,1408]{1,0:T(8,128)} async-done(((f32[6144,1408]{1,0:T(8,128)}), f32[384,1408]{1,0:T(8,128)}) %reduce-scatter.34.cloned.1.call-update) | async-done | bytes 2162704 | tf_op jit(solution)/shard_map/reduce_scatter | solution.py:678
  2875.2 236.7 %reduce-scatter.42.cloned.1.call-done = f32[88,4224]{1,0:T(8,128)} async-done(((f32[1408,4224]{1,0:T(8,128)}), f32[88,4224]{1,0:T(8,128)}) %reduce-scatter.42.cloned.1.call-update) | async-done | bytes 1486864
  3139.4 230.5 %all-reduce.43.cloned.1.call-done = (f32[176,1408]{1,0:T(8,128)}, f32[88,1408]{1,0:T(8,128)}, f32[88,4224]{1,0:T(8,128)}, f32[88,1408]{1,0:T(8,128)}, f32[88,140...) async-done(((f32[176,1408]{1,0:T(8,128)}, f32[88,1408]{1,0:T(8,128)}, f32[88,4224]{1,0:T(8,128)}, ...) | async-done | bytes 9506832 | tf_op jit(solution)/shard_map/psum | solution.py:710
  (969 shorter events, 908.8 us)
Async XLA Ops:
  8.8 232.4 %all-gather.22.cloned.1.call-start = ((), (), s32[]{:S(2)}) async-start(), calls=%async_computation.13 | async-start | bytes 12638208 | tf_op jit(solution)/shard_map/all_gather | solution.py:240
  9.6 317.0 %all-gather.30.cloned.1.call-start = ((), (), s32[]{:S(2)}) async-start(), calls=%async_computation.17 | async-start | bytes 4595712 | tf_op jit(solution)/shard_map/all_gather | solution.py:363
  86.5 307.0 %all-gather.24.cloned.1.call-start = ((), (), s32[]{:S(2)}) async-start(), calls=%async_computation.14 | async-start | bytes 12255232 | tf_op jit(solution)/shard_map/all_gather | solution.py:341
  271.3 216.9 %all-gather.26.cloned.1.call-start = ((), (), s32[]{:S(2)}) async-start(), calls=%async_computation.15 | async-start | bytes 12255232 | tf_op jit(solution)/shard_map/all_gather | solution.py:342
  273.9 305.1 %all-gather.28.cloned.1.call-start = ((), (), s32[]{:S(2)}) async-start(), calls=%async_computation.16 | async-start | bytes 4212736 | tf_op jit(solution)/shard_map/all_gather | solution.py:241
  274.7 313.8 %all-gather.32.cloned.1.call-start = ((), (), s32[]{:S(2)}) async-start(), calls=%async_computation.18 | async-start | bytes 4212736 | tf_op jit(solution)/shard_map/all_gather | solution.py:242
  275.4 362.7 %all-gather.34.cloned.1.call-start = ((), (), s32[]{:S(2)}) async-start(), calls=%async_computation.19 | async-start | bytes 4212736 | tf_op jit(solution)/shard_map/all_gather | solution.py:243
  276.2 458.8 %all-gather.36.cloned.1.call-start = ((), (), s32[]{:S(2)}) async-start(), calls=%async_computation.20 | async-start | bytes 18382848 | tf_op jit(solution)/shard_map/all_gather | solution.py:244
  276.8 556.1 %all-gather.38.cloned.1.call-start = ((), (), s32[]{:S(2)}) async-start(), calls=%async_computation.21 | async-start | bytes 18382848 | tf_op jit(solution)/shard_map/all_gather | solution.py:245
  277.5 836.7 %reduce-scatter.30.cloned.1.call-start = ((), (), s32[]{:S(2)}) async-start(), calls=%async_computation.25 | async-start | bytes 9191424 | tf_op jit(solution)/shard_map/reduce_scatter | solution.py:492
  894.8 223.7 %all-gather.40.cloned.1.call-start = ((), (), s32[]{:S(2)}) async-start(), calls=%async_computation.22 | async-start | bytes 12255232 | tf_op jit(solution)/shard_map/all_gather | solution.py:594
  895.5 305.4 %all-gather.42.cloned.1.call-start = ((), (), s32[]{:S(2)}) async-start(), calls=%async_computation.23 | async-start | bytes 12255232 | tf_op jit(solution)/shard_map/all_gather | solution.py:595
  937.0 578.3 %reduce-scatter.38.cloned.1.call-start = ((), (), s32[]{:S(2)}) async-start(), calls=%async_computation.29 | async-start | bytes 1531904
  1114.0 403.7 %all-reduce.39.cloned.1.call-start = ((), (), s32[]{:S(2)}) async-start(), calls=%async_computation.35 | async-start | bytes 319488
  1425.1 256.0 %reduce-scatter.44.cloned.1.call-start = ((), (), s32[]{:S(2)}) async-start(), calls=%async_computation.32 | async-start | bytes 8425472
  1430.7 357.9 %reduce-scatter.46.cloned.1.call-start = ((), (), s32[]{:S(2)}) async-start(), calls=%async_computation.33 | async-start | bytes 8425472
  1437.9 457.6 %reduce-scatter.48.cloned.1.call-start = ((), (), s32[]{:S(2)}) async-start(), calls=%async_computation.34 | async-start | bytes 8425472
  1443.6 559.3 %reduce-scatter.40.cloned.1.call-start = ((), (), s32[]{:S(2)}) async-start(), calls=%async_computation.30 | async-start | bytes 8425472
  1449.9 727.3 %reduce-scatter.28.cloned.1.call-start = ((), (), s32[]{:S(2)}) async-start(), calls=%async_computation.24 | async-start | bytes 16850944 | tf_op jit(solution)/shard_map/reduce_scatter | solution.py:671
  1461.1 1065.3 %reduce-scatter.32.cloned.1.call-start = ((), (), s32[]{:S(2)}) async-start(), calls=%async_computation.26 | async-start | bytes 36765696 | tf_op jit(solution)/shard_map/reduce_scatter | solution.py:677
  1480.6 1394.6 %reduce-scatter.34.cloned.1.call-start = ((), (), s32[]{:S(2)}) async-start(), calls=%async_computation.27 | async-start | bytes 36765696 | tf_op jit(solution)/shard_map/reduce_scatter | solution.py:678
  1498.0 1613.9 %reduce-scatter.42.cloned.1.call-start = ((), (), s32[]{:S(2)}) async-start(), calls=%async_computation.31 | async-start | bytes 25276416
  1511.9 1627.4 %all-reduce.41.cloned.1.call-start = ((), (), s32[]{:S(2)}) async-start(), calls=%async_computation.36 | async-start | bytes 327680 | tf_op jit(solution)/shard_map/psum | solution.py:710
  1576.3 1793.5 %all-reduce.43.cloned.1.call-start = ((), (), s32[]{:S(2)}) async-start(), calls=%async_computation.37 | async-start | bytes 19013632 | tf_op jit(solution)/shard_map/psum | solution.py:710
  (254 other events, 6116.7 us)
Sparse Core Ops, SparseCore 0:
  10.4 52.4 all-gather.19
  65.1 77.3 all-gather.17
  144.7 96.4 all-gather.21
  243.9 51.3 all-gather.29
  297.5 95.9 all-gather.23
  395.7 92.4 all-gather.25
  539.8 48.6 all-gather.31
  639.5 95.3 all-gather.35
  736.5 96.2 all-gather.37
  894.9 107.2 reduce-scatter.29
  1004.6 100.6 all-gather.39
  1107.5 93.4 all-gather.41
  1204.4 57.2 reduce-scatter.37
  1422.4 87.8 all-reduce.38
  1514.4 60.2 reduce-scatter.35
  1578.5 102.5 reduce-scatter.43
  1685.7 102.8 reduce-scatter.45
  1792.5 102.8 reduce-scatter.47
  1900.0 102.8 reduce-scatter.39
  2007.1 170.0 reduce-scatter.27
  2182.1 344.2 reduce-scatter.31
  2531.0 344.1 reduce-scatter.33
  2879.9 231.9 reduce-scatter.41
  3143.5 226.3 all-reduce.42
  (3 shorter events, 117.1 us)
where the time goes:
time: 3410 us; the launch traced here: 3400 us
  waiting for transfers between devices  2260 us (66%)
  matrix products  400 us (12%)
  local copies, waits for them, and re-layouts  294 us (9%)
  blocking collectives  282 us (8%)
  other arithmetic  106 us (3%)
    unnamed x35, waiting for transfers between devices  714 us
    reduce_scatter x1, waiting for transfers between devices, body(): lax.psum_scatter(grad_up, ('row', 'col'), scatter_dimension=0, tiled=True)  349 us
    reduce_scatter x1, waiting for transfers between devices, body(): lax.psum_scatter(grad_down, ('row', 'col'), scatter_dimension=0, tiled=True)  349 us
    psum x2, waiting for transfers between devices, body(): lax.psum((shard_embed, shard_skip, shard_shift, shard_qkv, shard_out, sha...  231 us
    reduce_scatter x1, waiting for transfers between devices, body(): lax.psum_scatter(grad_skip_weight, ('row', 'col'), scatter_dimension=0, t...  174 us
    unnamed x519, local copies, waits for them, and re-layouts  97.4 us
    all_gather x1, waiting for transfers between devices, body(): lax.all_gather(up_weight, ('row', 'col'), axis=0, tiled=True)  91.5 us
    all_gather x1, waiting for transfers between devices, body(): lax.all_gather(down_weight, ('row', 'col'), axis=0, tiled=True)  84.3 us
  transfers between devices with their start and end apart: 39, of which 21 were waited for; matrix products, arithmetic and copies ran while one was open for 20% of the time, Pallas kernels for 0%

commit v1 on v0

v1 whole, which is shorter than its diff:
```python
import functools
import math

import jax
import jax.numpy as jnp
import numpy as np
from jax import lax
from jax.experimental import pallas as pl
from jax.experimental.pallas import tpu as pltpu
from jax.sharding import PartitionSpec as P

D = 1408
HEADS = 16
HD = 88
FF = 6144
CLIP = 77
NORM_EPS = 1e-06
NEG_FILL = -1e30
STEPS = ((-1, -1), (-1, 0), (-1, 1), (0, -1), (0, 0), (0, 1), (1, -1), (1, 0), (1, 1))
GROUP = ("row", "col")
F32 = jnp.float32
BF = jnp.bfloat16
SCALE = 1.0 / math.sqrt(HD)
LOG2E = math.log2(math.e)
NT = (((1,), (1,)), ((), ()))
KEY_BLOCK = 256
QUERY_CHUNK = 1024


def with_halo(block, sides, width):
    for axis, dim in sides:
        count = lax.axis_size(axis)
        forward = [(i, i + 1) for i in range(count - 1)]
        backward = [(target, source) for source, target in forward]
        low = lax.ppermute(
            lax.slice_in_dim(block, block.shape[dim] - width, None, axis=dim), axis, forward
        )
        high = lax.ppermute(lax.slice_in_dim(block, 0, width, axis=dim), axis, backward)
        block = jnp.concatenate([low, block, high], axis=dim)
    return block


def dot(former, latter, former_dims, latter_dims):
    return lax.dot_general(
        former, latter, ((former_dims, latter_dims), ((), ())), preferred_element_type=F32
    )


def matmul(former, latter):
    return dot(former, latter, (former.ndim - 1,), (0,))


def matmul_back(former, latter):
    return dot(former, latter, (former.ndim - 1,), (1,))


def weight_grad(inputs, grads):
    lead = tuple(range(inputs.ndim - 1))
    return dot(inputs, grads, lead, lead)


def column_sum(grads):
    return jnp.sum(grads.astype(F32), axis=tuple(range(grads.ndim - 1)))


def layer_norm(values, scales, offsets):
    centre = values - jnp.mean(values, axis=-1, keepdims=True)
    spread = jnp.mean(centre * centre, axis=-1, keepdims=True)
    return centre * lax.rsqrt(spread + NORM_EPS) * scales + offsets


def angles_of(row_place, col_place):
    pair_index = np.arange(HD) // 2
    quarter = HD // 4
    within = np.where(pair_index < quarter, pair_index, pair_index - quarter).astype(np.float32)
    frequency = np.exp(np.float32(-math.log(10000.0)) * within / np.float32(quarter))
    by_row = jnp.asarray(pair_index < quarter)
    places = jnp.where(by_row[:, None], row_place[None, :], col_place[None, :])
    return places.astype(F32) * jnp.asarray(frequency.astype(np.float32))[:, None]


def gather_near(padded, tall, broad):
    return jnp.concatenate(
        [
            padded[..., 1 + step_row : 1 + step_row + tall, 1 + step_col : 1 + step_col + broad, :]
            for step_row, step_col in STEPS
        ],
        axis=-1,
    )


def spread_near(padded, tall, broad, channels):
    result = None
    for number, (step_row, step_col) in enumerate(STEPS):
        portion = padded[
            ...,
            1 - step_row : 1 - step_row + tall,
            1 - step_col : 1 - step_col + broad,
            number * channels : (number + 1) * channels,
        ]
        result = portion if result is None else result + portion
    return result


def cuts(vector, widths):
    ends = np.cumsum((0,) + widths)
    return [vector[..., ends[i] : ends[i + 1]] for i in range(len(widths))]


def swap_images(values, bit):
    count = lax.axis_size("img")
    return lax.ppermute(values, "img", [(i, i ^ bit) for i in range(count)])


def images_gather(values):
    blocks = values[None]
    while blocks.shape[0] < lax.axis_size("img"):
        blocks = jnp.concatenate([blocks, swap_images(blocks, blocks.shape[0])])
    return blocks


def images_scatter(parts):
    while parts.shape[0] > 1:
        half = parts.shape[0] // 2
        parts = parts[:half] + swap_images(parts[half:].astype(BF), half).astype(F32)
    return parts[0]


def images_sum(values, sent):
    bit = 1
    while bit < lax.axis_size("img"):
        values = values.astype(sent)
        values = values.astype(F32) + swap_images(values, bit).astype(F32)
        bit *= 2
    return values.astype(F32)


def exchange(values, axis, bit):
    size = lax.axis_size(axis)
    return lax.ppermute(values, axis, [(i, i ^ bit) for i in range(size)])


def halves(values, dim, bit):
    keep = lax.dynamic_index_in_dim(values, bit, dim, keepdims=False)
    return keep, lax.dynamic_index_in_dim(values, 1 - bit, dim, keepdims=False)


def core_features(values, dim, core):
    rows = lax.axis_size("row")
    block = values.shape[dim] // rows
    return jnp.concatenate(
        [
            lax.dynamic_slice_in_dim(values, (2 * i + core) * block, block, dim)
            for i in range(rows // 2)
        ],
        axis=dim,
    )


def row_first():
    rows, cols = lax.axis_size("row"), lax.axis_size("col")
    row_bits = [("row", 1 << i) for i in range(1, rows.bit_length() - 1)]
    return row_bits + [("col", 1 << i) for i in range(cols.bit_length() - 1)]


def col_first():
    return sorted(row_first())


def shard_sum(order, after, inputs, grads, input_lead, grad_lead, feature):
    core = lax.axis_index("row") % 2
    give = dot(core_features(inputs, feature, 1 - core), grads, input_lead, grad_lead)
    got = yield exchange(give.astype(BF), "row", 1)
    keep = dot(core_features(inputs, feature, core), grads, input_lead, grad_lead)
    part = yield from scatter_sum(order, keep + got.astype(F32))
    part = yield from after(part)
    return part


def image_parts(grads, dim):
    groups, me = lax.axis_size("img"), lax.axis_index("img")
    width = grads.shape[dim] // groups
    return [
        lax.dynamic_slice_in_dim(grads, (me ^ i) * width, width, dim) for i in range(groups)
    ]


def image_first_sum(order, after, inputs, grads, input_lead, grad_lead, feature, grad_feature):
    core = lax.axis_index("row") % 2
    parts = image_parts(grads, grad_feature)
    given = core_features(inputs, feature, 1 - core)
    gots = yield [
        exchange(dot(given, part, input_lead, grad_lead).astype(BF), "row", 1) for part in parts
    ]
    kept = core_features(inputs, feature, core)
    sums = [
        dot(kept, part, input_lead, grad_lead) + got.astype(F32) for part, got in zip(parts, gots)
    ]
    while len(sums) > 1:
        half = len(sums) // 2
        gots = yield [swap_images(part.astype(BF), half) for part in sums[half:]]
        sums = [part + got.astype(F32) for part, got in zip(sums, gots)]
    part = yield from scatter_sum(order, sums[0])
    part = yield from after(part)
    return part


def row_sum(order, after, values):
    rows = lax.axis_size("row")
    split = values.reshape(rows // 2, 2, -1, values.shape[-1])
    keep, give = halves(split, 1, lax.axis_index("row") % 2)
    got = yield exchange(give, "row", 1)
    part = yield from scatter_sum(order, keep.astype(F32) + got.astype(F32))
    part = yield from after(part)
    return part


def scatter_sum(order, part):
    dims = [d for d in reversed(row_first()) if d[0] == "row"]
    dims += [d for d in reversed(row_first()) if d[0] == "col"]
    width = part.shape[-1]
    part = part.reshape((2,) * len(dims) + (-1, width))
    for axis, bit in order:
        at = dims.index((axis, bit))
        keep, give = halves(part, at, lax.axis_index(axis) // bit % 2)
        del dims[at]
        got = yield exchange(give.astype(BF), axis, bit)
        part = keep + got.astype(F32)
    return part.reshape(-1, width)


def alone(part):
    return part
    yield


def over_images(part):
    bit = 1
    while bit < lax.axis_size("img"):
        part = part.astype(BF)
        got = yield swap_images(part, bit)
        part = part.astype(F32) + got.astype(F32)
        bit *= 2
    return part


def all_images(part):
    bit, blocks = 1, part.astype(BF)[None]
    while bit < lax.axis_size("img"):
        got = yield swap_images(blocks, bit)
        blocks = placed(blocks, got, lax.axis_index("img") // bit % 2, 0)
        blocks = blocks.reshape((-1,) + part.shape)
        bit *= 2
    return blocks


def placed(mine, other, bit, dim):
    first = lax.select(jnp.broadcast_to(bit == 0, mine.shape), mine, other)
    last = lax.select(jnp.broadcast_to(bit == 0, mine.shape), other, mine)
    return jnp.stack([first, last], axis=dim)


def gather_rows(values):
    rows, cols = lax.axis_size("row"), lax.axis_size("col")
    row_index, col_index = lax.axis_index("row"), lax.axis_index("col")
    tail = values.shape
    bit, blocks = cols // 2, values[None]
    while bit >= 1:
        blocks = placed(blocks, exchange(blocks, "col", bit), col_index // bit % 2, 1)
        blocks = blocks.reshape((-1,) + tail)
        bit //= 2
    blocks = blocks[None]
    bit = rows // 2
    while bit >= 1:
        blocks = placed(blocks, exchange(blocks, "row", bit), row_index // bit % 2, 1)
        blocks = blocks.reshape((-1, cols) + tail)
        bit //= 2
    return blocks.reshape((-1,) + tail[1:])


class Sums:
    def __init__(self):
        self.running = {}
        self.done = {}

    def begin(self, name, *work, order=None, after=over_images):
        kind = {1: row_sum, 5: shard_sum, 6: image_first_sum}[len(work)]
        maker = kind(order or row_first(), after, *work)
        self.running[name] = (maker, next(maker))

    def step(self, value, *names):
        names = [name for name in names if name in self.running]
        if not names:
            return value
        tied = lax.optimization_barrier((value, *[self.running[name][1] for name in names]))
        for name, got in zip(names, tied[1:]):
            self.move(name, got)
        return tied[0]

    def move(self, name, got):
        maker = self.running[name][0]
        try:
            self.running[name] = (maker, maker.send(got))
        except StopIteration as stop:
            del self.running[name]
            self.done[name] = stop.value

    def finish(self):
        while self.running:
            for name in list(self.running):
                self.move(name, self.running[name][1])
        return self.done


def unit_rows(values):
    centre = values - jnp.mean(values, axis=0, keepdims=True)
    rstd = lax.rsqrt(jnp.mean(centre * centre, axis=0, keepdims=True) + NORM_EPS)
    return centre * rstd, rstd


def swap_pairs(values, back):
    rows = values.shape[0]
    even = lax.broadcasted_iota(jnp.int32, values.shape, 0) % 2 == 0
    up = pltpu.roll(values, rows - 1, 0)
    down = pltpu.roll(values, 1, 0)
    return jnp.where(even, up, -down) if back else jnp.where(even, -up, down)


def turn(values, cos, sin):
    return values * cos + swap_pairs(values, False) * sin


def turn_back(values, cos, sin):
    return values * cos + swap_pairs(values, True) * sin


def tiles(ref, part, count):
    return jnp.concatenate([ref[s, 0, part] for s in range(count)], axis=1)


def key_blocks(geo, ext_ref, job):
    count, tile_rows, tile_cols, col_tiles, block_tiles = geo
    rows = ext_ref[job, 0] // tile_rows
    groups = ext_ref[job, 1] // (block_tiles * tile_cols)

    def place(i):
        block = i // groups * (col_tiles // block_tiles) + i % groups
        return pl.multiple_of(block * KEY_BLOCK, KEY_BLOCK)

    return rows * groups, place


def attend_kernel(
    geo, ext_ref, qkv_ref, cos_ref, sin_ref, head_ref, out_ref, keep_ref, total_ref,
    q_s, kt_s, v_s, m_s, l_s,
):
    count = geo[0]
    cos, sin = cos_ref[...], sin_ref[...]
    unit, _ = unit_rows(tiles(qkv_ref, 0, count).astype(F32))
    q_s[...] = turn(unit * head_ref[:, 0:1] + head_ref[:, 1:2], cos, sin).astype(BF)
    unit, _ = unit_rows(tiles(qkv_ref, 1, count).astype(F32))
    kt_s[...] = turn(unit * head_ref[:, 2:3] + head_ref[:, 3:4], cos, sin).T.astype(BF)
    v_s[...] = tiles(qkv_ref, 2, count)
    block_count, place = key_blocks(geo, ext_ref, pl.program_id(0))
    width = q_s.shape[1]
    m_s[...] = jnp.full_like(m_s, NEG_FILL)
    l_s[...] = jnp.zeros_like(l_s)
    keep_ref[0] = jnp.zeros(keep_ref.shape[1:], F32)

    def key_step(i, carry):
        first = place(i)
        keys = kt_s[pl.ds(first, KEY_BLOCK), :]
        vals = v_s[:, pl.ds(first, KEY_BLOCK)]
        for part in range(width // QUERY_CHUNK):
            cut = slice(part * QUERY_CHUNK, (part + 1) * QUERY_CHUNK)
            scores = jnp.dot(keys, q_s[:, cut], preferred_element_type=F32)
            old = m_s[:, cut]
            new = jnp.maximum(old, jnp.max(scores, axis=0, keepdims=True))
            probs = jnp.exp2((scores - new) * (SCALE * LOG2E))
            factor = jnp.exp2((old - new) * (SCALE * LOG2E))
            m_s[:, cut] = new
            l_s[:, cut] = l_s[:, cut] * factor + jnp.sum(probs, axis=0, keepdims=True)
            keep_ref[0, :, cut] = keep_ref[0, :, cut] * factor + jnp.dot(
                vals, probs.astype(BF), preferred_element_type=F32
            )
        return carry

    lax.fori_loop(0, block_count, key_step, 0)
    total_ref[0] = m_s[...] * (SCALE * LOG2E) + jnp.log2(l_s[...])
    mixed = keep_ref[0] / l_s[...]
    keep_ref[0] = mixed
    low = mixed.astype(BF)
    tile = width // count
    for s in range(count):
        out_ref[s, 0] = low[:, s * tile : (s + 1) * tile]


def attend(ext_jobs, qkv, cos, sin, head, geo):
    count, jobs, _, _, tile = qkv.shape
    width = count * tile
    work = 4 * jobs * width * width * HD
    return pl.pallas_call(
        functools.partial(attend_kernel, geo),
        grid=(jobs,),
        in_specs=[
            pl.BlockSpec(memory_space=pltpu.SMEM),
            pl.BlockSpec((count, 1, 3, HD, tile), lambda j: (0, j, 0, 0, 0)),
            pl.BlockSpec((HD, width), lambda j: (0, 0)),
            pl.BlockSpec((HD, width), lambda j: (0, 0)),
            pl.BlockSpec((HD, 4), lambda j: (0, 0)),
        ],
        out_specs=[
            pl.BlockSpec((count, 1, HD, tile), lambda j: (0, j, 0, 0)),
            pl.BlockSpec((1, HD, width), lambda j: (j, 0, 0)),
            pl.BlockSpec((1, 1, width), lambda j: (j, 0, 0)),
        ],
        out_shape=[
            jax.ShapeDtypeStruct((count, jobs, HD, tile), BF),
            jax.ShapeDtypeStruct((jobs, HD, width), F32),
            jax.ShapeDtypeStruct((jobs, 1, width), F32),
        ],
        scratch_shapes=[
            pltpu.VMEM((HD, width), BF),
            pltpu.VMEM((width, HD), BF),
            pltpu.VMEM((HD, width), BF),
            pltpu.VMEM((1, width), F32),
            pltpu.VMEM((1, width), F32),
        ],
        compiler_params=pltpu.CompilerParams(vmem_limit_bytes=48 * 2**20),
        cost_estimate=pl.CostEstimate(
            flops=3 * work, bytes_accessed=6 * 2**20, transcendentals=jobs * width * width
        ),
    )(ext_jobs, qkv, cos, sin, head)


def attend_back_kernel(
    geo, ext_ref, qkv_ref, dout_ref, keep_ref, total_ref, cos_ref, sin_ref, head_ref,
    grad_ref, head_grad_ref, q_s, k_s, kt_s, vt_s, do_s, delta_s, dq_s, dk_s, dv_s,
):
    count = geo[0]
    cos, sin = cos_ref[...], sin_ref[...]
    unit, _ = unit_rows(tiles(qkv_ref, 0, count).astype(F32))
    q_s[...] = turn(unit * head_ref[:, 0:1] + head_ref[:, 1:2], cos, sin).astype(BF)
    unit, _ = unit_rows(tiles(qkv_ref, 1, count).astype(F32))
    keys = turn(unit * head_ref[:, 2:3] + head_ref[:, 3:4], cos, sin)
    k_s[...] = keys.astype(BF)
    kt_s[...] = keys.T.astype(BF)
    vt_s[...] = tiles(qkv_ref, 2, count).astype(F32).T.astype(BF)
    dout = jnp.concatenate([dout_ref[s, 0] for s in range(count)], axis=1)
    do_s[...] = dout
    delta_s[...] = jnp.sum(dout.astype(F32) * keep_ref[0], axis=0, keepdims=True)
    block_count, place = key_blocks(geo, ext_ref, pl.program_id(0))
    width = q_s.shape[1]
    dq_s[...] = jnp.zeros_like(dq_s)
    dk_s[...] = jnp.zeros_like(dk_s)
    dv_s[...] = jnp.zeros_like(dv_s)

    def key_step(i, carry):
        first = place(i)
        keys_t = kt_s[pl.ds(first, KEY_BLOCK), :]
        vals_t = vt_s[pl.ds(first, KEY_BLOCK), :]
        keys_n = k_s[:, pl.ds(first, KEY_BLOCK)]
        dk = jnp.zeros((HD, KEY_BLOCK), F32)
        dv = jnp.zeros((HD, KEY_BLOCK), F32)
        for part in range(width // QUERY_CHUNK):
            cut = slice(part * QUERY_CHUNK, (part + 1) * QUERY_CHUNK)
            queries = q_s[:, cut]
            douts = do_s[:, cut]
            scores = jnp.dot(keys_t, queries, preferred_element_type=F32)
            probs = jnp.exp2(scores * (SCALE * LOG2E) - total_ref[0, :, cut])
            dprob = jnp.dot(vals_t, douts, preferred_element_type=F32)
            dscore = (probs * (dprob - delta_s[:, cut])).astype(BF)
            dv = dv + lax.dot_general(douts, probs.astype(BF), NT, preferred_element_type=F32)
            dk = dk + lax.dot_general(queries, dscore, NT, preferred_element_type=F32)
            dq_s[:, cut] += jnp.dot(keys_n, dscore, preferred_element_type=F32)
        dk_s[:, pl.ds(first, KEY_BLOCK)] = dk
        dv_s[:, pl.ds(first, KEY_BLOCK)] = dv
        return carry

    lax.fori_loop(0, block_count, key_step, 0)
    tile = width // count

    def lift(part, turned, at):
        unit, rstd = unit_rows(tiles(qkv_ref, part, count).astype(F32))
        dy = turn_back(turned * SCALE, cos, sin)
        head_grad_ref[0, :, at : at + 1] = jnp.sum(dy * unit, axis=1, keepdims=True)
        head_grad_ref[0, :, at + 1 : at + 2] = jnp.sum(dy, axis=1, keepdims=True)
        dunit = dy * head_ref[:, at : at + 1]
        along = jnp.mean(dunit * unit, axis=0, keepdims=True)
        dx = (dunit - jnp.mean(dunit, axis=0, keepdims=True) - unit * along) * rstd
        low = dx.astype(BF)
        for s in range(count):
            grad_ref[s, 0, part] = low[:, s * tile : (s + 1) * tile]

    lift(0, dq_s[...], 0)
    lift(1, dk_s[...], 2)
    low = dv_s[...].astype(BF)
    for s in range(count):
        grad_ref[s, 0, 2] = low[:, s * tile : (s + 1) * tile]


def attend_back(ext_jobs, qkv, dout, keep, total, cos, sin, head, geo):
    count, jobs, _, _, tile = qkv.shape
    width = count * tile
    work = 10 * jobs * width * width * HD
    return pl.pallas_call(
        functools.partial(attend_back_kernel, geo),
        grid=(jobs,),
        in_specs=[
            pl.BlockSpec(memory_space=pltpu.SMEM),
            pl.BlockSpec((count, 1, 3, HD, tile), lambda j: (0, j, 0, 0, 0)),
            pl.BlockSpec((count, 1, HD, tile), lambda j: (0, j, 0, 0)),
            pl.BlockSpec((1, HD, width), lambda j: (j, 0, 0)),
            pl.BlockSpec((1, 1, width), lambda j: (j, 0, 0)),
            pl.BlockSpec((HD, width), lambda j: (0, 0)),
            pl.BlockSpec((HD, width), lambda j: (0, 0)),
            pl.BlockSpec((HD, 4), lambda j: (0, 0)),
        ],
        out_specs=[
            pl.BlockSpec((count, 1, 3, HD, tile), lambda j: (0, j, 0, 0, 0)),
            pl.BlockSpec((1, HD, 4), lambda j: (j, 0, 0)),
        ],
        out_shape=[
            jax.ShapeDtypeStruct((count, jobs, 3, HD, tile), BF),
            jax.ShapeDtypeStruct((jobs, HD, 4), F32),
        ],
        scratch_shapes=[
            pltpu.VMEM((HD, width), BF),
            pltpu.VMEM((HD, width), BF),
            pltpu.VMEM((width, HD), BF),
            pltpu.VMEM((width, HD), BF),
            pltpu.VMEM((HD, width), BF),
            pltpu.VMEM((1, width), F32),
            pltpu.VMEM((HD, width), F32),
            pltpu.VMEM((HD, width), F32),
            pltpu.VMEM((HD, width), F32),
        ],
        compiler_params=pltpu.CompilerParams(vmem_limit_bytes=56 * 2**20),
        cost_estimate=pl.CostEstimate(
            flops=3 * work, bytes_accessed=8 * 2**20, transcendentals=jobs * width * width
        ),
    )(ext_jobs, qkv, dout, keep, total, cos, sin, head)


TN = (((0,), (0,)), ((), ()))
CROSS_HEADS = 2


def text_scores(len_ref, keys, queries, image):
    scores = lax.dot_general(keys, queries, TN, preferred_element_type=F32) * (SCALE * LOG2E)
    place = lax.broadcasted_iota(jnp.int32, scores.shape, 0)
    live = (place < len_ref[image, 0]) | (
        (place >= CLIP) & (place < CLIP + len_ref[image, 1])
    )
    return jnp.where(live, scores, NEG_FILL)


def cross_kernel(images, len_ref, rows_ref, text_ref, cos_ref, sin_ref, head_ref, out_ref, total_ref):
    tile = rows_ref.shape[2] // images
    slots = text_ref.shape[3] // images
    for h in range(CROSS_HEADS):
        unit, _ = unit_rows(rows_ref[h])
        queries = turn(unit * head_ref[:, 0:1] + head_ref[:, 1:2], cos_ref[...], sin_ref[...])
        queries = queries.astype(BF)
        for i in range(images):
            own, slot = slice(i * tile, (i + 1) * tile), slice(i * slots, (i + 1) * slots)
            scores = text_scores(len_ref, text_ref[0, h, :, slot], queries[:, own], i)
            top = jnp.max(scores, axis=0, keepdims=True)
            probs = jnp.exp2(scores - top)
            weight = jnp.sum(probs, axis=0, keepdims=True)
            low = (probs / weight).astype(BF)
            mixed = jnp.dot(text_ref[1, h, :, slot], low, preferred_element_type=F32)
            out_ref[h, :, own] = mixed.astype(BF)
            total_ref[h, :, own] = top + jnp.log2(weight)


def cross_back_kernel(
    images, len_ref, rows_ref, text_ref, dout_ref, total_ref, cos_ref, sin_ref, head_ref,
    grad_ref, text_grad_ref, head_grad_ref,
):
    tile = rows_ref.shape[2] // images
    slots = text_ref.shape[3] // images
    cos, sin = cos_ref[...], sin_ref[...]
    gain_grad = jnp.zeros((HD, 1), F32)
    shift_grad = jnp.zeros((HD, 1), F32)
    for h in range(CROSS_HEADS):
        unit, rstd = unit_rows(rows_ref[h])
        queries = turn(unit * head_ref[:, 0:1] + head_ref[:, 1:2], cos, sin).astype(BF)
        turned = []
        for i in range(images):
            own, slot = slice(i * tile, (i + 1) * tile), slice(i * slots, (i + 1) * slots)
            keys = text_ref[0, h, :, slot]
            douts = dout_ref[h, :, own]
            scores = text_scores(len_ref, keys, queries[:, own], i)
            probs = jnp.exp2(scores - total_ref[h, :, own])
            dprob = lax.dot_general(
                text_ref[1, h, :, slot], douts, TN, preferred_element_type=F32
            )
            delta = jnp.sum(probs * dprob, axis=0, keepdims=True)
            dscore = (probs * (dprob - delta)).astype(BF)
            low = probs.astype(BF)
            dkeys = lax.dot_general(queries[:, own], dscore, NT, preferred_element_type=F32)
            text_grad_ref[0, h, :, slot] = (dkeys * SCALE).astype(BF)
            text_grad_ref[1, h, :, slot] = lax.dot_general(
                douts, low, NT, preferred_element_type=F32
            ).astype(BF)
            turned.append(jnp.dot(keys, dscore, preferred_element_type=F32))
        dy = turn_back(jnp.concatenate(turned, axis=1) * SCALE, cos, sin)
        gain_grad += jnp.sum(dy * unit, axis=1, keepdims=True)
        shift_grad += jnp.sum(dy, axis=1, keepdims=True)
        dunit = dy * head_ref[:, 0:1]
        along_unit = jnp.mean(dunit * unit, axis=0, keepdims=True)
        dx = (dunit - jnp.mean(dunit, axis=0, keepdims=True) - unit * along_unit) * rstd
        grad_ref[h] = dx.astype(BF)
    head_grad_ref[0, :, 0:1] = gain_grad
    head_grad_ref[0, :, 1:2] = shift_grad


def cross_specs(width, slots):
    return dict(
        smem=pl.BlockSpec(memory_space=pltpu.SMEM),
        rows=pl.BlockSpec((CROSS_HEADS, HD, width), lambda h: (h, 0, 0)),
        text=pl.BlockSpec((2, CROSS_HEADS, HD, slots), lambda h: (0, h, 0, 0)),
        table=pl.BlockSpec((HD, width), lambda h: (0, 0)),
        head=pl.BlockSpec((HD, 2), lambda h: (0, 0)),
        total=pl.BlockSpec((CROSS_HEADS, 1, width), lambda h: (h, 0, 0)),
        head_grad=pl.BlockSpec((1, HD, 2), lambda h: (h, 0, 0)),
    )


def cross_attend(lengths, rows, text, cos, sin, head):
    heads, _, width = rows.shape
    slots = text.shape[3]
    sp = cross_specs(width, slots)
    return pl.pallas_call(
        functools.partial(cross_kernel, lengths.shape[0]),
        grid=(heads // CROSS_HEADS,),
        in_specs=[sp["smem"], sp["rows"], sp["text"], sp["table"], sp["table"], sp["head"]],
        out_specs=[sp["rows"], sp["total"]],
        out_shape=[
            jax.ShapeDtypeStruct((heads, HD, width), BF),
            jax.ShapeDtypeStruct((heads, 1, width), F32),
        ],
        compiler_params=pltpu.CompilerParams(vmem_limit_bytes=32 * 2**20),
        cost_estimate=pl.CostEstimate(
            flops=2**32, bytes_accessed=10 * 2**20, transcendentals=heads * width * slots
        ),
    )(lengths, rows, text, cos, sin, head)


def cross_attend_back(lengths, rows, text, dout, total, cos, sin, head):
    heads, _, width = rows.shape
    slots = text.shape[3]
    sp = cross_specs(width, slots)
    return pl.pallas_call(
        functools.partial(cross_back_kernel, lengths.shape[0]),
        grid=(heads // CROSS_HEADS,),
        in_specs=[
            sp["smem"], sp["rows"], sp["text"], sp["rows"], sp["total"], sp["table"], sp["table"],
            sp["head"],
        ],
        out_specs=[sp["rows"], sp["text"], sp["head_grad"]],
        out_shape=[
            jax.ShapeDtypeStruct((heads, HD, width), BF),
            jax.ShapeDtypeStruct((2, heads, HD, slots), BF),
            jax.ShapeDtypeStruct((heads // CROSS_HEADS, HD, 2), F32),
        ],
        compiler_params=pltpu.CompilerParams(vmem_limit_bytes=32 * 2**20),
        cost_estimate=pl.CostEstimate(
            flops=2**33, bytes_accessed=16 * 2**20, transcendentals=heads * width * slots
        ),
    )(lengths, rows, text, dout, total, cos, sin, head)


def all_to_all(values):
    return lax.all_to_all(values, GROUP, split_axis=0, concat_axis=0, tiled=True)


def body(
    latents, skip, temb, text, text_len, extent, embed_weight, skip_weight, shift_weight,
    qkv_weight, out_weight, cross_query, cross_keys, cross_out, up_weight, down_weight,
    final_weight, norm_gain, norm_shift, skip_gain, skip_shift, head_gain, head_shift,
    front_biases, all_biases, cross_bias, cotangent,
):
    img_count, tile_rows, tile_cols, patch_vals = latents.shape
    tokens = tile_rows * tile_cols
    near_vals = 9 * patch_vals
    row_count = lax.axis_size("row")
    col_count = lax.axis_size("col")
    count = row_count * col_count
    groups = lax.axis_size("img")
    jobs = img_count * HEADS // count
    row_index = lax.axis_index("row")
    col_index = lax.axis_index("col")
    group_index = lax.axis_index("img")
    device = row_index * col_count + col_index
    shard = D // count
    hid_shard = FF // count
    hid_part = hid_shard // groups

    small_widths = (
        norm_gain.size, norm_shift.size, skip_gain.size, skip_shift.size,
        head_gain.size, head_shift.size, front_biases.size, all_biases.size,
    )
    small = jnp.concatenate(
        [
            embed_weight.T.reshape(-1), final_weight.reshape(-1), norm_gain.reshape(-1),
            norm_shift.reshape(-1), skip_gain, skip_shift, head_gain, head_shift,
            front_biases, all_biases,
        ]
    )
    small_len = small.size
    padded_len = -(-(small_len + img_count * D) // 2048) * 2048
    time_act = jax.nn.silu(temb.astype(F32)).astype(BF)
    time_own = lax.dynamic_slice_in_dim(time_act, device * shard, shard, 1)
    shift_share = matmul(time_own, shift_weight).astype(BF).reshape(-1)
    small = jnp.pad(jnp.concatenate([small, shift_share]), (0, padded_len - small_len - shift_share.size))
    small_all = all_to_all(jnp.broadcast_to(small.reshape(1, -1, 128), (count, padded_len // 128, 128)))
    small_all = small_all.reshape(count, padded_len)
    first_rows = jnp.concatenate(
        [skip_weight] + [qkv_weight[:, i * D : (i + 1) * D] for i in range(3)]
    )
    first_all = lax.all_gather(first_rows, GROUP, axis=0, tiled=False)
    skip_full = first_all[:, : 2 * shard].reshape(2 * D, D)
    qkv_full = jnp.concatenate(
        [first_all[:, (2 + i) * shard : (3 + i) * shard].reshape(D, D) for i in range(3)], axis=1
    )
    trio = lax.all_gather(
        jnp.stack([out_weight, cross_query, cross_out]), GROUP, axis=0, tiled=False
    )
    out_full, cross_q_full, cross_o_full = [trio[:, i].reshape(D, D) for i in range(3)]
    up_part = lax.dynamic_index_in_dim(
        up_weight.reshape(shard, count, groups, hid_part), group_index, 2, keepdims=False
    ).reshape(shard, count * hid_part)
    up_full = lax.all_gather(up_part, GROUP, axis=0, tiled=True)
    down_part = lax.dynamic_index_in_dim(
        down_weight.reshape(groups, hid_part, D), group_index, 0, keepdims=False
    )
    down_full = lax.all_gather(down_part, GROUP, axis=0, tiled=True)

    wide = shard * near_vals
    embed_t = small_all[:, :wide].reshape(D, near_vals)
    final_full = small_all[:, wide : 2 * wide].reshape(D, near_vals)
    vectors = cuts(small_all[:, 2 * wide : small_len].astype(F32), small_widths)
    gain_rows = jnp.transpose(vectors[0].reshape(count, 3, shard), (1, 0, 2)).reshape(3, D)
    offset_rows = jnp.transpose(vectors[1].reshape(count, 3, shard), (1, 0, 2)).reshape(3, D)
    skip_gains, skip_offsets = vectors[2].reshape(-1), vectors[3].reshape(-1)
    head_gains, head_offsets = vectors[4].reshape(4, HD), vectors[5].reshape(4, HD)
    bias_embed, bias_skip, bias_shift, bias_qkv = cuts(vectors[6].reshape(-1), (D, D, D, 3 * D))
    bias_out, bias_cross_q, bias_cross_o, bias_up, bias_down = cuts(
        vectors[7].reshape(-1), (D, D, D, FF, D)
    )
    bias_up_part = lax.dynamic_index_in_dim(
        bias_up.reshape(count, groups, hid_part), group_index, 1, keepdims=False
    ).reshape(-1)

    local_rows = row_index * tile_rows + jnp.arange(tile_rows, dtype=jnp.int32)
    local_cols = col_index * tile_cols + jnp.arange(tile_cols, dtype=jnp.int32)
    inside = (
        (local_rows[None, :, None] < extent[:, 0, None, None])
        & (local_cols[None, None, :] < extent[:, 1, None, None])
    ).astype(F32)
    token_inside = inside.reshape(img_count, tokens, 1)
    own_angle = angles_of(
        jnp.tile(jnp.repeat(local_rows, tile_cols), img_count),
        jnp.tile(jnp.tile(local_cols, tile_rows), img_count),
    )
    own_cos, own_sin = jnp.cos(own_angle), jnp.sin(own_angle)
    every = np.arange(count * tokens)
    every_row = every // tokens // col_count * tile_rows + every % tokens // tile_cols
    every_col = every // tokens % col_count * tile_cols + every % tile_cols
    every_angle = angles_of(jnp.asarray(every_row), jnp.asarray(every_col))
    every_cos, every_sin = jnp.cos(every_angle), jnp.sin(every_angle)
    job_images = (device * jobs + jnp.arange(jobs, dtype=jnp.int32)) % img_count
    ext_jobs = jnp.take(extent, job_images, axis=0)
    geo = (count, tile_rows, tile_cols, col_count, KEY_BLOCK // tokens)

    def gelu_tanh(values):
        return jax.nn.gelu(values, approximate=True)

    text_width = cross_keys.shape[1]
    text_count = -(-text.shape[1] // 128) * 128
    text_wide = jnp.pad(text, ((0, 0), (0, text_count - text.shape[1]), (0, 0)))
    is_key = device * text_width + jnp.arange(text_width, dtype=jnp.int32) < D

    def text_norm(values, scales, offsets):
        per_head = values.reshape(text_width // HD, HD, -1)
        centre = per_head - jnp.mean(per_head, axis=1, keepdims=True)
        spread = jnp.mean(centre * centre, axis=1, keepdims=True)
        unit = centre * lax.rsqrt(spread + NORM_EPS) * scales[:, None] + offsets[:, None]
        return jnp.where(is_key[:, None], unit.reshape(values.shape), values)

    text_part = dot(cross_keys, text_wide, (0,), (2,)).reshape(text_width, -1)
    text_part = text_part + cross_bias.astype(F32)[:, None]
    text_normed, text_pull = jax.vjp(text_norm, text_part, head_gains[3], head_offsets[3])
    text_both = lax.all_gather(text_normed.astype(BF), GROUP, axis=0, tiled=True)
    text_both = text_both.reshape(2, HEADS, HD, img_count * text_count)
    shift_sums = small_all[:, small_len : small_len + img_count * D].astype(F32)
    shift_rows = jnp.sum(shift_sums, axis=0).reshape(img_count, D) + bias_shift

    lat_masked = (latents * inside[..., None]).astype(BF)
    cot_masked = (cotangent * inside[..., None]).astype(BF)
    rims = with_halo(
        jnp.concatenate([lat_masked, cot_masked], axis=-1), (("row", 1), ("col", 2)), 1
    )
    rims = rims.astype(F32)
    near = gather_near(rims[..., :patch_vals], tile_rows, tile_cols)
    near = near.reshape(img_count, tokens, near_vals).astype(BF)
    cot_near = gather_near(rims[..., patch_vals:], tile_rows, tile_cols)
    cot_near = cot_near.reshape(img_count, tokens, near_vals)
    embedded = matmul_back(near, embed_t) + bias_embed
    joined_full = jnp.concatenate(
        [embedded, skip.reshape(img_count, tokens, D).astype(F32)], axis=-1
    )
    skip_normed, skip_norm_pull = jax.vjp(layer_norm, joined_full, skip_gains, skip_offsets)
    skip_in = skip_normed.astype(BF)
    resid_in = matmul(skip_in, skip_full) + bias_skip
    self_norm, self_norm_pull = jax.vjp(layer_norm, resid_in, gain_rows[0], offset_rows[0])
    normed = (self_norm + shift_rows[:, None, :]).astype(BF)

    qkv_t = dot(qkv_full, normed, (0,), (2,)) + bias_qkv[:, None, None]
    qkv_t = qkv_t.astype(BF).reshape(3, HEADS, HD, img_count, tokens)
    qkv_jobs = all_to_all(
        jnp.transpose(qkv_t, (1, 3, 0, 2, 4)).reshape(count, jobs, 3, HD, tokens)
    )
    head_cols = jnp.stack([head_gains[0], head_offsets[0], head_gains[1], head_offsets[1]], axis=1)
    mixed_jobs, keep, total = attend(ext_jobs, qkv_jobs, every_cos, every_sin, head_cols, geo)
    mixed = all_to_all(mixed_jobs).reshape(HEADS, img_count, HD, tokens)
    attended_t = jnp.transpose(mixed, (1, 0, 2, 3)).reshape(img_count, D, tokens)
    resid_self = resid_in + dot(attended_t, out_full, (1,), (0,)) + bias_out

    cross_norm, cross_norm_pull = jax.vjp(layer_norm, resid_self, gain_rows[1], offset_rows[1])
    cross_in = cross_norm.astype(BF)
    all_tokens = img_count * tokens
    cross_rows = dot(cross_q_full, cross_in.reshape(all_tokens, D), (0,), (1,))
    cross_rows = (cross_rows + bias_cross_q[:, None]).reshape(HEADS, HD, all_tokens)
    cross_cols = jnp.stack([head_gains[2], head_offsets[2]], axis=1)
    cross_mixed, cross_total = cross_attend(
        text_len, cross_rows, text_both, own_cos, own_sin, cross_cols
    )
    cross_low = cross_mixed.reshape(D, all_tokens)
    cross_out_rows = dot(cross_low, cross_o_full, (0,), (0,)).reshape(img_count, tokens, D)
    resid_cross = resid_self + cross_out_rows + bias_cross_o

    mlp_norm, mlp_norm_pull = jax.vjp(layer_norm, resid_cross, gain_rows[2], offset_rows[2])
    mlp_in = images_gather(mlp_norm.astype(BF))
    hidden = matmul(mlp_in, up_full) + bias_up_part
    gelu_out, gelu_pull = jax.vjp(gelu_tanh, hidden)
    activated = gelu_out.astype(BF)
    resid_out = resid_cross + images_scatter(matmul(activated, down_full)) + bias_down
    resid_low = resid_out.astype(BF)
    emitted = matmul(resid_low, final_full) * token_inside
    emit_rim = with_halo(
        emitted.reshape(img_count, tile_rows, tile_cols, near_vals), (("row", 1), ("col", 2)), 1
    )
    out_latents = spread_near(emit_rim, tile_rows, tile_cols, patch_vals) * inside[..., None]

    sums = Sums()
    lead = (0, 1)
    grad_emitted = (cot_near * token_inside).astype(BF)
    grad_final = weight_grad(resid_low, grad_emitted)
    grad_resid_out = matmul_back(grad_emitted, final_full)
    grad_down_low = grad_resid_out.astype(BF)
    bias_down_grad = column_sum(grad_down_low)
    grad_down_rows = images_gather(grad_down_low)
    every_lead = (0, 1, 2)
    activated, out_latents = lax.optimization_barrier((activated, out_latents))
    sums.begin(
        "down", activated, grad_down_rows, every_lead, every_lead, 3, after=all_images
    )
    grad_hidden = gelu_pull(matmul_back(grad_down_rows, down_full))[0].astype(BF)
    sums.begin("up", mlp_in, grad_hidden, every_lead, every_lead, 3, after=all_images)
    bias_up_grad = column_sum(grad_hidden)
    grad_mlp_in = sums.step(matmul_back(grad_hidden, up_full), "down")
    grad_mlp_in = sums.step(images_scatter(grad_mlp_in), "up")
    grad_from_mlp, gain_mlp_grad, shift_mlp_grad = mlp_norm_pull(grad_mlp_in)
    grad_resid_cross = grad_resid_out + grad_from_mlp

    grad_cross_low = grad_resid_cross.astype(BF)
    grad_cross_flat = grad_cross_low.reshape(all_tokens, D)
    sums.begin("cross_o", cross_low, grad_cross_flat, (1,), (0,), 0)
    bias_cross_o_grad = column_sum(grad_cross_low)
    grad_cross_mixed = dot(cross_o_full, grad_cross_flat, (1,), (1,)).astype(BF)
    grad_cross_mixed = sums.step(grad_cross_mixed, "cross_o")
    grad_cross_rows, grad_text, cross_head_grads = cross_attend_back(
        text_len, cross_rows, text_both, grad_cross_mixed.reshape(HEADS, HD, all_tokens),
        cross_total, own_cos, own_sin, cross_cols,
    )
    cross_head_grads = jnp.sum(cross_head_grads, axis=0)
    grad_cross_rows = grad_cross_rows.reshape(D, all_tokens)
    sums.begin("text", grad_text.reshape(2 * D, img_count * text_count), after=alone)
    sums.begin("cross_q", cross_in.reshape(all_tokens, D), grad_cross_rows, (0,), (1,), 1)
    bias_cross_q_grad = jnp.sum(grad_cross_rows.astype(F32), axis=1)
    grad_cross_in = dot(grad_cross_rows, cross_q_full, (0,), (1,))
    grad_cross_in = sums.step(grad_cross_in, "text", "cross_q", "down")
    grad_from_cross, gain_cross_grad, shift_cross_grad = cross_norm_pull(
        grad_cross_in.reshape(img_count, tokens, D)
    )
    grad_resid_self = grad_resid_cross + grad_from_cross

    grad_out_rows = grad_resid_self.astype(BF)
    sums.begin("out", attended_t, grad_out_rows, (0, 2), lead, 1)
    bias_out_grad = column_sum(grad_out_rows)
    grad_attended = dot(out_full, grad_out_rows, (1,), (2,)).astype(BF)
    grad_attended = jnp.transpose(
        grad_attended.reshape(HEADS, HD, img_count, tokens), (0, 2, 1, 3)
    )
    grad_mixed_jobs = all_to_all(grad_attended.reshape(count, jobs, HD, tokens))
    grad_mixed_jobs = sums.step(grad_mixed_jobs, "out", "up", "cross_o", "down")
    grad_jobs, head_grads = attend_back(
        ext_jobs, qkv_jobs, grad_mixed_jobs, keep, total, every_cos, every_sin, head_cols, geo
    )
    grad_jobs = sums.step(grad_jobs, "text", "cross_q", "up", "cross_o")
    grad_qkv_t = sums.step(all_to_all(grad_jobs), "out", "down").reshape(HEADS, img_count, 3, HD, tokens)
    grad_qkv_t = jnp.transpose(grad_qkv_t, (2, 0, 3, 1, 4)).reshape(3 * D, img_count, tokens)
    head_grads = jnp.sum(head_grads, axis=0)

    sums.begin("qkv", normed, grad_qkv_t, (0, 1), (1, 2), 2, 0, after=all_images)
    bias_qkv_grad = jnp.sum(grad_qkv_t.astype(F32), axis=(1, 2))
    grad_normed = sums.step(
        dot(grad_qkv_t, qkv_full, (0,), (1,)), "up", "cross_o", "text", "cross_q"
    )
    grad_shift_rows = jnp.sum(grad_normed, axis=1)
    bias_shift_grad = jnp.sum(grad_shift_rows, axis=0)
    grad_from_self, gain_self_grad, shift_self_grad = self_norm_pull(grad_normed)
    grad_resid_in = grad_resid_self + grad_from_self
    grad_merged = sums.step(grad_resid_in.astype(BF), "qkv", "out", "text")
    skip_cut = D // 256 * 128
    sums.begin("skip_a", skip_in, grad_merged[..., :-skip_cut], lead, lead, 2)
    sums.begin("skip_b", skip_in, grad_merged[..., -skip_cut:], lead, lead, 2, order=col_first())
    bias_skip_grad = column_sum(grad_merged)
    grad_skip_normed = sums.step(matmul_back(grad_merged, skip_full), "skip_a", "skip_b", "cross_q", "cross_o")
    grad_joined, skip_gain_grad, skip_shift_grad = skip_norm_pull(grad_skip_normed)
    grad_skip = grad_joined[..., D:].reshape(img_count, tile_rows, tile_cols, D)
    grad_embedded = sums.step(grad_joined[..., :D].astype(BF), "up", "out", "cross_q", "qkv")
    grad_embed_t = weight_grad(grad_embedded, near)
    bias_embed_grad = column_sum(grad_embedded)
    grad_near = matmul(grad_embedded, embed_t).reshape(
        img_count, tile_rows, tile_cols, near_vals
    )
    near_rim = with_halo(grad_near, (("row", 1), ("col", 2)), 1)
    grad_latents = spread_near(near_rim, tile_rows, tile_cols, patch_vals) * inside[..., None]

    shards = sums.finish()
    grad_text_lin, head_gain_ck_grad, head_shift_ck_grad = text_pull(shards["text"])
    grad_text_low = grad_text_lin.astype(BF)
    grad_cross_keys = images_sum(
        dot(
            text_wide, grad_text_low.reshape(text_width, img_count, text_count), (0, 1), (1, 2)
        ),
        BF,
    )
    grad_cross_bias = images_sum(jnp.sum(grad_text_low.astype(F32), axis=1), F32)

    def by_device(vector):
        return vector.reshape(count, -1)

    def rows_by_device(rows):
        return jnp.transpose(rows.reshape(3, count, shard), (1, 0, 2)).reshape(count, -1)

    bias_up_all = jnp.where(
        (jnp.arange(groups) == group_index)[None, :, None],
        bias_up_grad.reshape(count, 1, hid_part),
        0.0,
    ).reshape(-1)
    small_grads = jnp.concatenate(
        [
            by_device(grad_embed_t),
            by_device(grad_final),
            rows_by_device(jnp.stack([gain_self_grad, gain_cross_grad, gain_mlp_grad])),
            rows_by_device(jnp.stack([shift_self_grad, shift_cross_grad, shift_mlp_grad])),
            by_device(skip_gain_grad),
            by_device(skip_shift_grad),
            by_device(
                jnp.concatenate(
                    [head_grads[:, 0], head_grads[:, 2], cross_head_grads[:, 0], head_gain_ck_grad]
                )
            ),
            by_device(
                jnp.concatenate(
                    [head_grads[:, 1], head_grads[:, 3], cross_head_grads[:, 1], head_shift_ck_grad]
                )
            ),
            by_device(
                jnp.concatenate([bias_embed_grad, bias_skip_grad, bias_shift_grad, bias_qkv_grad])
            ),
            by_device(
                jnp.concatenate(
                    [
                        bias_out_grad, bias_cross_q_grad, bias_cross_o_grad, bias_up_all,
                        bias_down_grad,
                    ]
                )
            ),
        ],
        axis=1,
    )
    shift_share = jnp.broadcast_to(grad_shift_rows.reshape(1, -1), (count, img_count * D))
    small_grads = jnp.concatenate([small_grads, shift_share], axis=1).astype(BF)
    small_grads = jnp.pad(small_grads, ((0, 0), (0, padded_len - small_grads.shape[1])))
    small_got = all_to_all(small_grads.reshape(count, -1, 128)).astype(F32)
    small_got = jnp.sum(small_got, axis=0).reshape(-1)
    small_sum = images_sum(small_got[:small_len], F32)
    total_parts = cuts(small_sum, (wide, wide) + small_widths)
    grad_shift = lax.dot_general(
        time_own.astype(F32),
        small_got[small_len : small_len + img_count * D].reshape(img_count, D),
        (((0,), (0,)), ((), ())),
        precision=lax.Precision.HIGHEST,
    )

    total_up = jnp.transpose(
        shards["up"].reshape(groups, shard, count, hid_part), (1, 2, 0, 3)
    ).reshape(shard, FF)
    total_down = shards["down"].reshape(hid_shard, D)
    return (
        out_latents,
        grad_latents,
        grad_skip,
        total_parts[0].reshape(shard, near_vals).T,
        jnp.concatenate([shards["skip_a"], shards["skip_b"]], axis=1),
        images_sum(grad_shift, F32),
        jnp.concatenate([shards["qkv"][i] for i in range(groups)], axis=1).astype(F32),
        shards["out"],
        shards["cross_q"],
        grad_cross_keys,
        shards["cross_o"],
        total_up.astype(F32),
        total_down.astype(F32),
        total_parts[1].reshape(shard, near_vals),
        total_parts[2].reshape(3, shard),
        total_parts[3].reshape(3, shard),
        total_parts[4],
        total_parts[5],
        total_parts[6],
        total_parts[7],
        total_parts[8],
        total_parts[9],
        grad_cross_bias,
    )


def solution(mesh):
    tile = P("img", "row", "col", None)
    rows = P(GROUP, None)
    columns = P(None, GROUP)
    vector = P(GROUP)
    return jax.shard_map(
        body,
        mesh=mesh,
        in_specs=(
            tile, tile, P("img", None), P("img", None, None), P("img", None), P("img", None),
            columns, rows, rows, rows, rows, rows, columns, rows, rows, rows, rows,
            columns, columns, vector, vector, vector, vector, vector, vector, vector, tile,
        ),
        out_specs=(
            tile, tile, tile, columns, rows, rows, rows, rows, rows, columns, rows, rows, rows,
            rows, columns, columns, vector, vector, vector, vector, vector, vector, vector,
        ),
        check_vma=False,
    )
```

time: 3410 us -> 1260 us (0.37)
  waiting for transfers between devices: 2260 us -> 522 us
  blocking collectives: 282 us -> 0 us
  matrix products: 400 us -> 154 us
  starting transfers between devices: 30.5 us -> 117 us
  local copies, waits for them, and re-layouts: 294 us -> 221 us
  Pallas kernels: 0 us -> 70.3 us
  other arithmetic: 106 us -> 145 us
    reduce_scatter x4 -> x0, waiting for transfers between devices: 872 us -> none  [the longest x1 349 us: body(): lax.psum_scatter(grad_up, ('row', 'col'), scatter_dimension=0, tiled=True)]
    unnamed x35 -> x5, waiting for transfers between devices: 714 us -> 0.08 us
    all_gather x13 -> x5, waiting for transfers between devices: 437 us -> 137 us  [the longest x1 65.7 us: body(): down_full = lax.all_gather(down_part, GROUP, axis=0, tiled=True)]
    dot_general x51 -> x42, matrix products: 391 us -> 154 us  [the longest x41 153 us: dot(): lax.dot_general(former, latter, ((former_dims, latter_dims), ((), ())), p...]
    psum x2 -> x0, waiting for transfers between devices: 231 us -> none  [body(): lax.psum((shard_embed, shard_skip, shard_shift, shard_qkv, shard_out, sha...]
    all_gather x6 -> x0, blocking collectives: 218 us -> none  [the longest x1 41.8 us: body(): lax.all_gather(embed_weight, ('row', 'col'), axis=1, tiled=True)]
    ppermute x0 -> x54, waiting for transfers between devices: none -> 213 us  [the longest x37 110 us: exchange(): return lax.ppermute(values, axis, [(i, i ^ bit) for i in range(size)])]
    all_to_all x0 -> x6, waiting for transfers between devices: none -> 163 us  [all_to_all(): lax.all_to_all(values, GROUP, split_axis=0, concat_axis=0, tiled=True)]
  transfers between devices with their start and end apart: 39 -> 77, of which waited for: 21 -> 31; matrix products, arithmetic and copies ran while one was open for 20% -> 37% of each run, Pallas kernels for 0% -> 6%
where the time goes in v1:
time: 1260 us; the launch traced here: 1250 us
  waiting for transfers between devices  522 us (41%)
  local copies, waits for them, and re-layouts  221 us (18%)
  matrix products  154 us (12%)
  other arithmetic  145 us (12%)
  starting transfers between devices  117 us (9%)
  Pallas kernels  70.3 us (6%)
  between operations  18.1 us (1%)
    all_to_all x6, waiting for transfers between devices, all_to_all(): lax.all_to_all(values, GROUP, split_axis=0, concat_axis=0, tiled=True)  163 us
    dot_general x41, matrix products, dot(): lax.dot_general(former, latter, ((former_dims, latter_dims), ((), ())), p...  153 us
    ppermute x37, waiting for transfers between devices, exchange(): return lax.ppermute(values, axis, [(i, i ^ bit) for i in range(size)])  110 us
    ppermute x17, waiting for transfers between devices, swap_images(): return lax.ppermute(values, 'img', [(i, i ^ bit) for i in range(count)])  103 us
    all_gather x1, waiting for transfers between devices, body(): down_full = lax.all_gather(down_part, GROUP, axis=0, tiled=True)  65.7 us
    unnamed x599, local copies, waits for them, and re-layouts  50.3 us
    all_gather x1, waiting for transfers between devices, body(): first_all = lax.all_gather(first_rows, GROUP, axis=0, tiled=False)  41.1 us
    all_to_all x6, starting transfers between devices, all_to_all(): lax.all_to_all(values, GROUP, split_axis=0, concat_axis=0, tiled=True)  38.7 us
  transfers between devices with their start and end apart: 77, of which 31 were waited for; matrix products, arithmetic and copies ran while one was open for 37% of the time, Pallas kernels for 6%

profile of v1, /device:TPU:0, one launch (start us, length us, event | category | flops | bytes accessed | tf_op | source)
XLA Modules:
  0.0 1248.0 jit_solution(9401594800005502568)
XLA Ops:
  25.3 27.6 %all-to-all-done = bf16[16,240,128]{2,1,0:T(8,128)(2,1)} async-done(((bf16[16,240,128]{2,1,0:T(8,128)(2,1)}), bf16[16,240,128]{2,1,0:T(8,128)(2,1)}, u32[]{:S(2)}, u32[]{:S(2)}) %all-to-all-start) | async-done | bytes 983072 | tf_op jit(solution)/shard_map/all_to_all | solution.py:676
  98.0 41.1 %all-gather.13.cloned.1.call-done = bf16[7040,1408]{1,0:T(8,128)(2,1)} async-done(((bf16[440,1408]{1,0:T(8,128)(2,1)}), bf16[7040,1408]{1,0:T(8,128)(2,1)}) %all-gather.13.cloned.1.call-update) | async-done | bytes 19824656 | tf_op jit(solution)/shard_map/all_gather | solution.py:723
  181.2 11.0 fusion.8
  193.8 10.5 all-to-all-start.1
  217.4 68.0 %all-to-all-done.1.qkv_ref = bf16[16,2,3,88,128]{4,3,2,1,0:T(8,128)(2,1)S(1)} async-done(((bf16[16,2,3,88,128]{4,3,2,1,0:T(8,128)(2,1)}), bf16[16,2,3,88,128]{4,3,2,1,0:T(8,128)(2,1)S(1)}, u32[]{:S(2)}, u32[]{:S(2)}) %all-to-all-start.1) | async-done | bytes 2162720 | tf_op jit(solution)/shard_map/all_to_all | solution.py:676
  287.0 15.6 %shard_map.488 = (bf16[16,2,88,128]{3,2,1,0:T(8,128)(2,1)S(1)}, f32[2,88,2048]{2,1,0:T(8,128)S(1)}, f32[2,1,2048]{2,1,0:T(1,128)S(1)}) custom-call(s32[2,2]{1,0:T(2,128)S(1)} %broadcast_select_fusion.2.ext_ref, bf16[16,2,3,88,128]{4,3,2,1,0:T(8,128)(2,1)S(1)} %all-to-all-done.1.qkv_ref, f32[88,2048]{1,0:T(8,128)S(1)} %copy-done.5, ...), custom_call_target="tpu_custom_call" | custom-call | flops 8858370048 | bytes 6291456 | tf_op jit(solution)/shard_map/pallas_call | solution.py:402
  318.4 25.9 %all-to-all-done.2 = bf16[16,2,88,128]{3,2,1,0:T(8,128)(2,1)S(1)} async-done(((bf16[16,2,88,128]{3,2,1,0:T(8,128)(2,1)}), bf16[16,2,88,128]{3,2,1,0:T(8,128)(2,1)S(1)}, u32[]{:S(2)}, u32[]{:S(2)}) %all-to-all-start.2) | async-done | bytes 720928 | tf_op jit(solution)/shard_map/all_to_all | solution.py:676
  355.2 12.6 %shard_map.489 = (bf16[16,88,256]{2,1,0:T(8,128)(2,1)S(1)}, f32[16,1,256]{2,1,0:T(1,128)S(1)}) custom-call(s32[2,2]{1,0:T(2,128)S(1)} %copy-done.10, f32[16,88,256]{2,1,0:T(8,128)S(1)} %bitcast.472, bf16[2,16,88,768]{3,2,1,0:T(8,128)(2,1)S(1)} %bitcast.468, f32[88,256]{1,0:T(8,128)S(1)} %get-tuple-element.382.cos_ref, ...), custom_call_target="tpu_custom_call" | custom-call | flops 4294967296 | bytes 10485760 | tf_op jit(solution)/shard_map/pallas_call | solution.py:635
  393.0 30.2 %all-gather.11.cloned.1.call-done = bf16[1408,3072]{1,0:T(8,128)(2,1)} async-done(((bf16[88,3072]{1,0:T(8,128)(2,1)}), bf16[1408,3072]{1,0:T(8,128)(2,1)}) %all-gather.11.cloned.1.call-update) | async-done | bytes 8650768 | tf_op jit(solution)/shard_map/all_gather | solution.py:735
  423.2 11.2 multiply_convert_fusion
  434.4 65.7 %all-gather.17.cloned.1.call-done = bf16[1,3072,1408]{2,1,0:T(8,128)(2,1)} async-done(((bf16[1,192,1408]{2,1,0:T(8,128)(2,1)}), bf16[1,3072,1408]{2,1,0:T(8,128)(2,1)}) %all-gather.17.cloned.1.call-update) | async-done | bytes 8650768 | tf_op jit(solution)/shard_map/all_gather | solution.py:739
  500.1 9.3 fusion.6
  515.1 13.5 %collective-permute-done.5 = bf16[1,2,128,1408]{3,2,1,0:T(8,128)(2,1)S(1)} collective-permute-done((bf16[1,2,128,1408]{3,2,1,0:T(8,128)(2,1)S(1)}, bf16[1,2,128,1408]{3,2,1,0:T(8,128)(2,1)S(1)}, u32[]{:S(2)}, u32[]{:S(2)}) %collective-permute-start.5) | collective-permute-done | bytes 720928 | tf_op jit(solution)/shard_map/ppermute | solution.py:112
  558.6 11.4 convert_reduce_fusion
  606.5 10.4 collective-permute-done.12
  642.6 15.7 %shard_map.490 = (bf16[16,88,256]{2,1,0:T(8,128)(2,1)S(1)}, bf16[2,16,88,768]{3,2,1,0:T(8,128)(2,1)S(1)}, f32[8,88,2]{2,1,0:T(8,128)S(1)}) custom-call(s32[2,2]{1,0:T(2,128)S(1)} %copy-done.10, f32[16,88,256]{2,1,0:T(8,128)S(1)} %bitcast.473, bf16[2,16,88,768]{3,2,1,0:T(8,128)(2,1)S(1)} %bitcast.471, bf16[16,88,256]{2,1,0:T(8,128)(2,1)S(1)} %bitcast.474, ...), custom_call_target="tpu_custom_call" | custom-call | flops 8589934592 | bytes 16777216 | tf_op jit(solution)/shard_map/pallas_call | solution.py:655
  731.9 20.6 %collective-permute-done.20 = bf16[2,2,88,1408]{3,2,0,1:T(8,128)(2,1)} collective-permute-done((bf16[2,2,88,1408]{3,2,0,1:T(8,128)(2,1)}, bf16[2,2,88,1408]{3,2,0,1:T(8,128)(2,1)}, u32[]{:S(2)}, u32[]{:S(2)}) %collective-permute-start.20) | collective-permute-done | bytes 991264 | tf_op jit(solution)/shard_map/ppermute | solution.py:140
  764.7 26.4 %shard_map.491 = (bf16[16,2,3,88,128]{4,3,2,1,0:T(8,128)(2,1)}, f32[2,88,4]{2,1,0:T(8,128)}) custom-call(s32[2,2]{1,0:T(2,128)} %copy-done.8, bf16[16,2,3,88,128]{4,3,2,1,0:T(8,128)(2,1)} %copy-done.3, bf16[16,2,88,128]{3,2,1,0:T(8,128)(2,1)} %all-to-all-done.3.dout_ref, f32[2,88,2048]{2,1,0:T(8,128)} %copy-done.11, f32[2,1,2048]{2,1,0:T(1,128)} %copy-done.12, ...), custom_call_target="tpu_custom_call" | custom-call | flops 22145925120 | bytes 8388608 | tf_op jit(solution)/shard_map/pallas_call | solution.py:506
  824.7 20.4 %collective-permute-done.27 = bf16[192,1408]{1,0:T(8,128)(2,1)} collective-permute-done((bf16[192,1408]{1,0:T(8,128)(2,1)}, bf16[192,1408]{1,0:T(8,128)(2,1)}, u32[]{:S(2)}, u32[]{:S(2)}) %collective-permute-start.27) | collective-permute-done | bytes 540704 | tf_op jit(solution)/shard_map/ppermute | solution.py:140
  846.5 40.4 %all-to-all-done.4 = bf16[16,2,3,88,128]{4,3,2,1,0:T(8,128)(2,1)S(1)} async-done(((bf16[16,2,3,88,128]{4,3,2,1,0:T(8,128)(2,1)}), bf16[16,2,3,88,128]{4,3,2,1,0:T(8,128)(2,1)S(1)}, u32[]{:S(2)}, u32[]{:S(2)}) %all-to-all-start.4) | async-done | bytes 2162720 | tf_op jit(solution)/shard_map/all_to_all | solution.py:676
  947.1 11.5 collective-permute-done.35
  1022.9 58.3 %collective-permute-done.42 = bf16[88,1408]{1,0:T(8,128)(2,1)S(1)} collective-permute-done((bf16[88,1408]{1,0:T(8,128)(2,1)}, bf16[88,1408]{1,0:T(8,128)(2,1)S(1)}, u32[]{:S(2)}, u32[]{:S(2)}) %collective-permute-start.42) | collective-permute-done | bytes 247840 | tf_op jit(solution)/shard_map/ppermute | solution.py:112
  1154.7 23.5 %collective-permute-done.55 = bf16[176,640]{1,0:T(8,128)(2,1)S(1)} collective-permute-done((bf16[176,640]{1,0:T(8,128)(2,1)S(1)}, bf16[176,640]{1,0:T(8,128)(2,1)S(1)}, u32[]{:S(2)}, u32[]{:S(2)}) %collective-permute-start.55) | collective-permute-done | bytes 225312 | tf_op jit(solution)/shard_map/ppermute | solution.py:140
  1214.9 14.0 %collective-permute-done.60 = bf16[88,2112]{1,0:T(8,128)(2,1)S(1)} collective-permute-done((bf16[88,2112]{1,0:T(8,128)(2,1)S(1)}, bf16[88,2112]{1,0:T(8,128)(2,1)S(1)}, u32[]{:S(2)}, u32[]{:S(2)}) %collective-permute-start.60) | collective-permute-done | bytes 371744 | tf_op jit(solution)/shard_map/ppermute | solution.py:140
  (1142 shorter events, 635.2 us)
Async XLA Ops:
  7.2 131.9 %all-gather.13.cloned.1.call-start = ((), (), s32[]{:S(2)}) async-start(), calls=%async_computation.8 | async-start | bytes 21063680 | tf_op jit(solution)/shard_map/all_gather | solution.py:723
  11.0 298.7 %all-gather.15.cloned.1.call-start = ((), (), s32[]{:S(2)}) async-start(), calls=%async_computation.9 | async-start | bytes 12638208 | tf_op jit(solution)/shard_map/all_gather | solution.py:728
  21.9 330.8 %all-gather.9.cloned.1.call-start = ((), (), s32[]{:S(2)}) async-start(), calls=%async_computation.6 | async-start | bytes 4595712 | tf_op jit(solution)/shard_map/all_gather | solution.py:796
  57.3 365.9 %all-gather.11.cloned.1.call-start = ((), (), s32[]{:S(2)}) async-start(), calls=%async_computation.7 | async-start | bytes 9191424 | tf_op jit(solution)/shard_map/all_gather | solution.py:735
  68.0 432.1 %all-gather.17.cloned.1.call-start = ((), (), s32[]{:S(2)}) async-start(), calls=%async_computation.10 | async-start | bytes 9191424 | tf_op jit(solution)/shard_map/all_gather | solution.py:739
  193.8 91.6 %all-to-all-start.1 = ((bf16[16,2,3,88,128]{4,3,2,1,0:T(8,128)(2,1)}), bf16[16,2,3,88,128]{4,3,2,1,0:T(8,128)(2,1)S(1)}, u32[]{:S(2)}, u32[]{:S(2)}) async-start(bf16[16,2,3,88,128]{4,3,2,1,0:T(8,128)(2,1)} %bitcast.517), calls=%async_computation.1 | async-start | bytes 4325376 | tf_op jit(solution)/shard_map/all_to_all | solution.py:676
  667.2 64.0 %collective-permute-start.19 = (bf16[2,2,88,3072]{3,2,1,0:T(8,128)(2,1)}, bf16[2,2,88,3072]{3,2,1,0:T(8,128)(2,1)}, u32[]{:S(2)}, u32[]{:S(2)}) collective-permute-start(bf16[2,2,88,3072]{3,2,1,0:T(8,128)(2,1)} %fusion.26), channel_id=1, source_target_pairs={{0,8},{4,12},{8,0},{12,4},{1,9},{5,13},{9,1},{13,5},{2,10},{6,14},... | collective-permute-start | bytes 6488072 | tf_op jit(solution)/shard_map/ppermute | solution.py:140
  674.1 78.3 %collective-permute-start.20 = (bf16[2,2,88,1408]{3,2,0,1:T(8,128)(2,1)}, bf16[2,2,88,1408]{3,2,0,1:T(8,128)(2,1)}, u32[]{:S(2)}, u32[]{:S(2)}) collective-permute-start(bf16[2,2,88,1408]{3,2,0,1:T(8,128)(2,1)} %fusion.54), channel_id=1, source_target_pairs={{0,8},{4,12},{8,0},{12,4},{1,9},{5,13},{9,1},{13,5},{2,10},{6,14},... | collective-permute-start | bytes 2973704 | tf_op jit(solution)/shard_map/ppermute | solution.py:140
  697.2 56.2 %all-to-all-start.3 = ((bf16[16,2,88,128]{3,2,1,0:T(8,128)(2,1)}), bf16[16,2,88,128]{3,2,1,0:T(8,128)(2,1)}, u32[]{:S(2)}, u32[]{:S(2)}) async-start(bf16[16,2,88,128]{3,2,1,0:T(8,128)(2,1)} %bitcast.457), calls=%async_computation.3 | async-start | bytes 1441792 | tf_op jit(solution)/shard_map/all_to_all | solution.py:676
  717.7 81.0 %collective-permute-start.22 = (bf16[2,2,176,768]{3,2,0,1:T(8,128)(2,1)}, bf16[2,2,176,768]{3,2,0,1:T(8,128)(2,1)}, u32[]{:S(2)}, u32[]{:S(2)}) collective-permute-start(bf16[2,2,176,768]{3,2,0,1:T(8,128)(2,1)} %fusion.50), channel_id=1, source_target_pairs={{0,8},{4,12},{8,0},{12,4},{1,9},{5,13},{9,1},{13,5},{2,10},{6,14},... | collective-permute-start | bytes 3244040 | tf_op jit(solution)/shard_map/ppermute | solution.py:140
  731.2 67.4 %collective-permute-start.23 = (bf16[2,2,88,1408]{3,2,0,1:T(8,128)(2,1)}, bf16[2,2,88,1408]{3,2,0,1:T(8,128)(2,1)}, u32[]{:S(2)}, u32[]{:S(2)}) collective-permute-start(bf16[2,2,88,1408]{3,2,0,1:T(8,128)(2,1)} %fusion.55), channel_id=1, source_target_pairs={{0,8},{4,12},{8,0},{12,4},{1,9},{5,13},{9,1},{13,5},{2,10},{6,14},... | collective-permute-start | bytes 2973704 | tf_op jit(solution)/shard_map/ppermute | solution.py:140
  798.9 88.0 %all-to-all-start.4 = ((bf16[16,2,3,88,128]{4,3,2,1,0:T(8,128)(2,1)}), bf16[16,2,3,88,128]{4,3,2,1,0:T(8,128)(2,1)S(1)}, u32[]{:S(2)}, u32[]{:S(2)}) async-start(bf16[16,2,3,88,128]{4,3,2,1,0:T(8,128)(2,1)} %get-tuple-element.101), calls=%async_computation.4 | async-start | bytes 4325376 | tf_op jit(solution)/shard_map/all_to_all | solution.py:676
  811.9 96.9 %collective-permute-start.29 = (bf16[88,1408]{1,0:T(8,128)(2,1)}, bf16[88,1408]{1,0:T(8,128)(2,1)}, u32[]{:S(2)}, u32[]{:S(2)}) collective-permute-start(bf16[88,1408]{1,0:T(8,128)(2,1)} %fusion.143), channel_id=1, source_target_pairs={{0,2},{1,3},{2,0},{3,1},{4,6},{5,7},{6,4},{7,5},{8,10},{9,11},{10,... | collective-permute-start | bytes 743432 | tf_op jit(solution)/shard_map/ppermute | solution.py:140
  821.7 88.7 %collective-permute-start.31 = (bf16[2,88,1408]{2,1,0:T(8,128)(2,1)}, bf16[2,88,1408]{2,1,0:T(8,128)(2,1)}, u32[]{:S(2)}, u32[]{:S(2)}) collective-permute-start(bf16[2,88,1408]{2,1,0:T(8,128)(2,1)} %fusion.99), channel_id=1, source_target_pairs={{0,1},{1,0},{2,3},{3,2},{4,5},{5,4},{6,7},{7,6},{8,9},{9,8},{10,11... | collective-permute-start | bytes 1486856 | tf_op jit(solution)/shard_map/ppermute | solution.py:140
  823.2 87.2 %collective-permute-start.30 = (bf16[2,176,768]{2,1,0:T(8,128)(2,1)S(1)}, bf16[2,176,768]{2,1,0:T(8,128)(2,1)S(1)}, u32[]{:S(2)}, u32[]{:S(2)}) collective-permute-start(bf16[2,176,768]{2,1,0:T(8,128)(2,1)S(1)} %fusion.93), channel_id=1, source_target_pairs={{0,1},{1,0},{2,3},{3,2},{4,5},{5,4},{6,7},{7,6},{8,9},{9,8},{10,11... | collective-permute-start | bytes 1622024 | tf_op jit(solution)/shard_map/ppermute | solution.py:140
  845.1 66.1 %collective-permute-start.28 = (bf16[88,3072]{1,0:T(8,128)(2,1)}, bf16[88,3072]{1,0:T(8,128)(2,1)}, u32[]{:S(2)}, u32[]{:S(2)}) collective-permute-start(bf16[88,3072]{1,0:T(8,128)(2,1)} %fusion.92), channel_id=1, source_target_pairs={{0,2},{1,3},{2,0},{3,1},{4,6},{5,7},{6,4},{7,5},{8,10},{9,11},{10,... | collective-permute-start | bytes 1622024 | tf_op jit(solution)/shard_map/ppermute | solution.py:140
  893.9 64.7 %collective-permute-start.34 = (bf16[2,88,1408]{2,1,0:T(8,128)(2,1)}, bf16[2,88,1408]{2,1,0:T(8,128)(2,1)}, u32[]{:S(2)}, u32[]{:S(2)}) collective-permute-start(bf16[2,88,1408]{2,1,0:T(8,128)(2,1)} %fusion.100), channel_id=1, source_target_pairs={{0,1},{1,0},{2,3},{3,2},{4,5},{5,4},{6,7},{7,6},{8,9},{9,8},{10,11... | collective-permute-start | bytes 1486856 | tf_op jit(solution)/shard_map/ppermute | solution.py:140
  918.5 76.5 %collective-permute-start.38 = (bf16[88,1408]{1,0:T(8,128)(2,1)}, bf16[88,1408]{1,0:T(8,128)(2,1)}, u32[]{:S(2)}, u32[]{:S(2)}) collective-permute-start(bf16[88,1408]{1,0:T(8,128)(2,1)} %fusion.144), channel_id=1, source_target_pairs={{0,2},{1,3},{2,0},{3,1},{4,6},{5,7},{6,4},{7,5},{8,10},{9,11},{10,... | collective-permute-start | bytes 743432 | tf_op jit(solution)/shard_map/ppermute | solution.py:140
  999.6 81.6 %collective-permute-start.43 = (bf16[704,2112]{1,0:T(8,128)(2,1)}, bf16[704,2112]{1,0:T(8,128)(2,1)}, u32[]{:S(2)}, u32[]{:S(2)}) collective-permute-start(bf16[704,2112]{1,0:T(8,128)(2,1)} %fusion.18), channel_id=1, source_target_pairs={{0,16},{16,0},{1,17},{17,1},{2,18},{18,2},{3,19},{19,3},{4,20},{20... | collective-permute-start | bytes 8921096 | tf_op jit(solution)/shard_map/ppermute | solution.py:112
  1006.8 74.4 %collective-permute-start.42 = (bf16[88,1408]{1,0:T(8,128)(2,1)}, bf16[88,1408]{1,0:T(8,128)(2,1)S(1)}, u32[]{:S(2)}, u32[]{:S(2)}) collective-permute-start(bf16[88,1408]{1,0:T(8,128)(2,1)} %fusion.102), channel_id=1, source_target_pairs={{0,16},{16,0},{1,17},{17,1},{2,18},{18,2},{3,19},{19,3},{4,20},{20... | collective-permute-start | bytes 743432 | tf_op jit(solution)/shard_map/ppermute | solution.py:112
  1020.6 95.9 %collective-permute-start.53 = (bf16[2,2,176,640]{3,2,0,1:T(8,128)(2,1)}, bf16[2,2,176,640]{3,2,0,1:T(8,128)(2,1)}, u32[]{:S(2)}, u32[]{:S(2)}) collective-permute-start(bf16[2,2,176,640]{3,2,0,1:T(8,128)(2,1)} %fusion.63), channel_id=1, source_target_pairs={{0,1},{1,0},{2,3},{3,2},{4,5},{5,4},{6,7},{7,6},{8,9},{9,8},{10,11... | collective-permute-start | bytes 2703368 | tf_op jit(solution)/shard_map/ppermute | solution.py:140
  1021.9 100.4 %collective-permute-start.49 = (bf16[2,2,176,768]{3,2,0,1:T(8,128)(2,1)}, bf16[2,2,176,768]{3,2,0,1:T(8,128)(2,1)}, u32[]{:S(2)}, u32[]{:S(2)}) collective-permute-start(bf16[2,2,176,768]{3,2,0,1:T(8,128)(2,1)} %fusion.51), channel_id=1, source_target_pairs={{0,8},{4,12},{8,0},{12,4},{1,9},{5,13},{9,1},{13,5},{2,10},{6,14},... | collective-permute-start | bytes 3244040 | tf_op jit(solution)/shard_map/ppermute | solution.py:140
  1085.9 94.5 %collective-permute-start.62 = (bf16[88,1408]{1,0:T(8,128)(2,1)S(1)}, bf16[88,1408]{1,0:T(8,128)(2,1)}, u32[]{:S(2)}, u32[]{:S(2)}) collective-permute-start(bf16[88,1408]{1,0:T(8,128)(2,1)S(1)} %fusion.101), channel_id=1, source_target_pairs={{0,16},{16,0},{1,17},{17,1},{2,18},{18,2},{3,19},{19,3},{4,20},{20... | collective-permute-start | bytes 743432 | tf_op jit(solution)/shard_map/ppermute | solution.py:112
  1089.1 104.8 %all-to-all-start.5 = ((bf16[16,240,128]{2,1,0:T(8,128)(2,1)}), bf16[16,240,128]{2,1,0:T(8,128)(2,1)S(1)}, u32[]{:S(2)}, u32[]{:S(2)}) async-start(bf16[16,240,128]{2,1,0:T(8,128)(2,1)} %bitcast.214), calls=%async_computation.5 | async-start | bytes 1966080 | tf_op jit(solution)/shard_map/all_to_all | solution.py:676
  (339 other events, 4583.3 us)
Sparse Core Ops, SparseCore 0:
  11.1 127.9 all-gather.12
  141.9 136.6 all-gather.14
  281.5 63.8 all-gather.8
  347.6 75.5 all-gather.10
  425.4 74.7 all-gather.16

commit v2 on v1

--- a/solution.py
+++ b/solution.py
@@ -136,6 +136,8 @@
 
 
 def exchange(values, axis, bit):
+    if bit is None:
+        return lax.psum_scatter(values, axis, scatter_dimension=0, tiled=True)
     size = lax.axis_size(axis)
     return lax.ppermute(values, axis, [(i, i ^ bit) for i in range(size)])
 
@@ -163,55 +165,19 @@
     return row_bits + [("col", 1 << i) for i in range(cols.bit_length() - 1)]
 
 
-def col_first():
-    return sorted(row_first())
-
-
 def shard_sum(order, after, inputs, grads, input_lead, grad_lead, feature):
     core = lax.axis_index("row") % 2
     give = dot(core_features(inputs, feature, 1 - core), grads, input_lead, grad_lead)
-    got = yield exchange(give.astype(BF), "row", 1)
+    (got,) = yield [give.astype(BF)], "row", 1
     keep = dot(core_features(inputs, feature, core), grads, input_lead, grad_lead)
     part = yield from scatter_sum(order, keep + got.astype(F32))
     part = yield from after(part)
     return part
 
 
-def image_parts(grads, dim):
-    groups, me = lax.axis_size("img"), lax.axis_index("img")
-    width = grads.shape[dim] // groups
-    return [
-        lax.dynamic_slice_in_dim(grads, (me ^ i) * width, width, dim) for i in range(groups)
-    ]
-
-
-def image_first_sum(order, after, inputs, grads, input_lead, grad_lead, feature, grad_feature):
-    core = lax.axis_index("row") % 2
-    parts = image_parts(grads, grad_feature)
-    given = core_features(inputs, feature, 1 - core)
-    gots = yield [
-        exchange(dot(given, part, input_lead, grad_lead).astype(BF), "row", 1) for part in parts
-    ]
-    kept = core_features(inputs, feature, core)
-    sums = [
-        dot(kept, part, input_lead, grad_lead) + got.astype(F32) for part, got in zip(parts, gots)
-    ]
-    while len(sums) > 1:
-        half = len(sums) // 2
-        gots = yield [swap_images(part.astype(BF), half) for part in sums[half:]]
-        sums = [part + got.astype(F32) for part, got in zip(sums, gots)]
-    part = yield from scatter_sum(order, sums[0])
-    part = yield from after(part)
-    return part
-
-
-def row_sum(order, after, values):
-    rows = lax.axis_size("row")
-    split = values.reshape(rows // 2, 2, -1, values.shape[-1])
-    keep, give = halves(split, 1, lax.axis_index("row") % 2)
-    got = yield exchange(give, "row", 1)
-    part = yield from scatter_sum(order, keep.astype(F32) + got.astype(F32))
-    part = yield from after(part)
+def offload_sum(after, part):
+    (got,) = yield [part.astype(BF)], GROUP, None
+    part = yield from after(got.astype(F32))
     return part
 
 
@@ -224,7 +190,7 @@
         at = dims.index((axis, bit))
         keep, give = halves(part, at, lax.axis_index(axis) // bit % 2)
         del dims[at]
-        got = yield exchange(give.astype(BF), axis, bit)
+        (got,) = yield [give.astype(BF)], axis, bit
         part = keep + got.astype(F32)
     return part.reshape(-1, width)
 
@@ -234,20 +200,10 @@
     yield
 
 
-def over_images(part):
-    bit = 1
-    while bit < lax.axis_size("img"):
-        part = part.astype(BF)
-        got = yield swap_images(part, bit)
-        part = part.astype(F32) + got.astype(F32)
-        bit *= 2
-    return part
-
-
 def all_images(part):
     bit, blocks = 1, part.astype(BF)[None]
     while bit < lax.axis_size("img"):
-        got = yield swap_images(blocks, bit)
+        (got,) = yield [blocks], "img", bit
         blocks = placed(blocks, got, lax.axis_index("img") // bit % 2, 0)
         blocks = blocks.reshape((-1,) + part.shape)
         bit *= 2
@@ -260,56 +216,50 @@
     return jnp.stack([first, last], axis=dim)
 
 
-def gather_rows(values):
-    rows, cols = lax.axis_size("row"), lax.axis_size("col")
-    row_index, col_index = lax.axis_index("row"), lax.axis_index("col")
-    tail = values.shape
-    bit, blocks = cols // 2, values[None]
-    while bit >= 1:
-        blocks = placed(blocks, exchange(blocks, "col", bit), col_index // bit % 2, 1)
-        blocks = blocks.reshape((-1,) + tail)
-        bit //= 2
-    blocks = blocks[None]
-    bit = rows // 2
-    while bit >= 1:
-        blocks = placed(blocks, exchange(blocks, "row", bit), row_index // bit % 2, 1)
-        blocks = blocks.reshape((-1, cols) + tail)
-        bit //= 2
-    return blocks.reshape((-1,) + tail[1:])
-
-
-class Sums:
+class Moves:
     def __init__(self):
         self.running = {}
         self.done = {}
 
-    def begin(self, name, *work, order=None, after=over_images):
-        kind = {1: row_sum, 5: shard_sum, 6: image_first_sum}[len(work)]
-        maker = kind(order or row_first(), after, *work)
-        self.running[name] = (maker, next(maker))
+    def begin(self, value, **makers):
+        return self.launch(value, {name: (maker, next(maker)) for name, maker in makers.items()})
+
+    def launch(self, value, wanted):
+        if not wanted:
+            return value
+        gives = {name: request[0] for name, (_, request) in wanted.items()}
+        value, gives = lax.optimization_barrier((value, gives))
+        for name, (maker, (_, axis, bit)) in wanted.items():
+            self.running[name] = (maker, [exchange(give, axis, bit) for give in gives[name]])
+        return value
 
     def step(self, value, *names):
         names = [name for name in names if name in self.running]
         if not names:
             return value
-        tied = lax.optimization_barrier((value, *[self.running[name][1] for name in names]))
-        for name, got in zip(names, tied[1:]):
-            self.move(name, got)
-        return tied[0]
-
-    def move(self, name, got):
-        maker = self.running[name][0]
-        try:
-            self.running[name] = (maker, maker.send(got))
-        except StopIteration as stop:
-            del self.running[name]
-            self.done[name] = stop.value
-
-    def finish(self):
-        while self.running:
-            for name in list(self.running):
-                self.move(name, self.running[name][1])
-        return self.done
+        value, gots = lax.optimization_barrier(
+            (value, {name: self.running[name][1] for name in names})
+        )
+        wanted = {}
+        for name in names:
+            maker = self.running.pop(name)[0]
+            try:
+                wanted[name] = (maker, maker.send(gots[name]))
+            except StopIteration as stop:
+                self.done[name] = stop.value
+        return self.launch(value, wanted)
+
+    def finish(self, *names):
+        waiting = [name for name in names if name in self.running]
+        while waiting:
+            for name in waiting:
+                maker, gots = self.running.pop(name)
+                try:
+                    gives, axis, bit = maker.send(gots)
+                    self.running[name] = (maker, [exchange(give, axis, bit) for give in gives])
+                except StopIteration as stop:
+                    self.done[name] = stop.value
+            waiting = [name for name in names if name in self.running]
 
 
 def unit_rows(values):
@@ -672,6 +622,257 @@
     )(lengths, rows, text, dout, total, cos, sin, head)
 
 
+MESH = pl.DeviceIdType.MESH
+
+
+def sum_plan(sizes, rows_first):
+    groups, row_count, cols = sizes
+    count, height = row_count * cols // 2, 16 * groups
+    image_bits = [("img", 1 << i) for i in range(groups.bit_length() - 1)]
+    row_bits = [("row", 1 << i) for i in range(1, row_count.bit_length() - 1)]
+    col_bits = [("col", 1 << i) for i in range(cols.bit_length() - 1)]
+    plan = []
+    for axis, bit in (row_bits + image_bits if rows_first else image_bits + row_bits) + col_bits:
+        if axis == "img":
+            height //= 2
+        else:
+            count //= 2
+        plan.append((axis, bit, count, height))
+    return plan
+
+
+def sum_kernel(sizes, steps, grads_ref, out_ref, *scratch):
+    groups, row_count, cols = sizes
+    height = 16 * groups
+    first_count = row_count * cols // 2
+    places = {axis: lax.axis_index(axis) for axis in ("img", "row", "col")}
+    plans = [sum_plan(sizes, False), sum_plan(sizes, True)]
+    stages = len(plans[0])
+    image_stages = groups.bit_length() - 1
+    held = [scratch[: stages + 1], scratch[stages + 1 : 2 * stages + 2]]
+    own, send_sem, recv_sem, spread_sem, spread_recv, own_sem, out_sem = scratch[2 * stages + 2 :]
+    core = places["row"] % 2
+
+    def partner(axis, bit):
+        place = dict(places)
+        part = place[axis] // bit % 2
+        place[axis] = place[axis] + bit - 2 * bit * part
+        return tuple(place[name] for name in ("img", "row", "col"))
+
+    def bit_of(axis, bit):
+        return places[axis] // bit % 2
+
+    def chunk_rows(kind, chunk):
+        return pl.multiple_of((2 * chunk + kind) * height, 16)
+
+    def first_copies(kind, chunk):
+        rows = pl.ds(chunk_rows(kind, chunk), height)
+        for i in range(row_count // 2):
+            shards = pl.ds((2 * i + 1 - core) * cols, cols)
+            yield pltpu.make_async_remote_copy(
+                src_ref=grads_ref.at[shards, rows],
+                dst_ref=held[kind][0].at[chunk, pl.ds(i * cols, cols)],
+                send_sem=send_sem.at[kind, 0, chunk],
+                recv_sem=recv_sem.at[kind, 0, chunk],
+                device_id=partner("row", 1),
+                device_id_type=MESH,
+            )
+
+    def own_copies(kind, chunk):
+        rows = pl.ds(chunk_rows(kind, chunk), height)
+        for i in range(row_count // 2):
+            shards = pl.ds((2 * i + core) * cols, cols)
+            yield pltpu.make_async_copy(
+                grads_ref.at[shards, rows],
+                own.at[kind, lax.rem(chunk, 2), pl.ds(i * cols, cols)],
+                own_sem.at[kind, lax.rem(chunk, 2)],
+            )
+
+    def split(kind, stage):
+        axis, bit, count, rows = plans[kind][stage]
+        part = bit_of(axis, bit)
+        if axis == "img":
+            return (
+                [((pl.ds(0, count), pl.ds(pl.multiple_of((1 - part) * rows, 16), rows)), pl.ds(0, count))],
+                lambda i: (i, pl.ds(pl.multiple_of(part * rows, 16), rows)),
+            )
+        if axis == "row":
+            return (
+                [((pl.ds((1 - part) * count, count), pl.ds(0, rows)), pl.ds(0, count))],
+                lambda i: (part * count + i, pl.ds(0, rows)),
+            )
+        return (
+            [((pl.ds(2 * i + 1 - part, 1), pl.ds(0, rows)), pl.ds(i, 1)) for i in range(count)],
+            lambda i: (2 * i + part, pl.ds(0, rows)),
+        )
+
+    def stage_copies(kind, stage, chunk):
+        axis, bit, count, rows = plans[kind][stage]
+        for (shards, lines), target in split(kind, stage)[0]:
+            yield pltpu.make_async_remote_copy(
+                src_ref=held[kind][stage].at[chunk, shards, lines],
+                dst_ref=held[kind][stage + 1].at[chunk, target],
+                send_sem=send_sem.at[kind, stage + 1, chunk],
+                recv_sem=recv_sem.at[kind, stage + 1, chunk],
+                device_id=partner(axis, bit),
+                device_id_type=MESH,
+            )
+
+    def whole(kind, stage, chunk):
+        buffer = held[kind][stage].at[chunk]
+        return pltpu.make_async_remote_copy(
+            src_ref=buffer,
+            dst_ref=buffer,
+            send_sem=send_sem.at[kind, stage, chunk],
+            recv_sem=recv_sem.at[kind, stage, chunk],
+            device_id=partner("row", 1),
+            device_id_type=MESH,
+        )
+
+    last_rows = plans[0][-1][3]
+
+    def out_rows(kind, chunk):
+        return pl.ds(pl.multiple_of(chunk_rows(kind, chunk) + image_place() * last_rows, 16), last_rows)
+
+    def image_place():
+        place = 0
+        for i in range(image_stages):
+            place = place + bit_of("img", 1 << i) * (1 << (image_stages - 1 - i))
+        return place
+
+    def spread_copies(kind, chunk):
+        for i in range(1, groups):
+            place = dict(places)
+            place["img"] = lax.rem(places["img"] + i, groups)
+            yield pltpu.make_async_remote_copy(
+                src_ref=held[kind][stages].at[chunk, 0],
+                dst_ref=out_ref.at[out_rows(kind, chunk)],
+                send_sem=spread_sem.at[kind, i, chunk],
+                recv_sem=spread_recv.at[kind, i, chunk],
+                device_id=tuple(place[name] for name in ("img", "row", "col")),
+                device_id_type=MESH,
+            )
+
+    def home_copy(kind, chunk):
+        return pltpu.make_async_copy(
+            held[kind][stages].at[chunk, 0],
+            out_ref.at[out_rows(kind, chunk)],
+            out_sem.at[kind, chunk],
+        )
+
+    def start(copies):
+        for copy in copies:
+            copy.start()
+
+    barrier = pltpu.get_barrier_semaphore()
+    near = [partner("row", 1)] + [partner(a, b) for a, b, _, _ in plans[0] if a != "img"]
+    for i in range(1, groups):
+        place = dict(places)
+        place["img"] = lax.rem(places["img"] + i, groups)
+        near.append(tuple(place[name] for name in ("img", "row", "col")))
+    for other in near:
+        pl.semaphore_signal(barrier, inc=1, device_id=other, device_id_type=MESH)
+    pl.semaphore_wait(barrier, len(near))
+
+    def begin(chunk):
+        for kind in range(2):
+            start(first_copies(kind, chunk))
+            start(own_copies(kind, chunk))
+
+    begin(0)
+
+    def time_step(t, carry):
+        for stage in range(stages, -1, -1):
+            chunk = t - stage
+
+            @pl.when(jnp.logical_and(chunk >= 0, chunk < steps))
+            def _(stage=stage, chunk=chunk):
+                if stage == 0:
+
+                    @pl.when(chunk + 1 < steps)
+                    def _():
+                        begin(chunk + 1)
+
+                for kind in range(2):
+                    buffer = held[kind][stage]
+                    whole(kind, stage, chunk).wait_recv()
+                    if stage == 0:
+                        for copy in own_copies(kind, chunk):
+                            copy.wait()
+                        count = first_count
+
+                        def add(i, carry, buffer=buffer, kind=kind):
+                            mine = own[kind, lax.rem(chunk, 2), i].astype(F32)
+                            buffer[chunk, i] = (buffer[chunk, i].astype(F32) + mine).astype(BF)
+                            return carry
+                    else:
+                        count = plans[kind][stage - 1][2]
+                        kept = split(kind, stage - 1)[1]
+                        before = held[kind][stage - 1]
+
+                        def add(i, carry, buffer=buffer, before=before, kept=kept):
+                            shard, lines = kept(i)
+                            mine = before[chunk, shard, lines].astype(F32)
+                            buffer[chunk, i] = (buffer[chunk, i].astype(F32) + mine).astype(BF)
+                            return carry
+
+                    lax.fori_loop(0, count, add, 0)
+                    if stage < stages:
+                        start(stage_copies(kind, stage, chunk))
+                    else:
+                        start(spread_copies(kind, chunk))
+                        home_copy(kind, chunk).start()
+
+        return carry
+
+    lax.fori_loop(0, steps + stages, time_step, 0)
+
+    def drain(chunk, carry):
+        for kind in range(2):
+            for stage in range(stages + 1):
+                whole(kind, stage, chunk).wait_send()
+            for copy in spread_copies(kind, chunk):
+                copy.wait()
+            home_copy(kind, chunk).wait()
+        return carry
+
+    lax.fori_loop(0, steps, drain, 0)
+
+
+def sum_everywhere(grads, sizes):
+    groups, row_count, cols = sizes
+    count, rows, width = grads.shape
+    height = 16 * groups
+    steps = rows // (2 * height)
+    first_count = count // 2
+    buffers = []
+    for kind in range(2):
+        plan = sum_plan(sizes, bool(kind))
+        buffers.append(pltpu.VMEM((steps, first_count, height, width), BF))
+        buffers += [pltpu.VMEM((steps, c, h, width), BF) for _, _, c, h in plan]
+    stages = len(sum_plan(sizes, False))
+    return pl.pallas_call(
+        functools.partial(sum_kernel, sizes, steps),
+        out_shape=jax.ShapeDtypeStruct((rows, width), BF),
+        in_specs=[pl.BlockSpec(memory_space=pl.ANY)],
+        out_specs=pl.BlockSpec(memory_space=pl.ANY),
+        scratch_shapes=buffers
+        + [
+            pltpu.VMEM((2, 2, first_count, height, width), BF),
+            pltpu.SemaphoreType.DMA((2, stages + 1, steps)),
+            pltpu.SemaphoreType.DMA((2, stages + 1, steps)),
+            pltpu.SemaphoreType.DMA((2, groups, steps)),
+            pltpu.SemaphoreType.DMA((2, groups, steps)),
+            pltpu.SemaphoreType.DMA((2, 2)),
+            pltpu.SemaphoreType.DMA((2, steps)),
+        ],
+        compiler_params=pltpu.CompilerParams(
+            collective_id=1, has_side_effects=True, vmem_limit_bytes=56 * 2**20
+        ),
+        cost_estimate=pl.CostEstimate(flops=2**28, bytes_accessed=2**28, transcendentals=0),
+    )(grads)
+
+
 def all_to_all(values):
     return lax.all_to_all(values, GROUP, split_axis=0, concat_axis=0, tiled=True)
 
@@ -717,26 +918,30 @@
     small = jnp.pad(jnp.concatenate([small, shift_share]), (0, padded_len - small_len - shift_share.size))
     small_all = all_to_all(jnp.broadcast_to(small.reshape(1, -1, 128), (count, padded_len // 128, 128)))
     small_all = small_all.reshape(count, padded_len)
-    first_rows = jnp.concatenate(
-        [skip_weight] + [qkv_weight[:, i * D : (i + 1) * D] for i in range(3)]
-    )
-    first_all = lax.all_gather(first_rows, GROUP, axis=0, tiled=False)
-    skip_full = first_all[:, : 2 * shard].reshape(2 * D, D)
-    qkv_full = jnp.concatenate(
-        [first_all[:, (2 + i) * shard : (3 + i) * shard].reshape(D, D) for i in range(3)], axis=1
-    )
-    trio = lax.all_gather(
-        jnp.stack([out_weight, cross_query, cross_out]), GROUP, axis=0, tiled=False
-    )
-    out_full, cross_q_full, cross_o_full = [trio[:, i].reshape(D, D) for i in range(3)]
+    def beside(values, parts):
+        return jnp.concatenate(jnp.split(values, parts, axis=0), axis=1)
+
+    def below(values, parts):
+        width = values.shape[1] // parts
+        blocks = [values[:, i * width : (i + 1) * width] for i in range(parts)]
+        return jnp.stack([b.reshape(count, -1, width) for b in blocks], axis=1).reshape(-1, width)
+
+    first_all = lax.all_gather(
+        jnp.concatenate([beside(skip_weight, 2), qkv_weight], axis=1), GROUP, axis=0, tiled=True
+    )
+    skip_full = below(first_all[:, : 2 * D], 2)
+    qkv_full = first_all[:, 2 * D :]
+    folds = hid_part // shard
+    fold_rows = hid_part // folds
     up_part = lax.dynamic_index_in_dim(
         up_weight.reshape(shard, count, groups, hid_part), group_index, 2, keepdims=False
     ).reshape(shard, count * hid_part)
-    up_full = lax.all_gather(up_part, GROUP, axis=0, tiled=True)
     down_part = lax.dynamic_index_in_dim(
         down_weight.reshape(groups, hid_part, D), group_index, 0, keepdims=False
     )
-    down_full = lax.all_gather(down_part, GROUP, axis=0, tiled=True)
+    third = jnp.concatenate(
+        [jnp.pad(up_part, ((0, fold_rows - shard), (0, 0))), beside(down_part, folds)], axis=1
+    )
 
     wide = shard * near_vals
     embed_t = small_all[:, :wide].reshape(D, near_vals)
@@ -793,8 +998,21 @@
     text_part = dot(cross_keys, text_wide, (0,), (2,)).reshape(text_width, -1)
     text_part = text_part + cross_bias.astype(F32)[:, None]
     text_normed, text_pull = jax.vjp(text_norm, text_part, head_gains[3], head_offsets[3])
-    text_both = lax.all_gather(text_normed.astype(BF), GROUP, axis=0, tiled=True)
-    text_both = text_both.reshape(2, HEADS, HD, img_count * text_count)
+    moves = Moves()
+    second_all = lax.all_gather(
+        jnp.concatenate(
+            [out_weight, cross_query, cross_out, beside(text_normed.astype(BF), 2)], axis=1
+        ),
+        GROUP,
+        axis=0,
+        tiled=True,
+    )
+    out_full, cross_q_full, cross_o_full = [second_all[:, i * D : (i + 1) * D] for i in range(3)]
+    text_both = below(second_all[:, 3 * D :], 2).reshape(2, HEADS, HD, img_count * text_count)
+    third_all = lax.all_gather(third, GROUP, axis=0, tiled=True)
+    third_rows = third_all.reshape(count, fold_rows, -1)
+    up_full = third_rows[:, :shard, : count * hid_part].reshape(D, count * hid_part)
+    down_full = below(third_all[:, count * hid_part :], folds)
     shift_sums = small_all[:, small_len : small_len + img_count * D].astype(F32)
     shift_rows = jnp.sum(shift_sums, axis=0).reshape(img_count, D) + bias_shift
 
@@ -855,8 +1073,8 @@
     )
     out_latents = spread_near(emit_rim, tile_rows, tile_cols, patch_vals) * inside[..., None]
 
-    sums = Sums()
     lead = (0, 1)
+    by_row = row_first()
     grad_emitted = (cot_near * token_inside).astype(BF)
     grad_final = weight_grad(resid_low, grad_emitted)
     grad_resid_out = matmul_back(grad_emitted, final_full)
@@ -865,74 +1083,76 @@
     grad_down_rows = images_gather(grad_down_low)
     every_lead = (0, 1, 2)
     activated, out_latents = lax.optimization_barrier((activated, out_latents))
-    sums.begin(
-        "down", activated, grad_down_rows, every_lead, every_lead, 3, after=all_images
+    grad_down_rows = moves.begin(
+        grad_down_rows,
+        down=shard_sum(by_row, all_images, activated, grad_down_rows, every_lead, every_lead, 3),
     )
     grad_hidden = gelu_pull(matmul_back(grad_down_rows, down_full))[0].astype(BF)
-    sums.begin("up", mlp_in, grad_hidden, every_lead, every_lead, 3, after=all_images)
+    grad_hidden = moves.begin(
+        grad_hidden,
+        up=shard_sum(by_row, all_images, mlp_in, grad_hidden, every_lead, every_lead, 3),
+    )
     bias_up_grad = column_sum(grad_hidden)
-    grad_mlp_in = sums.step(matmul_back(grad_hidden, up_full), "down")
-    grad_mlp_in = sums.step(images_scatter(grad_mlp_in), "up")
+    grad_mlp_in = images_scatter(matmul_back(grad_hidden, up_full))
     grad_from_mlp, gain_mlp_grad, shift_mlp_grad = mlp_norm_pull(grad_mlp_in)
     grad_resid_cross = grad_resid_out + grad_from_mlp
 
     grad_cross_low = grad_resid_cross.astype(BF)
     grad_cross_flat = grad_cross_low.reshape(all_tokens, D)
-    sums.begin("cross_o", cross_low, grad_cross_flat, (1,), (0,), 0)
+    whole_grads = {"cross_o": dot(cross_low, grad_cross_flat, (1,), (0,))}
     bias_cross_o_grad = column_sum(grad_cross_low)
     grad_cross_mixed = dot(cross_o_full, grad_cross_flat, (1,), (1,)).astype(BF)
-    grad_cross_mixed = sums.step(grad_cross_mixed, "cross_o")
     grad_cross_rows, grad_text, cross_head_grads = cross_attend_back(
         text_len, cross_rows, text_both, grad_cross_mixed.reshape(HEADS, HD, all_tokens),
         cross_total, own_cos, own_sin, cross_cols,
     )
     cross_head_grads = jnp.sum(cross_head_grads, axis=0)
     grad_cross_rows = grad_cross_rows.reshape(D, all_tokens)
-    sums.begin("text", grad_text.reshape(2 * D, img_count * text_count), after=alone)
-    sums.begin("cross_q", cross_in.reshape(all_tokens, D), grad_cross_rows, (0,), (1,), 1)
+    whole_grads["cross_q"] = dot(cross_in.reshape(all_tokens, D), grad_cross_rows, (0,), (1,))
     bias_cross_q_grad = jnp.sum(grad_cross_rows.astype(F32), axis=1)
     grad_cross_in = dot(grad_cross_rows, cross_q_full, (0,), (1,))
-    grad_cross_in = sums.step(grad_cross_in, "text", "cross_q", "down")
     grad_from_cross, gain_cross_grad, shift_cross_grad = cross_norm_pull(
         grad_cross_in.reshape(img_count, tokens, D)
     )
     grad_resid_self = grad_resid_cross + grad_from_cross
 
     grad_out_rows = grad_resid_self.astype(BF)
-    sums.begin("out", attended_t, grad_out_rows, (0, 2), lead, 1)
+    whole_grads["out"] = dot(attended_t, grad_out_rows, (0, 2), lead)
     bias_out_grad = column_sum(grad_out_rows)
     grad_attended = dot(out_full, grad_out_rows, (1,), (2,)).astype(BF)
     grad_attended = jnp.transpose(
         grad_attended.reshape(HEADS, HD, img_count, tokens), (0, 2, 1, 3)
     )
     grad_mixed_jobs = all_to_all(grad_attended.reshape(count, jobs, HD, tokens))
-    grad_mixed_jobs = sums.step(grad_mixed_jobs, "out", "up", "cross_o", "down")
+    grad_mixed_jobs = moves.step(grad_mixed_jobs, "down", "up")
     grad_jobs, head_grads = attend_back(
         ext_jobs, qkv_jobs, grad_mixed_jobs, keep, total, every_cos, every_sin, head_cols, geo
     )
-    grad_jobs = sums.step(grad_jobs, "text", "cross_q", "up", "cross_o")
-    grad_qkv_t = sums.step(all_to_all(grad_jobs), "out", "down").reshape(HEADS, img_count, 3, HD, tokens)
+    grad_qkv_t = moves.step(all_to_all(grad_jobs), "down", "up").reshape(
+        HEADS, img_count, 3, HD, tokens
+    )
+    grad_qkv_t = moves.begin(
+        grad_qkv_t, text=offload_sum(alone, grad_text.reshape(2 * D, img_count * text_count))
+    )
     grad_qkv_t = jnp.transpose(grad_qkv_t, (2, 0, 3, 1, 4)).reshape(3 * D, img_count, tokens)
     head_grads = jnp.sum(head_grads, axis=0)
 
-    sums.begin("qkv", normed, grad_qkv_t, (0, 1), (1, 2), 2, 0, after=all_images)
+    for i, name in enumerate(("query", "key", "value")):
+        whole_grads[name] = dot(normed, grad_qkv_t[i * D : (i + 1) * D], (0, 1), (1, 2))
     bias_qkv_grad = jnp.sum(grad_qkv_t.astype(F32), axis=(1, 2))
-    grad_normed = sums.step(
-        dot(grad_qkv_t, qkv_full, (0,), (1,)), "up", "cross_o", "text", "cross_q"
-    )
+    grad_normed = dot(grad_qkv_t, qkv_full, (0,), (1,))
+    grad_normed = moves.step(grad_normed, "down", "up")
     grad_shift_rows = jnp.sum(grad_normed, axis=1)
     bias_shift_grad = jnp.sum(grad_shift_rows, axis=0)
     grad_from_self, gain_self_grad, shift_self_grad = self_norm_pull(grad_normed)
     grad_resid_in = grad_resid_self + grad_from_self
-    grad_merged = sums.step(grad_resid_in.astype(BF), "qkv", "out", "text")
-    skip_cut = D // 256 * 128
-    sums.begin("skip_a", skip_in, grad_merged[..., :-skip_cut], lead, lead, 2)
-    sums.begin("skip_b", skip_in, grad_merged[..., -skip_cut:], lead, lead, 2, order=col_first())
+    grad_merged = moves.step(grad_resid_in.astype(BF), "down", "up")
+    whole_grads["skip"] = weight_grad(skip_in, grad_merged)
     bias_skip_grad = column_sum(grad_merged)
-    grad_skip_normed = sums.step(matmul_back(grad_merged, skip_full), "skip_a", "skip_b", "cross_q", "cross_o")
+    grad_skip_normed = matmul_back(grad_merged, skip_full)
     grad_joined, skip_gain_grad, skip_shift_grad = skip_norm_pull(grad_skip_normed)
     grad_skip = grad_joined[..., D:].reshape(img_count, tile_rows, tile_cols, D)
-    grad_embedded = sums.step(grad_joined[..., :D].astype(BF), "up", "out", "cross_q", "qkv")
+    grad_embedded = grad_joined[..., :D].astype(BF)
     grad_embed_t = weight_grad(grad_embedded, near)
     bias_embed_grad = column_sum(grad_embedded)
     grad_near = matmul(grad_embedded, embed_t).reshape(
@@ -941,7 +1161,19 @@
     near_rim = with_halo(grad_near, (("row", 1), ("col", 2)), 1)
     grad_latents = spread_near(near_rim, tile_rows, tile_cols, patch_vals) * inside[..., None]
 
-    shards = sums.finish()
+    moves.finish(*list(moves.running))
+    shards = moves.done
+    names = ("query", "key", "value", "skip", "out", "cross_q", "cross_o")
+    packed = [whole_grads[name].astype(BF).reshape(count, -1, D) for name in names]
+    packed_rows = sum(part.shape[1] for part in packed)
+    fill = -packed_rows % (32 * groups)
+    packed = jnp.pad(jnp.concatenate(packed, axis=1), ((0, 0), (0, fill), (0, 0)))
+    summed = sum_everywhere(packed, (groups, row_count, col_count)).astype(F32)
+    total_of, at = {}, 0
+    for name in names:
+        rows = whole_grads[name].shape[0] // count
+        total_of[name] = summed[at : at + rows]
+        at += rows
     grad_text_lin, head_gain_ck_grad, head_shift_ck_grad = text_pull(shards["text"])
     grad_text_low = grad_text_lin.astype(BF)
     grad_cross_keys = images_sum(
@@ -1018,13 +1250,13 @@
         grad_latents,
         grad_skip,
         total_parts[0].reshape(shard, near_vals).T,
-        jnp.concatenate([shards["skip_a"], shards["skip_b"]], axis=1),
+        total_of["skip"],
         images_sum(grad_shift, F32),
-        jnp.concatenate([shards["qkv"][i] for i in range(groups)], axis=1).astype(F32),
-        shards["out"],
-        shards["cross_q"],
+        jnp.concatenate([total_of[name] for name in ("query", "key", "value")], axis=1),
+        total_of["out"],
+        total_of["cross_q"],
         grad_cross_keys,
-        shards["cross_o"],
+        total_of["cross_o"],
         total_up.astype(F32),
         total_down.astype(F32),
         total_parts[1].reshape(shard, near_vals),

time: 1260 us -> 1230 us (0.976)
  Pallas kernels: 70.3 us -> 240 us
  other arithmetic: 145 us -> 83.1 us
  waiting for transfers between devices: 522 us -> 470 us
  local copies, waits for them, and re-layouts: 221 us -> 179 us
  starting transfers between devices: 117 us -> 81.7 us
    pallas_call x0 -> x1, Pallas kernels: none -> 170 us  [sum_everywhere(): pl.pallas_call(functools.partial(sum_kernel, sizes, steps), out_shape=jax...]
    ppermute x37 -> x10, waiting for transfers between devices: 110 us -> 183 us  [exchange(): return lax.ppermute(values, axis, [(i, i ^ bit) for i in range(size)])]
    ppermute x17 -> x8, waiting for transfers between devices: 103 us -> 43.8 us  [swap_images(): return lax.ppermute(values, 'img', [(i, i ^ bit) for i in range(count)])]
    all_gather x5 -> x3, waiting for transfers between devices: 137 us -> 95.4 us  [the longest x1 56.5 us: body(): third_all = lax.all_gather(third, GROUP, axis=0, tiled=True)]
    ppermute x37 -> x10, starting transfers between devices: 37.7 us -> 9.64 us  [exchange(): return lax.ppermute(values, axis, [(i, i ^ bit) for i in range(size)])]
    add x18 -> x4, other arithmetic: 35.6 us -> 12 us  [scatter_sum(): part = keep + got.astype(F32)]
    all_to_all x6, waiting for transfers between devices: 163 us -> 141 us  [all_to_all(): lax.all_to_all(values, GROUP, split_axis=0, concat_axis=0, tiled=True)]
    add x10 -> x0, other arithmetic: 20.7 us -> none  [the longest x3 8.38 us: shard_sum(): part = (yield from scatter_sum(order, keep + got.astype(F32)))]
  transfers between devices with their start and end apart: 77 -> 40, of which waited for: 31 -> 22; matrix products, arithmetic and copies ran while one was open for 37% -> 24% of each run, Pallas kernels for 6% -> 18%
where the time goes in v2:
time: 1230 us; the launch traced here: 1210 us
  waiting for transfers between devices  470 us (38%)
  Pallas kernels  240 us (20%)
  local copies, waits for them, and re-layouts  179 us (15%)
  matrix products  142 us (12%)
  other arithmetic  83.1 us (7%)
  starting transfers between devices  81.7 us (7%)
  between operations  17.9 us (1%)
    ppermute x10, waiting for transfers between devices, exchange(): return lax.ppermute(values, axis, [(i, i ^ bit) for i in range(size)])  183 us
    pallas_call x1, Pallas kernels, sum_everywhere(): pl.pallas_call(functools.partial(sum_kernel, sizes, steps), out_shape=jax...  170 us
    all_to_all x6, waiting for transfers between devices, all_to_all(): lax.all_to_all(values, GROUP, split_axis=0, concat_axis=0, tiled=True)  141 us
    dot_general x34, matrix products, dot(): lax.dot_general(former, latter, ((former_dims, latter_dims), ((), ())), p...  141 us
    all_gather x1, waiting for transfers between devices, body(): third_all = lax.all_gather(third, GROUP, axis=0, tiled=True)  56.5 us
    unnamed x439, local copies, waits for them, and re-layouts  54.6 us
    ppermute x8, waiting for transfers between devices, swap_images(): return lax.ppermute(values, 'img', [(i, i ^ bit) for i in range(count)])  43.8 us
    all_gather x1, waiting for transfers between devices, body(): lax.all_gather(jnp.concatenate([beside(skip_weight, 2), qkv_weight], axis...  38.8 us
  transfers between devices with their start and end apart: 40, of which 22 were waited for; matrix products, arithmetic and copies ran while one was open for 24% of the time, Pallas kernels for 18%

profile of v2, /device:TPU:0, one launch (start us, length us, event | category | flops | bytes accessed | tf_op | source)
XLA Modules:
  0.0 1213.2 jit_solution(8576616605767192225)
XLA Ops:
  27.4 24.0 %all-to-all-done = bf16[16,240,128]{2,1,0:T(8,128)(2,1)S(1)} async-done(((bf16[16,240,128]{2,1,0:T(8,128)(2,1)}), bf16[16,240,128]{2,1,0:T(8,128)(2,1)S(1)}, u32[]{:S(2)}, u32[]{:S(2)}) %all-to-all-start) | async-done | bytes 983072 | tf_op jit(solution)/shard_map/all_to_all | solution.py:877
  100.2 38.8 %all-gather.4.cloned.1.call-done = bf16[1408,7040]{1,0:T(8,128)(2,1)} async-done(((bf16[88,7040]{1,0:T(8,128)(2,1)}), bf16[1408,7040]{1,0:T(8,128)(2,1)}) %all-gather.4.cloned.1.call-update) | async-done | bytes 19824656 | tf_op jit(solution)/shard_map/all_gather | solution.py:929
  161.3 8.1 fusion.7
  171.0 8.8 all-to-all-start.1
  196.5 81.9 %all-to-all-done.1.qkv_ref = bf16[16,2,3,88,128]{4,3,2,1,0:T(8,128)(2,1)S(1)} async-done(((bf16[16,2,3,88,128]{4,3,2,1,0:T(8,128)(2,1)}), bf16[16,2,3,88,128]{4,3,2,1,0:T(8,128)(2,1)S(1)}, u32[]{:S(2)}, u32[]{:S(2)}) %all-to-all-start.1) | async-done | bytes 2162720 | tf_op jit(solution)/shard_map/all_to_all | solution.py:877
  280.1 15.6 %shard_map.488 = (bf16[16,2,88,128]{3,2,1,0:T(8,128)(2,1)S(1)}, f32[2,88,2048]{2,1,0:T(8,128)S(1)}, f32[2,1,2048]{2,1,0:T(1,128)S(1)}) custom-call(s32[2,2]{1,0:T(2,128)S(1)} %broadcast_select_fusion.2.ext_ref, bf16[16,2,3,88,128]{4,3,2,1,0:T(8,128)(2,1)S(1)} %all-to-all-done.1.qkv_ref, f32[88,2048]{1,0:T(8,128)S(1)} %copy-done.5, ...), custom_call_target="tpu_custom_call" | custom-call | flops 8858370048 | bytes 6291456 | tf_op jit(solution)/shard_map/pallas_call | solution.py:352
  310.5 12.7 %all-to-all-done.2 = bf16[16,2,88,128]{3,2,1,0:T(8,128)(2,1)S(1)} async-done(((bf16[16,2,88,128]{3,2,1,0:T(8,128)(2,1)}), bf16[16,2,88,128]{3,2,1,0:T(8,128)(2,1)S(1)}, u32[]{:S(2)}, u32[]{:S(2)}) %all-to-all-start.2) | async-done | bytes 720928 | tf_op jit(solution)/shard_map/all_to_all | solution.py:877
  332.2 12.6 %shard_map.489 = (bf16[16,88,256]{2,1,0:T(8,128)(2,1)S(1)}, f32[16,1,256]{2,1,0:T(1,128)S(1)}) custom-call(s32[2,2]{1,0:T(2,128)S(1)} %copy-done.9, f32[16,88,256]{2,1,0:T(8,128)S(1)} %bitcast.378, bf16[2,16,88,768]{3,2,1,0:T(8,128)(2,1)S(1)} %bitcast.374, f32[88,256]{1,0:T(8,128)S(1)} %get-tuple-element.343.cos_ref, ...), custom_call_target="tpu_custom_call" | custom-call | flops 4294967296 | bytes 10485760 | tf_op jit(solution)/shard_map/pallas_call | solution.py:585
  351.9 56.5 %all-gather.8.cloned.1.call-done = bf16[1536,5888]{1,0:T(8,128)(2,1)} async-done(((bf16[96,5888]{1,0:T(8,128)(2,1)}), bf16[1536,5888]{1,0:T(8,128)(2,1)}) %all-gather.8.cloned.1.call-update) | async-done | bytes 18087952 | tf_op jit(solution)/shard_map/all_gather | solution.py:1012
  429.9 12.4 %multiply_convert_fusion = (bf16[2,2,128,3072]{3,2,1,0:T(8,128)(2,1)S(1)}, f32[2,2,128,3072]{3,2,1,0:T(8,128)}) fusion(f32[3072]{0:T(1024)S(1)} %add.598, bf16[1408,3072,1,1]{1,0,3,2:T(8,128)(2,1)} %bitcast.398, bf16[1,2,128,1408]{3,2,1,0:T(8,128)(2,1)S(1)} %collective-permute-done.4, bf16[1,2,128,1408]{3,2,1,0:T(8,128)(2,1)S(1)} %fusion.84), kind=kOutput, calls=%fused_computation.33 | convolution fusion | flops 4445634560 | bytes 19542016 | tf_op jit(solution)/shard_map/dot_general | solution.py:44
  452.2 14.5 %collective-permute-done.5 = bf16[1,2,128,1408]{3,2,1,0:T(8,128)(2,1)S(1)} collective-permute-done((bf16[1,2,128,1408]{3,2,1,0:T(8,128)(2,1)S(1)}, bf16[1,2,128,1408]{3,2,1,0:T(8,128)(2,1)S(1)}, u32[]{:S(2)}, u32[]{:S(2)}) %collective-permute-start.5) | collective-permute-done | bytes 720928 | tf_op jit(solution)/shard_map/ppermute | solution.py:112
  500.1 13.1 %fusion.14 = bf16[2,2,128,3072]{3,2,1,0:T(8,128)(2,1)S(1)} fusion(f32[2,2,128,3072]{3,2,1,0:T(8,128)} %get-tuple-element.353, bf16[2,2,128,1408]{3,2,1,0:T(8,128)(2,1)S(1)} %pad_maximum_fusion.6, bf16[3072,1408,1,1]{1,0,3,2:T(8,128)(2,1)} %bitcast.402, f32[3072]{0:T(1024)S(1)} %copy-done.150), kind=kOutput, calls=%fused_computation.31 | convolution fusion | flops 4462215168 | bytes 19542016 | tf_op jit(solution)/shard_map/dot_general | solution.py:44
  525.1 16.0 %collective-permute-done.11 = bf16[1,2,128,1408]{3,2,1,0:T(8,128)(2,1)S(1)} collective-permute-done((bf16[1,2,128,1408]{3,2,1,0:T(8,128)(2,1)S(1)}, bf16[1,2,128,1408]{3,2,1,0:T(8,128)(2,1)S(1)}, u32[]{:S(2)}, u32[]{:S(2)}) %collective-permute-start.11) | collective-permute-done | bytes 720928 | tf_op jit(solution)/shard_map/ppermute | solution.py:112
  547.3 15.5 %shard_map.490 = (bf16[16,88,256]{2,1,0:T(8,128)(2,1)S(1)}, bf16[2,16,88,768]{3,2,1,0:T(8,128)(2,1)S(1)}, f32[8,88,2]{2,1,0:T(8,128)S(1)}) custom-call(s32[2,2]{1,0:T(2,128)S(1)} %copy-done.9, f32[16,88,256]{2,1,0:T(8,128)S(1)} %bitcast.379, bf16[2,16,88,768]{3,2,1,0:T(8,128)(2,1)S(1)} %bitcast.377, bf16[16,88,256]{2,1,0:T(8,128)(2,1)S(1)} %bitcast.380, ...), custom_call_target="tpu_custom_call" | custom-call | flops 8589934592 | bytes 16777216 | tf_op jit(solution)/shard_map/pallas_call | solution.py:605
  582.5 19.9 %all-to-all-done.3.dout_ref = bf16[16,2,88,128]{3,2,1,0:T(8,128)(2,1)} async-done(((bf16[16,2,88,128]{3,2,1,0:T(8,128)(2,1)}), bf16[16,2,88,128]{3,2,1,0:T(8,128)(2,1)}, u32[]{:S(2)}, u32[]{:S(2)}) %all-to-all-start.3) | async-done | bytes 720928 | tf_op jit(solution)/shard_map/all_to_all | solution.py:877
  613.1 8.2 bitcast_add_fusion
  625.3 26.3 %shard_map.491 = (bf16[16,2,3,88,128]{4,3,2,1,0:T(8,128)(2,1)}, f32[2,88,4]{2,1,0:T(8,128)}) custom-call(s32[2,2]{1,0:T(2,128)} %copy-done.8, bf16[16,2,3,88,128]{4,3,2,1,0:T(8,128)(2,1)} %copy-done.3, bf16[16,2,88,128]{3,2,1,0:T(8,128)(2,1)} %all-to-all-done.3.dout_ref, f32[2,88,2048]{2,1,0:T(8,128)} %copy-done.12, f32[2,1,2048]{2,1,0:T(1,128)} %copy-done.13, ...), custom_call_target="tpu_custom_call" | custom-call | flops 22145925120 | bytes 8388608 | tf_op jit(solution)/shard_map/pallas_call | solution.py:456
  686.1 43.3 %collective-permute-done.14 = bf16[2,2,192,1408]{3,2,1,0:T(8,128)(2,1)} collective-permute-done((bf16[2,2,192,1408]{3,2,1,0:T(8,128)(2,1)}, bf16[2,2,192,1408]{3,2,1,0:T(8,128)(2,1)}, u32[]{:S(2)}, u32[]{:S(2)}) %collective-permute-start.14) | collective-permute-done | bytes 2162720 | tf_op jit(solution)/shard_map/ppermute | solution.py:142
  729.4 45.9 %collective-permute-done.15 = bf16[2,2,88,3072]{3,2,1,0:T(8,128)(2,1)} collective-permute-done((bf16[2,2,88,3072]{3,2,1,0:T(8,128)(2,1)}, bf16[2,2,88,3072]{3,2,1,0:T(8,128)(2,1)}, u32[]{:S(2)}, u32[]{:S(2)}) %collective-permute-start.15) | collective-permute-done | bytes 2162720 | tf_op jit(solution)/shard_map/ppermute | solution.py:142
  809.4 8.5 fusion
  821.8 39.2 %collective-permute-done.17 = bf16[2,88,3072]{2,1,0:T(8,128)(2,1)} collective-permute-done((bf16[2,88,3072]{2,1,0:T(8,128)(2,1)}, bf16[2,88,3072]{2,1,0:T(8,128)(2,1)}, u32[]{:S(2)}, u32[]{:S(2)}) %collective-permute-start.17) | collective-permute-done | bytes 1081376 | tf_op jit(solution)/shard_map/ppermute | solution.py:142
  874.0 39.9 %collective-permute-done.18 = bf16[192,1408]{1,0:T(8,128)(2,1)} collective-permute-done((bf16[192,1408]{1,0:T(8,128)(2,1)}, bf16[192,1408]{1,0:T(8,128)(2,1)}, u32[]{:S(2)}, u32[]{:S(2)}) %collective-permute-start.18) | collective-permute-done | bytes 540704 | tf_op jit(solution)/shard_map/ppermute | solution.py:142
  913.8 11.2 collective-permute-done.19
  963.0 170.0 %shard_map.492 = bf16[704,1408]{1,0:T(8,128)(2,1)} custom-call(bf16[16,704,1408]{2,1,0:T(8,128)(2,1)} %constant_dynamic-update-slice_fusion.21.grads_ref), custom_call_target="tpu_custom_call" | custom-call | flops 268435456 | bytes 268435456 | tf_op jit(solution)/shard_map/pallas_call | solution.py:854
  (846 shorter events, 452.3 us)
Async XLA Ops:
  7.2 131.8 %all-gather.4.cloned.1.call-start = ((), (), s32[]{:S(2)}) async-start(), calls=%async_computation.7 | async-start | bytes 21063680 | tf_op jit(solution)/shard_map/all_gather | solution.py:929
  13.2 38.2 %all-to-all-start = ((bf16[16,240,128]{2,1,0:T(8,128)(2,1)}), bf16[16,240,128]{2,1,0:T(8,128)(2,1)S(1)}, u32[]{:S(2)}, u32[]{:S(2)}) async-start(bf16[16,240,128]{2,1,0:T(8,128)(2,1)} %broadcast_in_dim.200), calls=%async_computation | async-start | bytes 1966080 | tf_op jit(solution)/shard_map/all_to_all | solution.py:877
  20.6 285.0 %all-gather.6.cloned.1.call-start = ((), (), s32[]{:S(2)}) async-start(), calls=%async_computation.8 | async-start | bytes 17233920 | tf_op jit(solution)/shard_map/all_gather | solution.py:1002
  55.5 352.8 %all-gather.8.cloned.1.call-start = ((), (), s32[]{:S(2)}) async-start(), calls=%async_computation.9 | async-start | bytes 19218432 | tf_op jit(solution)/shard_map/all_gather | solution.py:1012
  171.0 107.4 %all-to-all-start.1 = ((bf16[16,2,3,88,128]{4,3,2,1,0:T(8,128)(2,1)}), bf16[16,2,3,88,128]{4,3,2,1,0:T(8,128)(2,1)S(1)}, u32[]{:S(2)}, u32[]{:S(2)}) async-start(bf16[16,2,3,88,128]{4,3,2,1,0:T(8,128)(2,1)} %bitcast.404), calls=%async_computation.1 | async-start | bytes 4325376 | tf_op jit(solution)/shard_map/all_to_all | solution.py:877
  297.7 25.5 %all-to-all-start.2 = ((bf16[16,2,88,128]{3,2,1,0:T(8,128)(2,1)}), bf16[16,2,88,128]{3,2,1,0:T(8,128)(2,1)S(1)}, u32[]{:S(2)}, u32[]{:S(2)}) async-start(bf16[16,2,88,128]{3,2,1,0:T(8,128)(2,1)} %copy-done.6), calls=%async_computation.2 | async-start | bytes 1441792 | tf_op jit(solution)/shard_map/all_to_all | solution.py:877
  350.3 79.6 %collective-permute-start.4 = (bf16[1,2,128,1408]{3,2,1,0:T(8,128)(2,1)S(1)}, bf16[1,2,128,1408]{3,2,1,0:T(8,128)(2,1)S(1)}, u32[]{:S(2)}, u32[]{:S(2)}) collective-permute-start(bf16[1,2,128,1408]{3,2,1,0:T(8,128)(2,1)S(1)} %fusion.84), channel_id=1, source_target_pairs={{0,16},{16,0},{1,17},{17,1},{2,18},{18,2},{3,19},{19,3},{4,20},{20... | collective-permute-start | bytes 2162696 | tf_op jit(solution)/shard_map/ppermute | solution.py:112
  447.6 19.1 %collective-permute-start.5 = (bf16[1,2,128,1408]{3,2,1,0:T(8,128)(2,1)S(1)}, bf16[1,2,128,1408]{3,2,1,0:T(8,128)(2,1)S(1)}, u32[]{:S(2)}, u32[]{:S(2)}) collective-permute-start(bf16[1,2,128,1408]{3,2,1,0:T(8,128)(2,1)S(1)} %slice.819), channel_id=1, source_target_pairs={{0,16},{16,0},{1,17},{17,1},{2,18},{18,2},{3,19},{19,3},{4,20},{20... | collective-permute-start | bytes 2162696 | tf_op jit(solution)/shard_map/ppermute | solution.py:112
  451.6 28.9 %collective-permute-start.10 = (bf16[1,2,128,1408]{3,2,1,0:T(8,128)(2,1)}, bf16[1,2,128,1408]{3,2,1,0:T(8,128)(2,1)}, u32[]{:S(2)}, u32[]{:S(2)}) collective-permute-start(bf16[1,2,128,1408]{3,2,1,0:T(8,128)(2,1)} %convert_bitcast_fusion.2), channel_id=1, source_target_pairs={{0,16},{16,0},{1,17},{17,1},{2,18},{18,2},{3,19},{19,3},{4,20},{20... | collective-permute-start | bytes 2162696 | tf_op jit(solution)/shard_map/ppermute | solution.py:112
  524.6 77.7 %collective-permute-start.12 = (bf16[1536,1408]{1,0:T(8,128)(2,1)}, bf16[1536,1408]{1,0:T(8,128)(2,1)}, u32[]{:S(2)}, u32[]{:S(2)}) collective-permute-start(bf16[1536,1408]{1,0:T(8,128)(2,1)} %bitcast_convert_fusion.2), channel_id=1, source_target_pairs={{0,4},{4,0},{8,12},{12,8},{1,5},{5,1},{9,13},{13,9},{2,6},{6,2},{1... | collective-permute-start | bytes 12976136 | tf_op jit(solution)/shard_map/ppermute | solution.py:142
  524.6 77.7 %collective-permute-start.13 = (bf16[704,3072]{1,0:T(8,128)(2,1)}, bf16[704,3072]{1,0:T(8,128)(2,1)}, u32[]{:S(2)}, u32[]{:S(2)}) collective-permute-start(bf16[704,3072]{1,0:T(8,128)(2,1)} %bitcast_convert_fusion.1), channel_id=1, source_target_pairs={{0,4},{4,0},{8,12},{12,8},{1,5},{5,1},{9,13},{13,9},{2,6},{6,2},{1... | collective-permute-start | bytes 12976136 | tf_op jit(solution)/shard_map/ppermute | solution.py:142
  578.2 24.2 %all-to-all-start.3 = ((bf16[16,2,88,128]{3,2,1,0:T(8,128)(2,1)}), bf16[16,2,88,128]{3,2,1,0:T(8,128)(2,1)}, u32[]{:S(2)}, u32[]{:S(2)}) async-start(bf16[16,2,88,128]{3,2,1,0:T(8,128)(2,1)} %bitcast.430), calls=%async_computation.3 | async-start | bytes 1441792 | tf_op jit(solution)/shard_map/all_to_all | solution.py:877
  651.7 123.6 %all-to-all-start.4 = ((bf16[16,2,3,88,128]{4,3,2,1,0:T(8,128)(2,1)}), bf16[16,2,3,88,128]{4,3,2,1,0:T(8,128)(2,1)}, u32[]{:S(2)}, u32[]{:S(2)}) async-start(bf16[16,2,3,88,128]{4,3,2,1,0:T(8,128)(2,1)} %get-tuple-element.81), calls=%async_computation.4 | async-start | bytes 4325376 | tf_op jit(solution)/shard_map/all_to_all | solution.py:877
  656.3 497.0 %reduce-scatter.2.cloned.1.call-start = ((), (), s32[]{:S(2)}) async-start(), calls=%async_computation.10 | async-start | bytes 4595712 | tf_op jit(solution)/shard_map/reduce_scatter | solution.py:140
  659.5 69.8 %collective-permute-start.14 = (bf16[2,2,192,1408]{3,2,1,0:T(8,128)(2,1)}, bf16[2,2,192,1408]{3,2,1,0:T(8,128)(2,1)}, u32[]{:S(2)}, u32[]{:S(2)}) collective-permute-start(bf16[2,2,192,1408]{3,2,1,0:T(8,128)(2,1)} %fusion.45), channel_id=1, source_target_pairs={{0,8},{4,12},{8,0},{12,4},{1,9},{5,13},{9,1},{13,5},{2,10},{6,14},... | collective-permute-start | bytes 6488072 | tf_op jit(solution)/shard_map/ppermute | solution.py:142
  661.4 113.9 %collective-permute-start.15 = (bf16[2,2,88,3072]{3,2,1,0:T(8,128)(2,1)}, bf16[2,2,88,3072]{3,2,1,0:T(8,128)(2,1)}, u32[]{:S(2)}, u32[]{:S(2)}) collective-permute-start(bf16[2,2,88,3072]{3,2,1,0:T(8,128)(2,1)} %fusion.46), channel_id=1, source_target_pairs={{0,8},{4,12},{8,0},{12,4},{1,9},{5,13},{9,1},{13,5},{2,10},{6,14},... | collective-permute-start | bytes 6488072 | tf_op jit(solution)/shard_map/ppermute | solution.py:142
  794.7 27.1 %collective-permute-start.16 = (bf16[2,192,1408]{2,1,0:T(8,128)(2,1)}, bf16[2,192,1408]{2,1,0:T(8,128)(2,1)}, u32[]{:S(2)}, u32[]{:S(2)}) collective-permute-start(bf16[2,192,1408]{2,1,0:T(8,128)(2,1)} %fusion.71), channel_id=1, source_target_pairs={{0,1},{1,0},{2,3},{3,2},{4,5},{5,4},{6,7},{7,6},{8,9},{9,8},{10,11... | collective-permute-start | bytes 3244040 | tf_op jit(solution)/shard_map/ppermute | solution.py:142
  796.2 64.8 %collective-permute-start.17 = (bf16[2,88,3072]{2,1,0:T(8,128)(2,1)}, bf16[2,88,3072]{2,1,0:T(8,128)(2,1)}, u32[]{:S(2)}, u32[]{:S(2)}) collective-permute-start(bf16[2,88,3072]{2,1,0:T(8,128)(2,1)} %fusion.72), channel_id=1, source_target_pairs={{0,1},{1,0},{2,3},{3,2},{4,5},{5,4},{6,7},{7,6},{8,9},{9,8},{10,11... | collective-permute-start | bytes 3244040 | tf_op jit(solution)/shard_map/ppermute | solution.py:142
  868.4 45.4 %collective-permute-start.18 = (bf16[192,1408]{1,0:T(8,128)(2,1)}, bf16[192,1408]{1,0:T(8,128)(2,1)}, u32[]{:S(2)}, u32[]{:S(2)}) collective-permute-start(bf16[192,1408]{1,0:T(8,128)(2,1)} %fusion.100), channel_id=1, source_target_pairs={{0,2},{1,3},{2,0},{3,1},{4,6},{5,7},{6,4},{7,5},{8,10},{9,11},{10,... | collective-permute-start | bytes 1622024 | tf_op jit(solution)/shard_map/ppermute | solution.py:142
  870.0 55.1 %collective-permute-start.19 = (bf16[88,3072]{1,0:T(8,128)(2,1)}, bf16[88,3072]{1,0:T(8,128)(2,1)}, u32[]{:S(2)}, u32[]{:S(2)}) collective-permute-start(bf16[88,3072]{1,0:T(8,128)(2,1)} %fusion.101), channel_id=1, source_target_pairs={{0,2},{1,3},{2,0},{3,1},{4,6},{5,7},{6,4},{7,5},{8,10},{9,11},{10,... | collective-permute-start | bytes 1622024 | tf_op jit(solution)/shard_map/ppermute | solution.py:142
  936.2 205.1 %collective-permute-start.21 = (f32[2,1,8,144]{3,2,1,0:T(8,128)S(1)}, f32[2,1,8,144]{3,2,1,0:T(8,128)S(1)}, u32[]{:S(2)}, u32[]{:S(2)}) collective-permute-start(f32[2,1,8,144]{3,2,1,0:T(8,128)S(1)} %get-tuple-element.304), channel_id=1, source_target_pairs={{4,0},{8,4},{12,8},{5,1},{9,5},{13,9},{6,2},{10,6},{14,10},{7,3},{... | collective-permute-start | bytes 27656 | tf_op jit(solution)/shard_map/ppermute | solution.py:38
  937.5 203.8 %collective-permute-start.20 = (f32[2,1,8,144]{3,2,1,0:T(8,128)S(1)}, f32[2,1,8,144]{3,2,1,0:T(8,128)S(1)}, u32[]{:S(2)}, u32[]{:S(2)}) collective-permute-start(f32[2,1,8,144]{3,2,1,0:T(8,128)S(1)} %get-tuple-element.303), channel_id=1, source_target_pairs={{0,4},{4,8},{8,12},{1,5},{5,9},{9,13},{2,6},{6,10},{10,14},{3,7},{... | collective-permute-start | bytes 27656 | tf_op jit(solution)/shard_map/ppermute | solution.py:35
  1135.9 27.2 %collective-permute-start.28 = (bf16[1,192,1408]{2,1,0:T(8,128)(2,1)S(1)}, bf16[1,192,1408]{2,1,0:T(8,128)(2,1)}, u32[]{:S(2)}, u32[]{:S(2)}) collective-permute-start(bf16[1,192,1408]{2,1,0:T(8,128)(2,1)S(1)} %fusion.102), channel_id=1, source_target_pairs={{0,16},{16,0},{1,17},{17,1},{2,18},{18,2},{3,19},{19,3},{4,20},{20... | collective-permute-start | bytes 1622024 | tf_op jit(solution)/shard_map/ppermute | solution.py:142
  1158.4 30.1 %all-to-all-start.5 = ((bf16[16,240,128]{2,1,0:T(8,128)(2,1)}), bf16[16,240,128]{2,1,0:T(8,128)(2,1)}, u32[]{:S(2)}, u32[]{:S(2)}) async-start(bf16[16,240,128]{2,1,0:T(8,128)(2,1)} %bitcast.168), calls=%async_computation.6 | async-start | bytes 1966080 | tf_op jit(solution)/shard_map/all_to_all | solution.py:877
  (217 other events, 3692.5 us)
Sparse Core Ops, SparseCore 0:
  11.1 127.8 all-gather.3
  141.8 163.7 all-gather.5
  307.2 101.1 all-gather.7
  796.9 109.4 reduce-scatter.1

commit v3 on v2

--- a/solution.py
+++ b/solution.py
@@ -1,5 +1,6 @@
 import functools
 import math
+from typing import NamedTuple
 
 import jax
 import jax.numpy as jnp
@@ -623,16 +624,25 @@
 
 
 MESH = pl.DeviceIdType.MESH
-
-
-def sum_plan(sizes, rows_first):
+LAG = 3
+
+
+class Kind(NamedTuple):
+    width: int
+    height: int
+    chunks: int
+    first_step: int
+    over_images: bool
+
+
+def sum_plan(sizes, kind):
     groups, row_count, cols = sizes
-    count, height = row_count * cols // 2, 16 * groups
+    count, height = row_count * cols // 2, kind.height
     image_bits = [("img", 1 << i) for i in range(groups.bit_length() - 1)]
     row_bits = [("row", 1 << i) for i in range(1, row_count.bit_length() - 1)]
     col_bits = [("col", 1 << i) for i in range(cols.bit_length() - 1)]
     plan = []
-    for axis, bit in (row_bits + image_bits if rows_first else image_bits + row_bits) + col_bits:
+    for axis, bit in (image_bits if kind.over_images else []) + row_bits + col_bits:
         if axis == "img":
             height //= 2
         else:
@@ -641,236 +651,247 @@
     return plan
 
 
-def sum_kernel(sizes, steps, grads_ref, out_ref, *scratch):
+def sum_kernel(sizes, kinds, *refs):
     groups, row_count, cols = sizes
-    height = 16 * groups
+    number = len(kinds)
+    grads_refs, out_refs, scratch = refs[:number], refs[number : 2 * number], refs[2 * number :]
     first_count = row_count * cols // 2
     places = {axis: lax.axis_index(axis) for axis in ("img", "row", "col")}
-    plans = [sum_plan(sizes, False), sum_plan(sizes, True)]
-    stages = len(plans[0])
+    plans = [sum_plan(sizes, kind) for kind in kinds]
     image_stages = groups.bit_length() - 1
-    held = [scratch[: stages + 1], scratch[stages + 1 : 2 * stages + 2]]
-    own, send_sem, recv_sem, spread_sem, spread_recv, own_sem, out_sem = scratch[2 * stages + 2 :]
+    held, own, sems = [], [], []
+    at = 0
+    for plan in plans:
+        held.append(scratch[at : at + len(plan) + 1])
+        own.append(scratch[at + len(plan) + 1])
+        sems.append(scratch[at + len(plan) + 2 : at + len(plan) + 8])
+        at += len(plan) + 8
     core = places["row"] % 2
+
+    def device_of(place):
+        return tuple(place[name] for name in ("img", "row", "col"))
 
     def partner(axis, bit):
         place = dict(places)
         part = place[axis] // bit % 2
         place[axis] = place[axis] + bit - 2 * bit * part
-        return tuple(place[name] for name in ("img", "row", "col"))
+        return device_of(place)
+
+    def other_images():
+        for i in range(1, groups):
+            place = dict(places)
+            place["img"] = lax.rem(places["img"] + i, groups)
+            yield i, device_of(place)
 
     def bit_of(axis, bit):
         return places[axis] // bit % 2
 
-    def chunk_rows(kind, chunk):
-        return pl.multiple_of((2 * chunk + kind) * height, 16)
-
-    def first_copies(kind, chunk):
-        rows = pl.ds(chunk_rows(kind, chunk), height)
+    def chunk_rows(k, chunk):
+        return pl.multiple_of(chunk * kinds[k].height, 16)
+
+    def first_copies(k, chunk):
+        rows = pl.ds(chunk_rows(k, chunk), kinds[k].height)
         for i in range(row_count // 2):
             shards = pl.ds((2 * i + 1 - core) * cols, cols)
             yield pltpu.make_async_remote_copy(
-                src_ref=grads_ref.at[shards, rows],
-                dst_ref=held[kind][0].at[chunk, pl.ds(i * cols, cols)],
-                send_sem=send_sem.at[kind, 0, chunk],
-                recv_sem=recv_sem.at[kind, 0, chunk],
+                src_ref=grads_refs[k].at[shards, rows],
+                dst_ref=held[k][0].at[chunk, pl.ds(i * cols, cols)],
+                send_sem=sems[k][0].at[0, chunk],
+                recv_sem=sems[k][1].at[0, chunk],
                 device_id=partner("row", 1),
                 device_id_type=MESH,
             )
 
-    def own_copies(kind, chunk):
-        rows = pl.ds(chunk_rows(kind, chunk), height)
+    def own_copies(k, chunk):
+        rows = pl.ds(chunk_rows(k, chunk), kinds[k].height)
         for i in range(row_count // 2):
             shards = pl.ds((2 * i + core) * cols, cols)
             yield pltpu.make_async_copy(
-                grads_ref.at[shards, rows],
-                own.at[kind, lax.rem(chunk, 2), pl.ds(i * cols, cols)],
-                own_sem.at[kind, lax.rem(chunk, 2)],
+                grads_refs[k].at[shards, rows],
+                own[k].at[lax.rem(chunk, 2), pl.ds(i * cols, cols)],
+                sems[k][4].at[lax.rem(chunk, 2)],
             )
 
-    def split(kind, stage):
-        axis, bit, count, rows = plans[kind][stage]
+    def split(k, stage):
+        axis, bit, count, rows = plans[k][stage]
         part = bit_of(axis, bit)
         if axis == "img":
-            return (
-                [((pl.ds(0, count), pl.ds(pl.multiple_of((1 - part) * rows, 16), rows)), pl.ds(0, count))],
-                lambda i: (i, pl.ds(pl.multiple_of(part * rows, 16), rows)),
-            )
+            give = pl.ds(pl.multiple_of((1 - part) * rows, 16), rows)
+            keep = pl.ds(pl.multiple_of(part * rows, 16), rows)
+            return [((pl.ds(0, count), give), pl.ds(0, count))], lambda i: (i, keep)
+        every = pl.ds(0, rows)
         if axis == "row":
-            return (
-                [((pl.ds((1 - part) * count, count), pl.ds(0, rows)), pl.ds(0, count))],
-                lambda i: (part * count + i, pl.ds(0, rows)),
-            )
+            give = pl.ds((1 - part) * count, count)
+            return [((give, every), pl.ds(0, count))], lambda i: (part * count + i, every)
         return (
-            [((pl.ds(2 * i + 1 - part, 1), pl.ds(0, rows)), pl.ds(i, 1)) for i in range(count)],
-            lambda i: (2 * i + part, pl.ds(0, rows)),
+            [((pl.ds(2 * i + 1 - part, 1), every), pl.ds(i, 1)) for i in range(count)],
+            lambda i: (2 * i + part, every),
         )
 
-    def stage_copies(kind, stage, chunk):
-        axis, bit, count, rows = plans[kind][stage]
-        for (shards, lines), target in split(kind, stage)[0]:
+    def stage_copies(k, stage, chunk):
+        axis, bit, _, _ = plans[k][stage]
+        for (shards, lines), target in split(k, stage)[0]:
             yield pltpu.make_async_remote_copy(
-                src_ref=held[kind][stage].at[chunk, shards, lines],
-                dst_ref=held[kind][stage + 1].at[chunk, target],
-                send_sem=send_sem.at[kind, stage + 1, chunk],
-                recv_sem=recv_sem.at[kind, stage + 1, chunk],
+                src_ref=held[k][stage].at[chunk, shards, lines],
+                dst_ref=held[k][stage + 1].at[chunk, target],
+                send_sem=sems[k][0].at[stage + 1, chunk],
+                recv_sem=sems[k][1].at[stage + 1, chunk],
                 device_id=partner(axis, bit),
                 device_id_type=MESH,
             )
 
-    def whole(kind, stage, chunk):
-        buffer = held[kind][stage].at[chunk]
+    def whole(k, stage, chunk):
+        buffer = held[k][stage].at[chunk]
         return pltpu.make_async_remote_copy(
             src_ref=buffer,
             dst_ref=buffer,
-            send_sem=send_sem.at[kind, stage, chunk],
-            recv_sem=recv_sem.at[kind, stage, chunk],
+            send_sem=sems[k][0].at[stage, chunk],
+            recv_sem=sems[k][1].at[stage, chunk],
             device_id=partner("row", 1),
             device_id_type=MESH,
         )
 
-    last_rows = plans[0][-1][3]
-
-    def out_rows(kind, chunk):
-        return pl.ds(pl.multiple_of(chunk_rows(kind, chunk) + image_place() * last_rows, 16), last_rows)
-
-    def image_place():
+    def home(k, chunk):
+        rows = plans[k][-1][3]
+        if not kinds[k].over_images:
+            return out_refs[k].at[places["img"], pl.ds(chunk_rows(k, chunk), rows)]
         place = 0
         for i in range(image_stages):
             place = place + bit_of("img", 1 << i) * (1 << (image_stages - 1 - i))
-        return place
-
-    def spread_copies(kind, chunk):
-        for i in range(1, groups):
-            place = dict(places)
-            place["img"] = lax.rem(places["img"] + i, groups)
+        return out_refs[k].at[pl.ds(pl.multiple_of(chunk_rows(k, chunk) + place * rows, 16), rows)]
+
+    def spread_copies(k, chunk):
+        for i, other in other_images():
             yield pltpu.make_async_remote_copy(
-                src_ref=held[kind][stages].at[chunk, 0],
-                dst_ref=out_ref.at[out_rows(kind, chunk)],
-                send_sem=spread_sem.at[kind, i, chunk],
-                recv_sem=spread_recv.at[kind, i, chunk],
-                device_id=tuple(place[name] for name in ("img", "row", "col")),
+                src_ref=held[k][-1].at[chunk, 0],
+                dst_ref=home(k, chunk),
+                send_sem=sems[k][2].at[i, chunk],
+                recv_sem=sems[k][3].at[i, chunk],
+                device_id=other,
                 device_id_type=MESH,
             )
 
-    def home_copy(kind, chunk):
+    def home_copy(k, chunk):
         return pltpu.make_async_copy(
-            held[kind][stages].at[chunk, 0],
-            out_ref.at[out_rows(kind, chunk)],
-            out_sem.at[kind, chunk],
+            held[k][-1].at[chunk, 0], home(k, chunk), sems[k][5].at[chunk]
         )
 
     def start(copies):
         for copy in copies:
             copy.start()
 
+    def begin(k, chunk):
+        start(first_copies(k, chunk))
+        start(own_copies(k, chunk))
+
     barrier = pltpu.get_barrier_semaphore()
     near = [partner("row", 1)] + [partner(a, b) for a, b, _, _ in plans[0] if a != "img"]
-    for i in range(1, groups):
-        place = dict(places)
-        place["img"] = lax.rem(places["img"] + i, groups)
-        near.append(tuple(place[name] for name in ("img", "row", "col")))
+    near += [other for _, other in other_images()]
     for other in near:
         pl.semaphore_signal(barrier, inc=1, device_id=other, device_id_type=MESH)
     pl.semaphore_wait(barrier, len(near))
 
-    def begin(chunk):
-        for kind in range(2):
-            start(first_copies(kind, chunk))
-            start(own_copies(kind, chunk))
-
-    begin(0)
+    for k in range(number):
+        begin(k, 0)
+
+    def advance(k, stage, chunk):
+        if stage == 0:
+
+            @pl.when(chunk + 1 < kinds[k].chunks)
+            def _():
+                begin(k, chunk + 1)
+
+        buffer = held[k][stage]
+        whole(k, stage, chunk).wait_recv()
+        if stage == 0:
+            count = first_count
+            for copy in own_copies(k, chunk):
+                copy.wait()
+
+            def mine(i):
+                return own[k][lax.rem(chunk, 2), i]
+        else:
+            count = plans[k][stage - 1][2]
+            kept = split(k, stage - 1)[1]
+
+            def mine(i):
+                shard, lines = kept(i)
+                return held[k][stage - 1][chunk, shard, lines]
+
+        def add(i, carry):
+            both = buffer[chunk, i].astype(F32) + mine(i).astype(F32)
+            buffer[chunk, i] = both.astype(BF)
+            return carry
+
+        lax.fori_loop(0, count, add, 0)
+        if stage < len(plans[k]):
+            start(stage_copies(k, stage, chunk))
+        else:
+            start(spread_copies(k, chunk))
+            home_copy(k, chunk).start()
 
     def time_step(t, carry):
-        for stage in range(stages, -1, -1):
-            chunk = t - stage
-
-            @pl.when(jnp.logical_and(chunk >= 0, chunk < steps))
-            def _(stage=stage, chunk=chunk):
-                if stage == 0:
-
-                    @pl.when(chunk + 1 < steps)
-                    def _():
-                        begin(chunk + 1)
-
-                for kind in range(2):
-                    buffer = held[kind][stage]
-                    whole(kind, stage, chunk).wait_recv()
-                    if stage == 0:
-                        for copy in own_copies(kind, chunk):
-                            copy.wait()
-                        count = first_count
-
-                        def add(i, carry, buffer=buffer, kind=kind):
-                            mine = own[kind, lax.rem(chunk, 2), i].astype(F32)
-                            buffer[chunk, i] = (buffer[chunk, i].astype(F32) + mine).astype(BF)
-                            return carry
-                    else:
-                        count = plans[kind][stage - 1][2]
-                        kept = split(kind, stage - 1)[1]
-                        before = held[kind][stage - 1]
-
-                        def add(i, carry, buffer=buffer, before=before, kept=kept):
-                            shard, lines = kept(i)
-                            mine = before[chunk, shard, lines].astype(F32)
-                            buffer[chunk, i] = (buffer[chunk, i].astype(F32) + mine).astype(BF)
-                            return carry
-
-                    lax.fori_loop(0, count, add, 0)
-                    if stage < stages:
-                        start(stage_copies(kind, stage, chunk))
-                    else:
-                        start(spread_copies(kind, chunk))
-                        home_copy(kind, chunk).start()
+        for stage in range(max(len(plan) for plan in plans), -1, -1):
+            for k, kind in enumerate(kinds):
+                if stage <= len(plans[k]):
+                    chunk = t - LAG * stage - kind.first_step
+
+                    @pl.when(jnp.logical_and(chunk >= 0, chunk < kind.chunks))
+                    def _(k=k, stage=stage, chunk=chunk):
+                        advance(k, stage, chunk)
 
         return carry
 
-    lax.fori_loop(0, steps + stages, time_step, 0)
-
-    def drain(chunk, carry):
-        for kind in range(2):
-            for stage in range(stages + 1):
-                whole(kind, stage, chunk).wait_send()
-            for copy in spread_copies(kind, chunk):
+    last = max(k.first_step + k.chunks + LAG * len(plan) for k, plan in zip(kinds, plans))
+    lax.fori_loop(0, last, time_step, 0)
+
+    for k, kind in enumerate(kinds):
+
+        def drain(chunk, carry, k=k):
+            for stage in range(len(plans[k]) + 1):
+                whole(k, stage, chunk).wait_send()
+            for copy in spread_copies(k, chunk):
                 copy.wait()
-            home_copy(kind, chunk).wait()
-        return carry
-
-    lax.fori_loop(0, steps, drain, 0)
-
-
-def sum_everywhere(grads, sizes):
+            home_copy(k, chunk).wait()
+            return carry
+
+        lax.fori_loop(0, kind.chunks, drain, 0)
+
+
+def sum_everywhere(projections, down, up, sizes):
     groups, row_count, cols = sizes
-    count, rows, width = grads.shape
-    height = 16 * groups
-    steps = rows // (2 * height)
-    first_count = count // 2
-    buffers = []
-    for kind in range(2):
-        plan = sum_plan(sizes, bool(kind))
-        buffers.append(pltpu.VMEM((steps, first_count, height, width), BF))
-        buffers += [pltpu.VMEM((steps, c, h, width), BF) for _, _, c, h in plan]
-    stages = len(sum_plan(sizes, False))
+    first_count = row_count * cols // 2
+    kinds = [Kind(D, 16 * groups, projections.shape[1] // (16 * groups), 0, True)]
+    kinds.append(Kind(up.shape[2], 16, up.shape[1] // 16, 0, False))
+    kinds.append(Kind(D, 16, down.shape[1] // 16, kinds[1].chunks, False))
+    scratch = []
+    for kind in kinds:
+        plan = sum_plan(sizes, kind)
+        shapes = [(first_count, kind.height)] + [(c, h) for _, _, c, h in plan]
+        scratch += [pltpu.VMEM((kind.chunks, c, h, kind.width), BF) for c, h in shapes]
+        scratch.append(pltpu.VMEM((2, first_count, kind.height, kind.width), BF))
+        stage_sems = pltpu.SemaphoreType.DMA((len(plan) + 1, kind.chunks))
+        spread_sems = pltpu.SemaphoreType.DMA((groups, kind.chunks))
+        scratch += [
+            stage_sems, stage_sems, spread_sems, spread_sems,
+            pltpu.SemaphoreType.DMA((2,)), pltpu.SemaphoreType.DMA((kind.chunks,)),
+        ]
+    space = pl.BlockSpec(memory_space=pl.ANY)
     return pl.pallas_call(
-        functools.partial(sum_kernel, sizes, steps),
-        out_shape=jax.ShapeDtypeStruct((rows, width), BF),
-        in_specs=[pl.BlockSpec(memory_space=pl.ANY)],
-        out_specs=pl.BlockSpec(memory_space=pl.ANY),
-        scratch_shapes=buffers
-        + [
-            pltpu.VMEM((2, 2, first_count, height, width), BF),
-            pltpu.SemaphoreType.DMA((2, stages + 1, steps)),
-            pltpu.SemaphoreType.DMA((2, stages + 1, steps)),
-            pltpu.SemaphoreType.DMA((2, groups, steps)),
-            pltpu.SemaphoreType.DMA((2, groups, steps)),
-            pltpu.SemaphoreType.DMA((2, 2)),
-            pltpu.SemaphoreType.DMA((2, steps)),
-        ],
+        functools.partial(sum_kernel, sizes, kinds),
+        out_shape=[
+            jax.ShapeDtypeStruct(projections.shape[1:], BF),
+            jax.ShapeDtypeStruct((groups,) + up.shape[1:], BF),
+            jax.ShapeDtypeStruct((groups,) + down.shape[1:], BF),
+        ],
+        in_specs=[space] * 3,
+        out_specs=[space] * 3,
+        scratch_shapes=scratch,
         compiler_params=pltpu.CompilerParams(
-            collective_id=1, has_side_effects=True, vmem_limit_bytes=56 * 2**20
+            collective_id=1, has_side_effects=True, vmem_limit_bytes=58 * 2**20
         ),
         cost_estimate=pl.CostEstimate(flops=2**28, bytes_accessed=2**28, transcendentals=0),
-    )(grads)
+    )(projections, up, down)
 
 
 def all_to_all(values):
@@ -1082,16 +1103,9 @@
     bias_down_grad = column_sum(grad_down_low)
     grad_down_rows = images_gather(grad_down_low)
     every_lead = (0, 1, 2)
-    activated, out_latents = lax.optimization_barrier((activated, out_latents))
-    grad_down_rows = moves.begin(
-        grad_down_rows,
-        down=shard_sum(by_row, all_images, activated, grad_down_rows, every_lead, every_lead, 3),
-    )
+    whole_down = dot(activated, grad_down_rows, every_lead, every_lead)
     grad_hidden = gelu_pull(matmul_back(grad_down_rows, down_full))[0].astype(BF)
-    grad_hidden = moves.begin(
-        grad_hidden,
-        up=shard_sum(by_row, all_images, mlp_in, grad_hidden, every_lead, every_lead, 3),
-    )
+    whole_up = dot(mlp_in, grad_hidden, every_lead, every_lead)
     bias_up_grad = column_sum(grad_hidden)
     grad_mlp_in = images_scatter(matmul_back(grad_hidden, up_full))
     grad_from_mlp, gain_mlp_grad, shift_mlp_grad = mlp_norm_pull(grad_mlp_in)
@@ -1124,13 +1138,10 @@
         grad_attended.reshape(HEADS, HD, img_count, tokens), (0, 2, 1, 3)
     )
     grad_mixed_jobs = all_to_all(grad_attended.reshape(count, jobs, HD, tokens))
-    grad_mixed_jobs = moves.step(grad_mixed_jobs, "down", "up")
     grad_jobs, head_grads = attend_back(
         ext_jobs, qkv_jobs, grad_mixed_jobs, keep, total, every_cos, every_sin, head_cols, geo
     )
-    grad_qkv_t = moves.step(all_to_all(grad_jobs), "down", "up").reshape(
-        HEADS, img_count, 3, HD, tokens
-    )
+    grad_qkv_t = all_to_all(grad_jobs).reshape(HEADS, img_count, 3, HD, tokens)
     grad_qkv_t = moves.begin(
         grad_qkv_t, text=offload_sum(alone, grad_text.reshape(2 * D, img_count * text_count))
     )
@@ -1141,12 +1152,11 @@
         whole_grads[name] = dot(normed, grad_qkv_t[i * D : (i + 1) * D], (0, 1), (1, 2))
     bias_qkv_grad = jnp.sum(grad_qkv_t.astype(F32), axis=(1, 2))
     grad_normed = dot(grad_qkv_t, qkv_full, (0,), (1,))
-    grad_normed = moves.step(grad_normed, "down", "up")
     grad_shift_rows = jnp.sum(grad_normed, axis=1)
     bias_shift_grad = jnp.sum(grad_shift_rows, axis=0)
     grad_from_self, gain_self_grad, shift_self_grad = self_norm_pull(grad_normed)
     grad_resid_in = grad_resid_self + grad_from_self
-    grad_merged = moves.step(grad_resid_in.astype(BF), "down", "up")
+    grad_merged = grad_resid_in.astype(BF)
     whole_grads["skip"] = weight_grad(skip_in, grad_merged)
     bias_skip_grad = column_sum(grad_merged)
     grad_skip_normed = matmul_back(grad_merged, skip_full)
@@ -1166,9 +1176,16 @@
     names = ("query", "key", "value", "skip", "out", "cross_q", "cross_o")
     packed = [whole_grads[name].astype(BF).reshape(count, -1, D) for name in names]
     packed_rows = sum(part.shape[1] for part in packed)
-    fill = -packed_rows % (32 * groups)
+    fill = -packed_rows % (16 * groups)
     packed = jnp.pad(jnp.concatenate(packed, axis=1), ((0, 0), (0, fill), (0, 0)))
-    summed = sum_everywhere(packed, (groups, row_count, col_count)).astype(F32)
+    up_rows = jnp.pad(
+        whole_up.astype(BF).reshape(count, shard, -1), ((0, 0), (0, -shard % 16), (0, 0))
+    )
+    down_rows = whole_down.astype(BF).reshape(count, hid_part, D)
+    summed, up_sums, down_sums = sum_everywhere(
+        packed, down_rows, up_rows, (groups, row_count, col_count)
+    )
+    summed = summed.astype(F32)
     total_of, at = {}, 0
     for name in names:
         rows = whole_grads[name].shape[0] // count
@@ -1242,9 +1259,9 @@
     )
 
     total_up = jnp.transpose(
-        shards["up"].reshape(groups, shard, count, hid_part), (1, 2, 0, 3)
+        up_sums[:, :shard].reshape(groups, shard, count, hid_part), (1, 2, 0, 3)
     ).reshape(shard, FF)
-    total_down = shards["down"].reshape(hid_shard, D)
+    total_down = down_sums.reshape(hid_shard, D)
     return (
         out_latents,
         grad_latents,

time: 1230 us -> 1040 us (0.85)
  waiting for transfers between devices: 470 us -> 239 us
  Pallas kernels: 240 us -> 308 us
  other arithmetic: 83.1 us -> 57.9 us
    ppermute x10 -> x0, waiting for transfers between devices: 183 us -> none  [exchange(): return lax.ppermute(values, axis, [(i, i ^ bit) for i in range(size)])]
    pallas_call x1, Pallas kernels: 170 us -> 238 us  [sum_everywhere(): pl.pallas_call(functools.partial(sum_kernel, sizes, kinds), out_shape=[ja...]
    ppermute x8, waiting for transfers between devices: 43.8 us -> 21.1 us  [swap_images(): return lax.ppermute(values, 'img', [(i, i ^ bit) for i in range(count)])]
    all_to_all x6, waiting for transfers between devices: 141 us -> 120 us  [all_to_all(): lax.all_to_all(values, GROUP, split_axis=0, concat_axis=0, tiled=True)]
    unnamed x439 -> x421, local copies, waits for them, and re-layouts: 54.6 us -> 52.9 us
    dot_general x34 -> x32, matrix products: 141 us -> 142 us  [dot(): lax.dot_general(former, latter, ((former_dims, latter_dims), ((), ())), p...]
  transfers between devices with their start and end apart: 40 -> 30, of which waited for: 22 -> 12; matrix products, arithmetic and copies ran while one was open for 24% -> 29% of each run, Pallas kernels for 18% -> 26%
where the time goes in v3:
time: 1040 us; the launch traced here: 1020 us
  Pallas kernels  308 us (30%)
  waiting for transfers between devices  239 us (23%)
  local copies, waits for them, and re-layouts  181 us (17%)
  matrix products  144 us (14%)
  starting transfers between devices  74.4 us (7%)
  other arithmetic  57.9 us (6%)
  between operations  17.5 us (2%)
    pallas_call x1, Pallas kernels, sum_everywhere(): pl.pallas_call(functools.partial(sum_kernel, sizes, kinds), out_shape=[ja...  238 us
    dot_general x32, matrix products, dot(): lax.dot_general(former, latter, ((former_dims, latter_dims), ((), ())), p...  142 us
    all_to_all x6, waiting for transfers between devices, all_to_all(): lax.all_to_all(values, GROUP, split_axis=0, concat_axis=0, tiled=True)  120 us
    all_gather x1, waiting for transfers between devices, body(): third_all = lax.all_gather(third, GROUP, axis=0, tiled=True)  56.6 us
    unnamed x421, local copies, waits for them, and re-layouts  52.9 us
    all_gather x1, waiting for transfers between devices, body(): lax.all_gather(jnp.concatenate([beside(skip_weight, 2), qkv_weight], axis...  38.2 us
    all_to_all x6, starting transfers between devices, all_to_all(): lax.all_to_all(values, GROUP, split_axis=0, concat_axis=0, tiled=True)  35 us
    pallas_call x1, Pallas kernels, attend_back(): pl.pallas_call(functools.partial(attend_back_kernel, geo), grid=(jobs,),...  26.3 us
  transfers between devices with their start and end apart: 30, of which 12 were waited for; matrix products, arithmetic and copies ran while one was open for 29% of the time, Pallas kernels for 26%

profile of v3, /device:TPU:0, one launch (start us, length us, event | category | flops | bytes accessed | tf_op | source)
XLA Modules:
  0.0 1021.5 jit_solution(5595132576421834425)
XLA Ops:
  13.1 7.4 all-to-all-start
  27.3 24.0 %all-to-all-done = bf16[16,240,128]{2,1,0:T(8,128)(2,1)S(1)} async-done(((bf16[16,240,128]{2,1,0:T(8,128)(2,1)}), bf16[16,240,128]{2,1,0:T(8,128)(2,1)S(1)}, u32[]{:S(2)}, u32[]{:S(2)}) %all-to-all-start) | async-done | bytes 983072 | tf_op jit(solution)/shard_map/all_to_all | solution.py:898
  100.7 38.2 %all-gather.4.cloned.1.call-done = bf16[1408,7040]{1,0:T(8,128)(2,1)} async-done(((bf16[88,7040]{1,0:T(8,128)(2,1)}), bf16[1408,7040]{1,0:T(8,128)(2,1)}) %all-gather.4.cloned.1.call-update) | async-done | bytes 19824656 | tf_op jit(solution)/shard_map/all_gather | solution.py:950
  152.3 7.3 fusion.151
  161.1 8.1 fusion.7
  170.8 8.6 all-to-all-start.1
  201.2 76.8 %all-to-all-done.1.qkv_ref = bf16[16,2,3,88,128]{4,3,2,1,0:T(8,128)(2,1)S(1)} async-done(((bf16[16,2,3,88,128]{4,3,2,1,0:T(8,128)(2,1)}), bf16[16,2,3,88,128]{4,3,2,1,0:T(8,128)(2,1)S(1)}, u32[]{:S(2)}, u32[]{:S(2)}) %all-to-all-start.1) | async-done | bytes 2162720 | tf_op jit(solution)/shard_map/all_to_all | solution.py:898
  279.6 15.6 %shard_map.488 = (bf16[16,2,88,128]{3,2,1,0:T(8,128)(2,1)S(1)}, f32[2,88,2048]{2,1,0:T(8,128)S(1)}, f32[2,1,2048]{2,1,0:T(1,128)S(1)}) custom-call(s32[2,2]{1,0:T(2,128)S(1)} %broadcast_select_fusion.ext_ref, bf16[16,2,3,88,128]{4,3,2,1,0:T(8,128)(2,1)S(1)} %all-to-all-done.1.qkv_ref, f32[88,2048]{1,0:T(8,128)S(1)} %copy-done.5, ...), custom_call_target="tpu_custom_call" | custom-call | flops 8858370048 | bytes 6291456 | tf_op jit(solution)/shard_map/pallas_call | solution.py:353
  312.1 10.7 %all-to-all-done.2 = bf16[16,2,88,128]{3,2,1,0:T(8,128)(2,1)S(1)} async-done(((bf16[16,2,88,128]{3,2,1,0:T(8,128)(2,1)}), bf16[16,2,88,128]{3,2,1,0:T(8,128)(2,1)S(1)}, u32[]{:S(2)}, u32[]{:S(2)}) %all-to-all-start.2) | async-done | bytes 720928 | tf_op jit(solution)/shard_map/all_to_all | solution.py:898
  331.8 12.6 %shard_map.489 = (bf16[16,88,256]{2,1,0:T(8,128)(2,1)S(1)}, f32[16,1,256]{2,1,0:T(1,128)S(1)}) custom-call(s32[2,2]{1,0:T(2,128)S(1)} %copy-done.9, f32[16,88,256]{2,1,0:T(8,128)S(1)} %bitcast.328, bf16[2,16,88,768]{3,2,1,0:T(8,128)(2,1)S(1)} %bitcast.324, f32[88,256]{1,0:T(8,128)S(1)} %get-tuple-element.280.cos_ref, ...), custom_call_target="tpu_custom_call" | custom-call | flops 4294967296 | bytes 10485760 | tf_op jit(solution)/shard_map/pallas_call | solution.py:586
  351.4 56.6 %all-gather.8.cloned.1.call-done = bf16[1536,5888]{1,0:T(8,128)(2,1)} async-done(((bf16[96,5888]{1,0:T(8,128)(2,1)}), bf16[1536,5888]{1,0:T(8,128)(2,1)}) %all-gather.8.cloned.1.call-update) | async-done | bytes 18087952 | tf_op jit(solution)/shard_map/all_gather | solution.py:1033
  414.1 7.7 slice.662
  421.8 7.8 pad_maximum_fusion
  429.6 10.6 %fusion.62 = f32[2,2,128,3072]{3,2,1,0:T(8,128)} fusion(bf16[1408,3072,1,1]{1,0,3,2:T(8,128)(2,1)} %bitcast.347, bf16[1,2,128,1408]{3,2,1,0:T(8,128)(2,1)S(1)} %collective-permute-done.4, bf16[1,2,128,1408]{3,2,1,0:T(8,128)(2,1)S(1)} %fusion.63), kind=kOutput, calls=%fused_computation.121 | convolution fusion | flops 4429905920 | bytes 16384000 | tf_op jit(solution)/shard_map/dot_general | solution.py:45
  440.3 12.6 %convert_reduce_fusion = (bf16[3072]{0:T(1024)(128)(2,1)S(1)}, bf16[2,2,128,3072]{3,2,1,0:T(8,128)(2,1)}) fusion(f32[2,2,128,3072]{3,2,1,0:T(8,128)} %fusion.62, f32[3072]{0:T(1024)S(1)} %add.485, bf16[3072,1408,1,1]{1,0,3,2:T(8,128)(2,1)S(1)} %bitcast.345, bf16[1,2,128,1408]{3,2,1,0:T(8,128)(2,1)} %collective-permute-done.10, ...), kind=kOutput, calls=%fused_computation.30 | convolution fusion | flops 4466078720 | bytes 19548160 | tf_op jit(solution)/shard_map/dot_general | solution.py:45
  462.6 8.1 fusion.122
  482.5 11.7 %collective-permute-done.5 = bf16[1,2,128,1408]{3,2,1,0:T(8,128)(2,1)} collective-permute-done((bf16[1,2,128,1408]{3,2,1,0:T(8,128)(2,1)}, bf16[1,2,128,1408]{3,2,1,0:T(8,128)(2,1)}, u32[]{:S(2)}, u32[]{:S(2)}) %collective-permute-start.5) | collective-permute-done | bytes 720928 | tf_op jit(solution)/shard_map/ppermute | solution.py:113
  502.2 15.4 %shard_map.490 = (bf16[16,88,256]{2,1,0:T(8,128)(2,1)S(1)}, bf16[2,16,88,768]{3,2,1,0:T(8,128)(2,1)S(1)}, f32[8,88,2]{2,1,0:T(8,128)S(1)}) custom-call(s32[2,2]{1,0:T(2,128)S(1)} %copy-done.9, f32[16,88,256]{2,1,0:T(8,128)S(1)} %bitcast.329, bf16[2,16,88,768]{3,2,1,0:T(8,128)(2,1)S(1)} %bitcast.327, bf16[16,88,256]{2,1,0:T(8,128)(2,1)S(1)} %bitcast.330, ...), custom_call_target="tpu_custom_call" | custom-call | flops 8589934592 | bytes 16777216 | tf_op jit(solution)/shard_map/pallas_call | solution.py:606
  537.2 10.2 %bitcast_convert_fusion.1 = bf16[1408,3072]{1,0:T(8,128)(2,1)} fusion(bf16[2,2,128,3072]{3,2,1,0:T(8,128)(2,1)} %get-tuple-element.293, bf16[1,2,128,1408]{3,2,1,0:T(8,128)(2,1)} %copy-done.183, bf16[1,2,128,1408]{3,2,1,0:T(8,128)(2,1)S(1)} %copy-done.80), kind=kOutput, calls=%fused_computation.2 | convolution fusion | flops 4434231296 | bytes 13238272 | tf_op jit(solution)/shard_map/dot_general | solution.py:45
  547.5 8.1 pad.24.refs_1_
  557.0 26.3 %shard_map.491 = (bf16[16,2,3,88,128]{4,3,2,1,0:T(8,128)(2,1)}, f32[2,88,4]{2,1,0:T(8,128)}) custom-call(s32[2,2]{1,0:T(2,128)} %copy-done.8, bf16[16,2,3,88,128]{4,3,2,1,0:T(8,128)(2,1)} %copy-done.3, bf16[16,2,88,128]{3,2,1,0:T(8,128)(2,1)} %all-to-all-done.3.dout_ref, f32[2,88,2048]{2,1,0:T(8,128)} %copy-done.12, f32[2,1,2048]{2,1,0:T(1,128)} %copy-done.13, ...), custom_call_target="tpu_custom_call" | custom-call | flops 22145925120 | bytes 8388608 | tf_op jit(solution)/shard_map/pallas_call | solution.py:457
  588.2 11.4 %bitcast_convert_fusion = bf16[3072,1408]{1,0:T(8,128)(2,1)} fusion(bf16[1,2,128,1408]{3,2,1,0:T(8,128)(2,1)} %collective-permute-done.10, bf16[1,2,128,1408]{3,2,1,0:T(8,128)(2,1)} %convert_bitcast_fusion.1, f32[2,2,128,3072]{3,2,1,0:T(8,128)} %fusion.62, f32[3072]{0:T(1024)S(1)} %copy-done.138), kind=kOutput, calls=%fused_computation.1 | convolution fusion | flops 4449959936 | bytes 16396288 | tf_op jit(solution)/shard_map/dot_general | solution.py:45
  643.5 7.4 fusion.124
  713.2 237.7 %shard_map.492 = (bf16[704,1408]{1,0:T(8,128)(2,1)}, bf16[2,96,3072]{2,1,0:T(8,128)(2,1)}, bf16[2,192,1408]{2,1,0:T(8,128)(2,1)}) custom-call(bf16[16,704,1408]{2,1,0:T(8,128)(2,1)} %constant_dynamic-update-slice_fusion.21.refs_0_, bf16[16,96,3072]{2,1,0:T(8,128)(2,1)} %pad.24.refs_1_, bf16[16,192,1408]{2,1,0:T(8,128)(2,1)} %bitcast.352), custom_call_target="tpu_custom_call" | custom-call | flops 268435456 | bytes 268435456 | tf_op jit(solution)/shard_map/pallas_call | solution.py:880
  (783 shorter events, 363.3 us)
Async XLA Ops:
  7.3 131.6 %all-gather.4.cloned.1.call-start = ((), (), s32[]{:S(2)}) async-start(), calls=%async_computation.7 | async-start | bytes 21063680 | tf_op jit(solution)/shard_map/all_gather | solution.py:950
  13.1 38.2 %all-to-all-start = ((bf16[16,240,128]{2,1,0:T(8,128)(2,1)}), bf16[16,240,128]{2,1,0:T(8,128)(2,1)S(1)}, u32[]{:S(2)}, u32[]{:S(2)}) async-start(bf16[16,240,128]{2,1,0:T(8,128)(2,1)} %broadcast_in_dim.186), calls=%async_computation | async-start | bytes 1966080 | tf_op jit(solution)/shard_map/all_to_all | solution.py:898
  20.5 286.6 %all-gather.6.cloned.1.call-start = ((), (), s32[]{:S(2)}) async-start(), calls=%async_computation.8 | async-start | bytes 17233920 | tf_op jit(solution)/shard_map/all_gather | solution.py:1023
  55.5 352.5 %all-gather.8.cloned.1.call-start = ((), (), s32[]{:S(2)}) async-start(), calls=%async_computation.9 | async-start | bytes 19218432 | tf_op jit(solution)/shard_map/all_gather | solution.py:1033
  74.7 7.8 collective-permute-start.3
  76.0 6.5 collective-permute-start.2
  170.8 107.2 %all-to-all-start.1 = ((bf16[16,2,3,88,128]{4,3,2,1,0:T(8,128)(2,1)}), bf16[16,2,3,88,128]{4,3,2,1,0:T(8,128)(2,1)S(1)}, u32[]{:S(2)}, u32[]{:S(2)}) async-start(bf16[16,2,3,88,128]{4,3,2,1,0:T(8,128)(2,1)} %bitcast.351), calls=%async_computation.1 | async-start | bytes 4325376 | tf_op jit(solution)/shard_map/all_to_all | solution.py:898
  297.3 25.5 %all-to-all-start.2 = ((bf16[16,2,88,128]{3,2,1,0:T(8,128)(2,1)}), bf16[16,2,88,128]{3,2,1,0:T(8,128)(2,1)S(1)}, u32[]{:S(2)}, u32[]{:S(2)}) async-start(bf16[16,2,88,128]{3,2,1,0:T(8,128)(2,1)} %copy-done.6), calls=%async_computation.2 | async-start | bytes 1441792 | tf_op jit(solution)/shard_map/all_to_all | solution.py:898
  305.5 134.8 %collective-permute-start.10 = (bf16[1,2,128,1408]{3,2,1,0:T(8,128)(2,1)}, bf16[1,2,128,1408]{3,2,1,0:T(8,128)(2,1)}, u32[]{:S(2)}, u32[]{:S(2)}) collective-permute-start(bf16[1,2,128,1408]{3,2,1,0:T(8,128)(2,1)} %convert_bitcast_fusion.1), channel_id=1, source_target_pairs={{0,16},{16,0},{1,17},{17,1},{2,18},{18,2},{3,19},{19,3},{4,20},{20... | collective-permute-start | bytes 2162696 | tf_op jit(solution)/shard_map/ppermute | solution.py:113
  349.9 79.7 %collective-permute-start.4 = (bf16[1,2,128,1408]{3,2,1,0:T(8,128)(2,1)S(1)}, bf16[1,2,128,1408]{3,2,1,0:T(8,128)(2,1)S(1)}, u32[]{:S(2)}, u32[]{:S(2)}) collective-permute-start(bf16[1,2,128,1408]{3,2,1,0:T(8,128)(2,1)S(1)} %fusion.63), channel_id=1, source_target_pairs={{0,16},{16,0},{1,17},{17,1},{2,18},{18,2},{3,19},{19,3},{4,20},{20... | collective-permute-start | bytes 2162696 | tf_op jit(solution)/shard_map/ppermute | solution.py:113
  461.0 19.4 %collective-permute-start.11 = (bf16[1,2,128,1408]{3,2,1,0:T(8,128)(2,1)}, bf16[1,2,128,1408]{3,2,1,0:T(8,128)(2,1)S(1)}, u32[]{:S(2)}, u32[]{:S(2)}) collective-permute-start(bf16[1,2,128,1408]{3,2,1,0:T(8,128)(2,1)} %slice.823), channel_id=1, source_target_pairs={{0,16},{16,0},{1,17},{17,1},{2,18},{18,2},{3,19},{19,3},{4,20},{20... | collective-permute-start | bytes 2162696 | tf_op jit(solution)/shard_map/ppermute | solution.py:113
  472.5 21.7 %collective-permute-start.5 = (bf16[1,2,128,1408]{3,2,1,0:T(8,128)(2,1)}, bf16[1,2,128,1408]{3,2,1,0:T(8,128)(2,1)}, u32[]{:S(2)}, u32[]{:S(2)}) collective-permute-start(bf16[1,2,128,1408]{3,2,1,0:T(8,128)(2,1)} %slice.824), channel_id=1, source_target_pairs={{0,16},{16,0},{1,17},{17,1},{2,18},{18,2},{3,19},{19,3},{4,20},{20... | collective-permute-start | bytes 2162696 | tf_op jit(solution)/shard_map/ppermute | solution.py:113
  531.7 25.4 %all-to-all-start.3 = ((bf16[16,2,88,128]{3,2,1,0:T(8,128)(2,1)}), bf16[16,2,88,128]{3,2,1,0:T(8,128)(2,1)}, u32[]{:S(2)}, u32[]{:S(2)}) async-start(bf16[16,2,88,128]{3,2,1,0:T(8,128)(2,1)} %bitcast.316), calls=%async_computation.3 | async-start | bytes 1441792 | tf_op jit(solution)/shard_map/all_to_all | solution.py:898
  583.4 55.6 %all-to-all-start.4 = ((bf16[16,2,3,88,128]{4,3,2,1,0:T(8,128)(2,1)}), bf16[16,2,3,88,128]{4,3,2,1,0:T(8,128)(2,1)}, u32[]{:S(2)}, u32[]{:S(2)}) async-start(bf16[16,2,3,88,128]{4,3,2,1,0:T(8,128)(2,1)} %get-tuple-element.44), calls=%async_computation.4 | async-start | bytes 4325376 | tf_op jit(solution)/shard_map/all_to_all | solution.py:898
  588.1 369.8 %reduce-scatter.2.cloned.1.call-start = ((), (), s32[]{:S(2)}) async-start(), calls=%async_computation.10 | async-start | bytes 4595712 | tf_op jit(solution)/shard_map/reduce_scatter | solution.py:141
  600.2 16.9 %collective-permute-start.7 = (f32[2,1,8,144]{3,2,1,0:T(8,128)S(1)}, f32[2,1,8,144]{3,2,1,0:T(8,128)S(1)}, u32[]{:S(2)}, u32[]{:S(2)}) collective-permute-start(f32[2,1,8,144]{3,2,1,0:T(8,128)S(1)} %get-tuple-element.243), channel_id=1, source_target_pairs={{4,0},{8,4},{12,8},{5,1},{9,5},{13,9},{6,2},{10,6},{14,10},{7,3},{... | collective-permute-start | bytes 27656 | tf_op jit(solution)/shard_map/ppermute | solution.py:39
  601.5 15.7 %collective-permute-start.6 = (f32[2,1,8,144]{3,2,1,0:T(8,128)S(1)}, f32[2,1,8,144]{3,2,1,0:T(8,128)S(1)}, u32[]{:S(2)}, u32[]{:S(2)}) collective-permute-start(f32[2,1,8,144]{3,2,1,0:T(8,128)S(1)} %get-tuple-element.242), channel_id=1, source_target_pairs={{0,4},{4,8},{8,12},{1,5},{5,9},{9,13},{2,6},{6,10},{10,14},{3,7},{... | collective-permute-start | bytes 27656 | tf_op jit(solution)/shard_map/ppermute | solution.py:36
  617.2 10.8 %collective-permute-start.9 = (f32[2,18,1,144]{3,2,1,0:T(1,128)S(1)}, f32[2,18,1,144]{3,2,1,0:T(1,128)S(1)}, u32[]{:S(2)}, u32[]{:S(2)}) collective-permute-start(f32[2,18,1,144]{3,2,1,0:T(1,128)S(1)} %get-tuple-element.230), channel_id=1, source_target_pairs={{0,1},{1,2},{2,3},{4,5},{5,6},{6,7},{8,9},{9,10},{10,11},{12,13},{... | collective-permute-start | bytes 62216 | tf_op jit(solution)/shard_map/ppermute | solution.py:36
  621.0 7.1 collective-permute-start.8
  664.1 320.4 %collective-permute-start.13 = (f32[2,1,8,144]{3,2,1,0:T(8,128)}, f32[2,1,8,144]{3,2,1,0:T(8,128)S(1)}, u32[]{:S(2)}, u32[]{:S(2)}) collective-permute-start(f32[2,1,8,144]{3,2,1,0:T(8,128)} %get-tuple-element.241), channel_id=1, source_target_pairs={{4,0},{8,4},{12,8},{5,1},{9,5},{13,9},{6,2},{10,6},{14,10},{7,3},{... | collective-permute-start | bytes 27656 | tf_op jit(solution)/shard_map/ppermute | solution.py:39
  665.4 319.1 %collective-permute-start.12 = (f32[2,1,8,144]{3,2,1,0:T(8,128)}, f32[2,1,8,144]{3,2,1,0:T(8,128)S(1)}, u32[]{:S(2)}, u32[]{:S(2)}) collective-permute-start(f32[2,1,8,144]{3,2,1,0:T(8,128)} %get-tuple-element.240), channel_id=1, source_target_pairs={{0,4},{4,8},{8,12},{1,5},{5,9},{9,13},{2,6},{6,10},{10,14},{3,7},{... | collective-permute-start | bytes 27656 | tf_op jit(solution)/shard_map/ppermute | solution.py:36
  962.5 34.4 %all-to-all-start.5 = ((bf16[16,240,128]{2,1,0:T(8,128)(2,1)}), bf16[16,240,128]{2,1,0:T(8,128)(2,1)}, u32[]{:S(2)}, u32[]{:S(2)}) async-start(bf16[16,240,128]{2,1,0:T(8,128)(2,1)} %bitcast.146), calls=%async_computation.6 | async-start | bytes 1966080 | tf_op jit(solution)/shard_map/all_to_all | solution.py:898
  983.2 12.7 %collective-permute-start.18 = (bf16[1024,176]{0,1:T(8,128)(2,1)S(1)}, bf16[1024,176]{0,1:T(8,128)(2,1)S(1)}, u32[]{:S(2)}, u32[]{:S(2)}) collective-permute-start(bf16[1024,176]{0,1:T(8,128)(2,1)S(1)} %fusion.57), channel_id=1, source_target_pairs={{0,16},{16,0},{1,17},{17,1},{2,18},{18,2},{3,19},{19,3},{4,20},{20... | collective-permute-start | bytes 1081352 | tf_op jit(solution)/shard_map/ppermute | solution.py:113
  1000.4 13.3 %collective-permute-start.17 = (f32[88,1408]{1,0:T(8,128)S(1)}, f32[88,1408]{1,0:T(8,128)S(1)}, u32[]{:S(2)}, u32[]{:S(2)}) collective-permute-start(f32[88,1408]{1,0:T(8,128)S(1)} %fusion.118), channel_id=1, source_target_pairs={{0,16},{16,0},{1,17},{17,1},{2,18},{18,2},{3,19},{19,3},{4,20},{20... | collective-permute-start | bytes 1486856 | tf_op jit(solution)/shard_map/ppermute | solution.py:113
  (198 other events, 2606.7 us)
Sparse Core Ops, SparseCore 0:
  11.0 127.8 all-gather.3
  141.7 163.7 all-gather.5
  307.1 100.8 all-gather.7
  670.1 78.9 reduce-scatter.1

commit v4 on v3

--- a/solution.py
+++ b/solution.py
@@ -625,24 +625,30 @@
 
 MESH = pl.DeviceIdType.MESH
 LAG = 3
+ROW_SHARE = 5
 
 
 class Kind(NamedTuple):
+    operand: int
+    first_row: int
     width: int
     height: int
     chunks: int
-    first_step: int
-    over_images: bool
+    stride: int
+    order: tuple
 
 
 def sum_plan(sizes, kind):
     groups, row_count, cols = sizes
     count, height = row_count * cols // 2, kind.height
-    image_bits = [("img", 1 << i) for i in range(groups.bit_length() - 1)]
-    row_bits = [("row", 1 << i) for i in range(1, row_count.bit_length() - 1)]
-    col_bits = [("col", 1 << i) for i in range(cols.bit_length() - 1)]
+    firsts = {"img": (0, groups), "row": (1, row_count), "col": (0, cols)}
     plan = []
-    for axis, bit in (image_bits if kind.over_images else []) + row_bits + col_bits:
+    for axis, i in [
+        (axis, i)
+        for axis in kind.order
+        for i in range(firsts[axis][0], firsts[axis][1].bit_length() - 1)
+    ]:
+        bit = 1 << i
         if axis == "img":
             height //= 2
         else:
@@ -653,7 +659,7 @@
 
 def sum_kernel(sizes, kinds, *refs):
     groups, row_count, cols = sizes
-    number = len(kinds)
+    number = 1 + max(kind.operand for kind in kinds)
     grads_refs, out_refs, scratch = refs[:number], refs[number : 2 * number], refs[2 * number :]
     first_count = row_count * cols // 2
     places = {axis: lax.axis_index(axis) for axis in ("img", "row", "col")}
@@ -687,14 +693,14 @@
         return places[axis] // bit % 2
 
     def chunk_rows(k, chunk):
-        return pl.multiple_of(chunk * kinds[k].height, 16)
+        return pl.multiple_of(kinds[k].first_row + chunk * kinds[k].height, 16)
 
     def first_copies(k, chunk):
         rows = pl.ds(chunk_rows(k, chunk), kinds[k].height)
         for i in range(row_count // 2):
             shards = pl.ds((2 * i + 1 - core) * cols, cols)
             yield pltpu.make_async_remote_copy(
-                src_ref=grads_refs[k].at[shards, rows],
+                src_ref=grads_refs[kinds[k].operand].at[shards, rows],
                 dst_ref=held[k][0].at[chunk, pl.ds(i * cols, cols)],
                 send_sem=sems[k][0].at[0, chunk],
                 recv_sem=sems[k][1].at[0, chunk],
@@ -707,7 +713,7 @@
         for i in range(row_count // 2):
             shards = pl.ds((2 * i + core) * cols, cols)
             yield pltpu.make_async_copy(
-                grads_refs[k].at[shards, rows],
+                grads_refs[kinds[k].operand].at[shards, rows],
                 own[k].at[lax.rem(chunk, 2), pl.ds(i * cols, cols)],
                 sems[k][4].at[lax.rem(chunk, 2)],
             )
@@ -753,12 +759,13 @@
 
     def home(k, chunk):
         rows = plans[k][-1][3]
-        if not kinds[k].over_images:
-            return out_refs[k].at[places["img"], pl.ds(chunk_rows(k, chunk), rows)]
+        out_ref = out_refs[kinds[k].operand]
+        if "img" not in kinds[k].order:
+            return out_ref.at[places["img"], pl.ds(chunk_rows(k, chunk), rows)]
         place = 0
         for i in range(image_stages):
             place = place + bit_of("img", 1 << i) * (1 << (image_stages - 1 - i))
-        return out_refs[k].at[pl.ds(pl.multiple_of(chunk_rows(k, chunk) + place * rows, 16), rows)]
+        return out_ref.at[pl.ds(pl.multiple_of(chunk_rows(k, chunk) + place * rows, 16), rows)]
 
     def spread_copies(k, chunk):
         for i, other in other_images():
@@ -791,7 +798,7 @@
         pl.semaphore_signal(barrier, inc=1, device_id=other, device_id_type=MESH)
     pl.semaphore_wait(barrier, len(near))
 
-    for k in range(number):
+    for k in range(len(kinds)):
         begin(k, 0)
 
     def advance(k, stage, chunk):
@@ -834,15 +841,17 @@
         for stage in range(max(len(plan) for plan in plans), -1, -1):
             for k, kind in enumerate(kinds):
                 if stage <= len(plans[k]):
-                    chunk = t - LAG * stage - kind.first_step
-
-                    @pl.when(jnp.logical_and(chunk >= 0, chunk < kind.chunks))
+                    since = t - LAG * stage
+                    chunk = since // kind.stride
+                    due = jnp.logical_and(since >= 0, since % kind.stride == 0)
+
+                    @pl.when(jnp.logical_and(due, chunk < kind.chunks))
                     def _(k=k, stage=stage, chunk=chunk):
                         advance(k, stage, chunk)
 
         return carry
 
-    last = max(k.first_step + k.chunks + LAG * len(plan) for k, plan in zip(kinds, plans))
+    last = max(k.stride * k.chunks + LAG * len(plan) for k, plan in zip(kinds, plans))
     lax.fori_loop(0, last, time_step, 0)
 
     for k, kind in enumerate(kinds):
@@ -861,9 +870,16 @@
 def sum_everywhere(projections, down, up, sizes):
     groups, row_count, cols = sizes
     first_count = row_count * cols // 2
-    kinds = [Kind(D, 16 * groups, projections.shape[1] // (16 * groups), 0, True)]
-    kinds.append(Kind(up.shape[2], 16, up.shape[1] // 16, 0, False))
-    kinds.append(Kind(D, 16, down.shape[1] // 16, kinds[1].chunks, False))
+    height = 16 * groups
+    chunks = projections.shape[1] // height
+    late = max(1, chunks * ROW_SHARE // 22)
+    early = chunks - late
+    kinds = [
+        Kind(0, 0, D, height, early, 1, ("img", "row", "col")),
+        Kind(0, early * height, D, height, late, 3, ("row", "img", "col")),
+        Kind(1, 0, up.shape[2], 16, up.shape[1] // 16, 3, ("row", "col")),
+        Kind(2, 0, D, 16, down.shape[1] // 16, 1, ("col", "row")),
+    ]
     scratch = []
     for kind in kinds:
         plan = sum_plan(sizes, kind)
@@ -1122,6 +1138,10 @@
     )
     cross_head_grads = jnp.sum(cross_head_grads, axis=0)
     grad_cross_rows = grad_cross_rows.reshape(D, all_tokens)
+    grad_cross_rows = moves.begin(
+        grad_cross_rows,
+        text=offload_sum(alone, grad_text.reshape(2 * D, img_count * text_count)),
+    )
     whole_grads["cross_q"] = dot(cross_in.reshape(all_tokens, D), grad_cross_rows, (0,), (1,))
     bias_cross_q_grad = jnp.sum(grad_cross_rows.astype(F32), axis=1)
     grad_cross_in = dot(grad_cross_rows, cross_q_full, (0,), (1,))
@@ -1142,9 +1162,6 @@
         ext_jobs, qkv_jobs, grad_mixed_jobs, keep, total, every_cos, every_sin, head_cols, geo
     )
     grad_qkv_t = all_to_all(grad_jobs).reshape(HEADS, img_count, 3, HD, tokens)
-    grad_qkv_t = moves.begin(
-        grad_qkv_t, text=offload_sum(alone, grad_text.reshape(2 * D, img_count * text_count))
-    )
     grad_qkv_t = jnp.transpose(grad_qkv_t, (2, 0, 3, 1, 4)).reshape(3 * D, img_count, tokens)
     head_grads = jnp.sum(head_grads, axis=0)
 

time: 1040 us -> 1000 us (0.962)
  Pallas kernels: 308 us -> 282 us
    pallas_call x1, Pallas kernels: 238 us -> 212 us  [sum_everywhere(): pl.pallas_call(functools.partial(sum_kernel, sizes, kinds), out_shape=[ja...]
    unnamed x421 -> x409, local copies, waits for them, and re-layouts: 52.9 us -> 52.9 us
  transfers between devices with their start and end apart: 30 -> 30, of which waited for: 12 -> 13; matrix products, arithmetic and copies ran while one was open for 29% -> 32% of each run, Pallas kernels for 26% -> 24%
where the time goes in v4:
time: 1000 us; the launch traced here: 988 us
  Pallas kernels  282 us (28%)
  waiting for transfers between devices  231 us (23%)
  local copies, waits for them, and re-layouts  181 us (18%)
  matrix products  143 us (14%)
  starting transfers between devices  75 us (8%)
  other arithmetic  59.3 us (6%)
  between operations  17.4 us (2%)
    pallas_call x1, Pallas kernels, sum_everywhere(): pl.pallas_call(functools.partial(sum_kernel, sizes, kinds), out_shape=[ja...  212 us
    dot_general x32, matrix products, dot(): lax.dot_general(former, latter, ((former_dims, latter_dims), ((), ())), p...  142 us
    all_to_all x6, waiting for transfers between devices, all_to_all(): lax.all_to_all(values, GROUP, split_axis=0, concat_axis=0, tiled=True)  113 us
    all_gather x1, waiting for transfers between devices, body(): third_all = lax.all_gather(third, GROUP, axis=0, tiled=True)  54.5 us
    unnamed x409, local copies, waits for them, and re-layouts  52.9 us
    all_gather x1, waiting for transfers between devices, body(): lax.all_gather(jnp.concatenate([beside(skip_weight, 2), qkv_weight], axis...  38.6 us
    all_to_all x6, starting transfers between devices, all_to_all(): lax.all_to_all(values, GROUP, split_axis=0, concat_axis=0, tiled=True)  34.9 us
    pallas_call x1, Pallas kernels, attend_back(): pl.pallas_call(functools.partial(attend_back_kernel, geo), grid=(jobs,),...  26.3 us
  transfers between devices with their start and end apart: 30, of which 13 were waited for; matrix products, arithmetic and copies ran while one was open for 32% of the time, Pallas kernels for 24%

profile of v4, /device:TPU:0, one launch (start us, length us, event | category | flops | bytes accessed | tf_op | source)
XLA Modules:
  0.0 988.3 jit_solution(15835166333898076495)
XLA Ops:
  13.1 7.4 all-to-all-start
  27.3 24.0 %all-to-all-done = bf16[16,240,128]{2,1,0:T(8,128)(2,1)S(1)} async-done(((bf16[16,240,128]{2,1,0:T(8,128)(2,1)}), bf16[16,240,128]{2,1,0:T(8,128)(2,1)S(1)}, u32[]{:S(2)}, u32[]{:S(2)}) %all-to-all-start) | async-done | bytes 983072 | tf_op jit(solution)/shard_map/all_to_all | solution.py:914
  100.3 38.6 %all-gather.4.cloned.1.call-done = bf16[1408,7040]{1,0:T(8,128)(2,1)} async-done(((bf16[88,7040]{1,0:T(8,128)(2,1)}), bf16[1408,7040]{1,0:T(8,128)(2,1)}) %all-gather.4.cloned.1.call-update) | async-done | bytes 19824656 | tf_op jit(solution)/shard_map/all_gather | solution.py:966
  152.3 7.2 fusion.149
  161.1 8.1 fusion.7
  170.8 8.9 all-to-all-start.1
  201.4 76.3 %all-to-all-done.1.qkv_ref = bf16[16,2,3,88,128]{4,3,2,1,0:T(8,128)(2,1)S(1)} async-done(((bf16[16,2,3,88,128]{4,3,2,1,0:T(8,128)(2,1)}), bf16[16,2,3,88,128]{4,3,2,1,0:T(8,128)(2,1)S(1)}, u32[]{:S(2)}, u32[]{:S(2)}) %all-to-all-start.1) | async-done | bytes 2162720 | tf_op jit(solution)/shard_map/all_to_all | solution.py:914
  279.3 15.6 %shard_map.488 = (bf16[16,2,88,128]{3,2,1,0:T(8,128)(2,1)S(1)}, f32[2,88,2048]{2,1,0:T(8,128)S(1)}, f32[2,1,2048]{2,1,0:T(1,128)S(1)}) custom-call(s32[2,2]{1,0:T(2,128)S(1)} %broadcast_select_fusion.ext_ref, bf16[16,2,3,88,128]{4,3,2,1,0:T(8,128)(2,1)S(1)} %all-to-all-done.1.qkv_ref, f32[88,2048]{1,0:T(8,128)S(1)} %copy-done.7, ...), custom_call_target="tpu_custom_call" | custom-call | flops 8858370048 | bytes 6291456 | tf_op jit(solution)/shard_map/pallas_call | solution.py:353
  311.6 10.8 %all-to-all-done.2 = bf16[16,2,88,128]{3,2,1,0:T(8,128)(2,1)S(1)} async-done(((bf16[16,2,88,128]{3,2,1,0:T(8,128)(2,1)}), bf16[16,2,88,128]{3,2,1,0:T(8,128)(2,1)S(1)}, u32[]{:S(2)}, u32[]{:S(2)}) %all-to-all-start.2) | async-done | bytes 720928 | tf_op jit(solution)/shard_map/all_to_all | solution.py:914
  331.4 12.6 %shard_map.489 = (bf16[16,88,256]{2,1,0:T(8,128)(2,1)S(1)}, f32[16,1,256]{2,1,0:T(1,128)S(1)}) custom-call(s32[2,2]{1,0:T(2,128)S(1)} %copy-done.11, f32[16,88,256]{2,1,0:T(8,128)S(1)} %bitcast.325, bf16[2,16,88,768]{3,2,1,0:T(8,128)(2,1)S(1)} %bitcast.318, f32[88,256]{1,0:T(8,128)S(1)} %get-tuple-element.278.cos_ref, ...), custom_call_target="tpu_custom_call" | custom-call | flops 4294967296 | bytes 10485760 | tf_op jit(solution)/shard_map/pallas_call | solution.py:586
  353.4 54.5 %all-gather.8.cloned.1.call-done = bf16[1536,5888]{1,0:T(8,128)(2,1)} async-done(((bf16[96,5888]{1,0:T(8,128)(2,1)}), bf16[1536,5888]{1,0:T(8,128)(2,1)}) %all-gather.8.cloned.1.call-update) | async-done | bytes 18087952 | tf_op jit(solution)/shard_map/all_gather | solution.py:1049
  413.9 7.7 slice.662
  421.6 7.8 pad_maximum_fusion
  429.4 9.5 fusion.61
  438.9 12.1 %convert_reduce_fusion = (bf16[3072]{0:T(1024)(128)(2,1)S(1)}, bf16[2,2,128,3072]{3,2,1,0:T(8,128)(2,1)}) fusion(f32[2,2,128,3072]{3,2,1,0:T(8,128)} %fusion.61, f32[3072]{0:T(1024)S(1)} %add.485, bf16[3072,1408,1,1]{1,0,3,2:T(8,128)(2,1)S(1)} %bitcast.344, bf16[1,2,128,1408]{3,2,1,0:T(8,128)(2,1)} %collective-permute-done.10, ...), kind=kOutput, calls=%fused_computation.30 | convolution fusion | flops 4466078720 | bytes 19548160 | tf_op jit(solution)/shard_map/dot_general | solution.py:45
  461.1 8.3 fusion.121
  480.8 11.6 %collective-permute-done.5 = bf16[1,2,128,1408]{3,2,1,0:T(8,128)(2,1)} collective-permute-done((bf16[1,2,128,1408]{3,2,1,0:T(8,128)(2,1)}, bf16[1,2,128,1408]{3,2,1,0:T(8,128)(2,1)}, u32[]{:S(2)}, u32[]{:S(2)}) %collective-permute-start.5) | collective-permute-done | bytes 720928 | tf_op jit(solution)/shard_map/ppermute | solution.py:113
  500.6 15.4 %shard_map.490 = (bf16[16,88,256]{2,1,0:T(8,128)(2,1)S(1)}, bf16[2,16,88,768]{3,2,1,0:T(8,128)(2,1)S(1)}, f32[8,88,2]{2,1,0:T(8,128)S(1)}) custom-call(s32[2,2]{1,0:T(2,128)S(1)} %copy-done.11, f32[16,88,256]{2,1,0:T(8,128)S(1)} %bitcast.326, bf16[2,16,88,768]{3,2,1,0:T(8,128)(2,1)S(1)} %bitcast.321, bf16[16,88,256]{2,1,0:T(8,128)(2,1)S(1)} %bitcast.327, ...), custom_call_target="tpu_custom_call" | custom-call | flops 8589934592 | bytes 16777216 | tf_op jit(solution)/shard_map/pallas_call | solution.py:606
  535.1 10.4 %bitcast_convert_fusion.1 = bf16[1408,3072]{1,0:T(8,128)(2,1)} fusion(bf16[2,2,128,3072]{3,2,1,0:T(8,128)(2,1)} %get-tuple-element.292, bf16[1,2,128,1408]{3,2,1,0:T(8,128)(2,1)} %collective-permute-done.4, bf16[1,2,128,1408]{3,2,1,0:T(8,128)(2,1)} %copy-done.74), kind=kOutput, calls=%fused_computation.2 | convolution fusion | flops 4434231296 | bytes 13238272 | tf_op jit(solution)/shard_map/dot_general | solution.py:45
  545.5 8.1 pad.24.refs_1_
  554.9 26.3 %shard_map.491 = (bf16[16,2,3,88,128]{4,3,2,1,0:T(8,128)(2,1)}, f32[2,88,4]{2,1,0:T(8,128)}) custom-call(s32[2,2]{1,0:T(2,128)} %copy-done.10, bf16[16,2,3,88,128]{4,3,2,1,0:T(8,128)(2,1)} %copy-done.5, bf16[16,2,88,128]{3,2,1,0:T(8,128)(2,1)} %all-to-all-done.3.dout_ref, f32[2,88,2048]{2,1,0:T(8,128)} %copy-done.12, f32[2,1,2048]{2,1,0:T(1,128)} %copy-done.13, ...), custom_call_target="tpu_custom_call" | custom-call | flops 22145925120 | bytes 8388608 | tf_op jit(solution)/shard_map/pallas_call | solution.py:457
  586.2 11.2 %bitcast_convert_fusion = bf16[3072,1408]{1,0:T(8,128)(2,1)} fusion(bf16[1,2,128,1408]{3,2,1,0:T(8,128)(2,1)} %collective-permute-done.10, bf16[1,2,128,1408]{3,2,1,0:T(8,128)(2,1)} %copy-done.75, f32[2,2,128,3072]{3,2,1,0:T(8,128)} %fusion.61, f32[3072]{0:T(1024)S(1)} %copy-done.133), kind=kOutput, calls=%fused_computation.1 | convolution fusion | flops 4449959936 | bytes 16396288 | tf_op jit(solution)/shard_map/dot_general | solution.py:45
  638.9 7.4 fusion.123
  707.4 211.9 %shard_map.492 = (bf16[704,1408]{1,0:T(8,128)(2,1)}, bf16[2,96,3072]{2,1,0:T(8,128)(2,1)}, bf16[2,192,1408]{2,1,0:T(8,128)(2,1)}) custom-call(bf16[16,704,1408]{2,1,0:T(8,128)(2,1)} %constant_dynamic-update-slice_fusion.21.refs_0_, bf16[16,96,3072]{2,1,0:T(8,128)(2,1)} %pad.24.refs_1_, bf16[16,192,1408]{2,1,0:T(8,128)(2,1)} %bitcast.351), custom_call_target="tpu_custom_call" | custom-call | flops 268435456 | bytes 268435456 | tf_op jit(solution)/shard_map/pallas_call | solution.py:896
  (770 shorter events, 359.2 us)
Async XLA Ops:
  7.3 131.6 %all-gather.4.cloned.1.call-start = ((), (), s32[]{:S(2)}) async-start(), calls=%async_computation.7 | async-start | bytes 21063680 | tf_op jit(solution)/shard_map/all_gather | solution.py:966
  13.1 38.2 %all-to-all-start = ((bf16[16,240,128]{2,1,0:T(8,128)(2,1)}), bf16[16,240,128]{2,1,0:T(8,128)(2,1)S(1)}, u32[]{:S(2)}, u32[]{:S(2)}) async-start(bf16[16,240,128]{2,1,0:T(8,128)(2,1)} %broadcast_in_dim.186), calls=%async_computation | async-start | bytes 1966080 | tf_op jit(solution)/shard_map/all_to_all | solution.py:914
  20.5 286.0 %all-gather.6.cloned.1.call-start = ((), (), s32[]{:S(2)}) async-start(), calls=%async_computation.8 | async-start | bytes 17233920 | tf_op jit(solution)/shard_map/all_gather | solution.py:1039
  55.4 352.5 %all-gather.8.cloned.1.call-start = ((), (), s32[]{:S(2)}) async-start(), calls=%async_computation.9 | async-start | bytes 19218432 | tf_op jit(solution)/shard_map/all_gather | solution.py:1049
  74.2 7.8 collective-permute-start.3
  75.5 6.5 collective-permute-start.2
  170.8 106.9 %all-to-all-start.1 = ((bf16[16,2,3,88,128]{4,3,2,1,0:T(8,128)(2,1)}), bf16[16,2,3,88,128]{4,3,2,1,0:T(8,128)(2,1)S(1)}, u32[]{:S(2)}, u32[]{:S(2)}) async-start(bf16[16,2,3,88,128]{4,3,2,1,0:T(8,128)(2,1)} %bitcast.350), calls=%async_computation.1 | async-start | bytes 4325376 | tf_op jit(solution)/shard_map/all_to_all | solution.py:914
  297.0 25.4 %all-to-all-start.2 = ((bf16[16,2,88,128]{3,2,1,0:T(8,128)(2,1)}), bf16[16,2,88,128]{3,2,1,0:T(8,128)(2,1)S(1)}, u32[]{:S(2)}, u32[]{:S(2)}) async-start(bf16[16,2,88,128]{3,2,1,0:T(8,128)(2,1)} %copy-done.8), calls=%async_computation.2 | async-start | bytes 1441792 | tf_op jit(solution)/shard_map/all_to_all | solution.py:914
  304.6 134.3 %collective-permute-start.10 = (bf16[1,2,128,1408]{3,2,1,0:T(8,128)(2,1)S(1)}, bf16[1,2,128,1408]{3,2,1,0:T(8,128)(2,1)}, u32[]{:S(2)}, u32[]{:S(2)}) collective-permute-start(bf16[1,2,128,1408]{3,2,1,0:T(8,128)(2,1)S(1)} %convert_bitcast_fusion.1), channel_id=1, source_target_pairs={{0,16},{16,0},{1,17},{17,1},{2,18},{18,2},{3,19},{19,3},{4,20},{20... | collective-permute-start | bytes 2162696 | tf_op jit(solution)/shard_map/ppermute | solution.py:113
  351.1 78.3 %collective-permute-start.4 = (bf16[1,2,128,1408]{3,2,1,0:T(8,128)(2,1)S(1)}, bf16[1,2,128,1408]{3,2,1,0:T(8,128)(2,1)}, u32[]{:S(2)}, u32[]{:S(2)}) collective-permute-start(bf16[1,2,128,1408]{3,2,1,0:T(8,128)(2,1)S(1)} %fusion.62), channel_id=1, source_target_pairs={{0,16},{16,0},{1,17},{17,1},{2,18},{18,2},{3,19},{19,3},{4,20},{20... | collective-permute-start | bytes 2162696 | tf_op jit(solution)/shard_map/ppermute | solution.py:113
  459.2 19.5 %collective-permute-start.11 = (bf16[1,2,128,1408]{3,2,1,0:T(8,128)(2,1)}, bf16[1,2,128,1408]{3,2,1,0:T(8,128)(2,1)}, u32[]{:S(2)}, u32[]{:S(2)}) collective-permute-start(bf16[1,2,128,1408]{3,2,1,0:T(8,128)(2,1)} %slice.821), channel_id=1, source_target_pairs={{0,16},{16,0},{1,17},{17,1},{2,18},{18,2},{3,19},{19,3},{4,20},{20... | collective-permute-start | bytes 2162696 | tf_op jit(solution)/shard_map/ppermute | solution.py:113
  471.3 21.1 %collective-permute-start.5 = (bf16[1,2,128,1408]{3,2,1,0:T(8,128)(2,1)}, bf16[1,2,128,1408]{3,2,1,0:T(8,128)(2,1)}, u32[]{:S(2)}, u32[]{:S(2)}) collective-permute-start(bf16[1,2,128,1408]{3,2,1,0:T(8,128)(2,1)} %slice.822), channel_id=1, source_target_pairs={{0,16},{16,0},{1,17},{17,1},{2,18},{18,2},{3,19},{19,3},{4,20},{20... | collective-permute-start | bytes 2162696 | tf_op jit(solution)/shard_map/ppermute | solution.py:113
  529.5 25.4 %all-to-all-start.3 = ((bf16[16,2,88,128]{3,2,1,0:T(8,128)(2,1)}), bf16[16,2,88,128]{3,2,1,0:T(8,128)(2,1)}, u32[]{:S(2)}, u32[]{:S(2)}) async-start(bf16[16,2,88,128]{3,2,1,0:T(8,128)(2,1)} %bitcast.376), calls=%async_computation.3 | async-start | bytes 1441792 | tf_op jit(solution)/shard_map/all_to_all | solution.py:914
  581.3 55.8 %all-to-all-start.4 = ((bf16[16,2,3,88,128]{4,3,2,1,0:T(8,128)(2,1)}), bf16[16,2,3,88,128]{4,3,2,1,0:T(8,128)(2,1)}, u32[]{:S(2)}, u32[]{:S(2)}) async-start(bf16[16,2,3,88,128]{4,3,2,1,0:T(8,128)(2,1)} %get-tuple-element.46), calls=%async_computation.4 | async-start | bytes 4325376 | tf_op jit(solution)/shard_map/all_to_all | solution.py:914
  586.2 340.1 %reduce-scatter.2.cloned.1.call-start = ((), (), s32[]{:S(2)}) async-start(), calls=%async_computation.10 | async-start | bytes 4595712 | tf_op jit(solution)/shard_map/reduce_scatter | solution.py:141
  599.7 22.5 %collective-permute-start.7 = (f32[2,1,8,144]{3,2,1,0:T(8,128)S(1)}, f32[2,1,8,144]{3,2,1,0:T(8,128)S(1)}, u32[]{:S(2)}, u32[]{:S(2)}) collective-permute-start(f32[2,1,8,144]{3,2,1,0:T(8,128)S(1)} %get-tuple-element.241), channel_id=1, source_target_pairs={{4,0},{8,4},{12,8},{5,1},{9,5},{13,9},{6,2},{10,6},{14,10},{7,3},{... | collective-permute-start | bytes 27656 | tf_op jit(solution)/shard_map/ppermute | solution.py:39
  601.0 21.2 %collective-permute-start.6 = (f32[2,1,8,144]{3,2,1,0:T(8,128)S(1)}, f32[2,1,8,144]{3,2,1,0:T(8,128)S(1)}, u32[]{:S(2)}, u32[]{:S(2)}) collective-permute-start(f32[2,1,8,144]{3,2,1,0:T(8,128)S(1)} %get-tuple-element.240), channel_id=1, source_target_pairs={{0,4},{4,8},{8,12},{1,5},{5,9},{9,13},{2,6},{6,10},{10,14},{3,7},{... | collective-permute-start | bytes 27656 | tf_op jit(solution)/shard_map/ppermute | solution.py:36
  622.2 8.6 collective-permute-start.9
  659.5 291.9 %collective-permute-start.13 = (f32[2,1,8,144]{3,2,1,0:T(8,128)}, f32[2,1,8,144]{3,2,1,0:T(8,128)S(1)}, u32[]{:S(2)}, u32[]{:S(2)}) collective-permute-start(f32[2,1,8,144]{3,2,1,0:T(8,128)} %get-tuple-element.239), channel_id=1, source_target_pairs={{4,0},{8,4},{12,8},{5,1},{9,5},{13,9},{6,2},{10,6},{14,10},{7,3},{... | collective-permute-start | bytes 27656 | tf_op jit(solution)/shard_map/ppermute | solution.py:39
  660.8 290.6 %collective-permute-start.12 = (f32[2,1,8,144]{3,2,1,0:T(8,128)}, f32[2,1,8,144]{3,2,1,0:T(8,128)S(1)}, u32[]{:S(2)}, u32[]{:S(2)}) collective-permute-start(f32[2,1,8,144]{3,2,1,0:T(8,128)} %get-tuple-element.238), channel_id=1, source_target_pairs={{0,4},{4,8},{8,12},{1,5},{5,9},{9,13},{2,6},{6,10},{10,14},{3,7},{... | collective-permute-start | bytes 27656 | tf_op jit(solution)/shard_map/ppermute | solution.py:36
  930.8 32.9 %all-to-all-start.5 = ((bf16[16,240,128]{2,1,0:T(8,128)(2,1)}), bf16[16,240,128]{2,1,0:T(8,128)(2,1)}, u32[]{:S(2)}, u32[]{:S(2)}) async-start(bf16[16,240,128]{2,1,0:T(8,128)(2,1)} %bitcast.143), calls=%async_computation.6 | async-start | bytes 1966080 | tf_op jit(solution)/shard_map/all_to_all | solution.py:914
  951.0 11.8 %collective-permute-start.18 = (bf16[1024,176]{0,1:T(8,128)(2,1)S(1)}, bf16[1024,176]{0,1:T(8,128)(2,1)S(1)}, u32[]{:S(2)}, u32[]{:S(2)}) collective-permute-start(bf16[1024,176]{0,1:T(8,128)(2,1)S(1)} %fusion.56), channel_id=1, source_target_pairs={{0,16},{16,0},{1,17},{17,1},{2,18},{18,2},{3,19},{19,3},{4,20},{20... | collective-permute-start | bytes 1081352 | tf_op jit(solution)/shard_map/ppermute | solution.py:113
  951.5 6.7 collective-permute-start.15
  967.9 12.6 %collective-permute-start.17 = (f32[88,1408]{1,0:T(8,128)S(1)}, f32[88,1408]{1,0:T(8,128)S(1)}, u32[]{:S(2)}, u32[]{:S(2)}) collective-permute-start(f32[88,1408]{1,0:T(8,128)S(1)} %fusion.117), channel_id=1, source_target_pairs={{0,16},{16,0},{1,17},{17,1},{2,18},{18,2},{3,19},{19,3},{4,20},{20... | collective-permute-start | bytes 1486856 | tf_op jit(solution)/shard_map/ppermute | solution.py:113
  (192 other events, 2721.9 us)
Sparse Core Ops, SparseCore 0:
  11.0 127.8 all-gather.3
  141.7 164.2 all-gather.5
  307.5 100.2 all-gather.7
  611.3 75.0 reduce-scatter.1

commit v5 on v4

--- a/solution.py
+++ b/solution.py
@@ -1036,16 +1036,26 @@
     text_part = text_part + cross_bias.astype(F32)[:, None]
     text_normed, text_pull = jax.vjp(text_norm, text_part, head_gains[3], head_offsets[3])
     moves = Moves()
+    even_group = group_index % 2 == 0
     second_all = lax.all_gather(
         jnp.concatenate(
-            [out_weight, cross_query, cross_out, beside(text_normed.astype(BF), 2)], axis=1
+            [
+                out_weight,
+                lax.select(jnp.broadcast_to(even_group, cross_out.shape), cross_query, cross_out),
+                beside(text_normed.astype(BF), 2),
+            ],
+            axis=1,
         ),
         GROUP,
         axis=0,
         tiled=True,
     )
-    out_full, cross_q_full, cross_o_full = [second_all[:, i * D : (i + 1) * D] for i in range(3)]
-    text_both = below(second_all[:, 3 * D :], 2).reshape(2, HEADS, HD, img_count * text_count)
+    out_full, cross_mine = second_all[:, :D], second_all[:, D : 2 * D]
+    cross_other = exchange(cross_mine, "img", 1)
+    choose = jnp.broadcast_to(even_group, cross_mine.shape)
+    cross_q_full = lax.select(choose, cross_mine, cross_other)
+    cross_o_full = lax.select(choose, cross_other, cross_mine)
+    text_both = below(second_all[:, 2 * D :], 2).reshape(2, HEADS, HD, img_count * text_count)
     third_all = lax.all_gather(third, GROUP, axis=0, tiled=True)
     third_rows = third_all.reshape(count, fold_rows, -1)
     up_full = third_rows[:, :shard, : count * hid_part].reshape(D, count * hid_part)
@@ -1190,24 +1200,6 @@
 
     moves.finish(*list(moves.running))
     shards = moves.done
-    names = ("query", "key", "value", "skip", "out", "cross_q", "cross_o")
-    packed = [whole_grads[name].astype(BF).reshape(count, -1, D) for name in names]
-    packed_rows = sum(part.shape[1] for part in packed)
-    fill = -packed_rows % (16 * groups)
-    packed = jnp.pad(jnp.concatenate(packed, axis=1), ((0, 0), (0, fill), (0, 0)))
-    up_rows = jnp.pad(
-        whole_up.astype(BF).reshape(count, shard, -1), ((0, 0), (0, -shard % 16), (0, 0))
-    )
-    down_rows = whole_down.astype(BF).reshape(count, hid_part, D)
-    summed, up_sums, down_sums = sum_everywhere(
-        packed, down_rows, up_rows, (groups, row_count, col_count)
-    )
-    summed = summed.astype(F32)
-    total_of, at = {}, 0
-    for name in names:
-        rows = whole_grads[name].shape[0] // count
-        total_of[name] = summed[at : at + rows]
-        at += rows
     grad_text_lin, head_gain_ck_grad, head_shift_ck_grad = text_pull(shards["text"])
     grad_text_low = grad_text_lin.astype(BF)
     grad_cross_keys = images_sum(
@@ -1264,8 +1256,27 @@
     shift_share = jnp.broadcast_to(grad_shift_rows.reshape(1, -1), (count, img_count * D))
     small_grads = jnp.concatenate([small_grads, shift_share], axis=1).astype(BF)
     small_grads = jnp.pad(small_grads, ((0, 0), (0, padded_len - small_grads.shape[1])))
-    small_got = all_to_all(small_grads.reshape(count, -1, 128)).astype(F32)
-    small_got = jnp.sum(small_got, axis=0).reshape(-1)
+    small_got = all_to_all(small_grads.reshape(count, -1, 128))
+    names = ("query", "key", "value", "skip", "out", "cross_q", "cross_o")
+    packed = [whole_grads[name].astype(BF).reshape(count, -1, D) for name in names]
+    packed_rows = sum(part.shape[1] for part in packed)
+    fill = -packed_rows % (16 * groups)
+    packed = jnp.pad(jnp.concatenate(packed, axis=1), ((0, 0), (0, fill), (0, 0)))
+    up_rows = jnp.pad(
+        whole_up.astype(BF).reshape(count, shard, -1), ((0, 0), (0, -shard % 16), (0, 0))
+    )
+    down_rows = whole_down.astype(BF).reshape(count, hid_part, D)
+    packed, small_got = lax.optimization_barrier((packed, small_got))
+    summed, up_sums, down_sums = sum_everywhere(
+        packed, down_rows, up_rows, (groups, row_count, col_count)
+    )
+    summed = summed.astype(F32)
+    total_of, at = {}, 0
+    for name in names:
+        rows = whole_grads[name].shape[0] // count
+        total_of[name] = summed[at : at + rows]
+        at += rows
+    small_got = jnp.sum(small_got.astype(F32), axis=0).reshape(-1)
     small_sum = images_sum(small_got[:small_len], F32)
     total_parts = cuts(small_sum, (wide, wide) + small_widths)
     grad_shift = lax.dot_general(

time: 1000 us -> 994 us (level)
    all_gather x1, waiting for transfers between devices: 0.01 us -> 79.9 us  [body(): lax.all_gather(jnp.concatenate([out_weight, lax.select(jnp.broadcast_to(e...]
    all_to_all x6, waiting for transfers between devices: 113 us -> 52.3 us  [all_to_all(): lax.all_to_all(values, GROUP, split_axis=0, concat_axis=0, tiled=True)]
    all_gather x1, waiting for transfers between devices: 54.5 us -> 0.01 us  [body(): third_all = lax.all_gather(third, GROUP, axis=0, tiled=True)]
    ppermute x0 -> x1, waiting for transfers between devices: none -> 35.2 us  [exchange(): return lax.ppermute(values, axis, [(i, i ^ bit) for i in range(size)])]
    unnamed x409 -> x399, local copies, waits for them, and re-layouts: 52.9 us -> 48.3 us
  transfers between devices with their start and end apart: 30 -> 31, of which waited for: 13 -> 13; matrix products, arithmetic and copies ran while one was open for 32% -> 32% of each run, Pallas kernels for 24% -> 3%
where the time goes in v5:
time: 994 us; the launch traced here: 978 us
  Pallas kernels  279 us (28%)
  waiting for transfers between devices  228 us (23%)
  local copies, waits for them, and re-layouts  174 us (18%)
  matrix products  142 us (14%)
  starting transfers between devices  73.8 us (7%)
  other arithmetic  63.7 us (6%)
  between operations  17.3 us (2%)
    pallas_call x1, Pallas kernels, sum_everywhere(): pl.pallas_call(functools.partial(sum_kernel, sizes, kinds), out_shape=[ja...  209 us
    dot_general x32, matrix products, dot(): lax.dot_general(former, latter, ((former_dims, latter_dims), ((), ())), p...  140 us
    all_gather x1, waiting for transfers between devices, body(): lax.all_gather(jnp.concatenate([out_weight, lax.select(jnp.broadcast_to(e...  79.9 us
    all_to_all x6, waiting for transfers between devices, all_to_all(): lax.all_to_all(values, GROUP, split_axis=0, concat_axis=0, tiled=True)  52.3 us
    unnamed x399, local copies, waits for them, and re-layouts  48.3 us
    all_gather x1, waiting for transfers between devices, body(): lax.all_gather(jnp.concatenate([beside(skip_weight, 2), qkv_weight], axis...  40.4 us
    ppermute x1, waiting for transfers between devices, exchange(): return lax.ppermute(values, axis, [(i, i ^ bit) for i in range(size)])  35.2 us
    all_to_all x6, starting transfers between devices, all_to_all(): lax.all_to_all(values, GROUP, split_axis=0, concat_axis=0, tiled=True)  34.4 us
  transfers between devices with their start and end apart: 31, of which 13 were waited for; matrix products, arithmetic and copies ran while one was open for 32% of the time, Pallas kernels for 3%

profile of v5, /device:TPU:0, one launch (start us, length us, event | category | flops | bytes accessed | tf_op | source)
XLA Modules:
  0.0 978.2 jit_solution(4979690972179692720)
XLA Ops:
  13.1 7.4 all-to-all-start
  26.1 25.2 %all-to-all-done = bf16[16,240,128]{2,1,0:T(8,128)(2,1)S(1)} async-done(((bf16[16,240,128]{2,1,0:T(8,128)(2,1)}), bf16[16,240,128]{2,1,0:T(8,128)(2,1)S(1)}, u32[]{:S(2)}, u32[]{:S(2)}) %all-to-all-start) | async-done | bytes 983072 | tf_op jit(solution)/shard_map/all_to_all | solution.py:914
  98.5 40.4 %all-gather.4.cloned.1.call-done = bf16[1408,7040]{1,0:T(8,128)(2,1)} async-done(((bf16[88,7040]{1,0:T(8,128)(2,1)}), bf16[1408,7040]{1,0:T(8,128)(2,1)}) %all-gather.4.cloned.1.call-update) | async-done | bytes 19824656 | tf_op jit(solution)/shard_map/all_gather | solution.py:966
  160.9 8.1 fusion.7
  170.6 8.9 all-to-all-start.1
  201.3 79.9 %all-gather.6.cloned.1.call-done = bf16[1408,4352]{1,0:T(8,128)(2,1)} async-done(((bf16[88,4352]{1,0:T(8,128)(2,1)}), bf16[1408,4352]{1,0:T(8,128)(2,1)}) %all-gather.6.cloned.1.call-update) | async-done | bytes 12255248 | tf_op jit(solution)/shard_map/all_gather | solution.py:1040
  288.9 15.6 %shard_map.488 = (bf16[16,2,88,128]{3,2,1,0:T(8,128)(2,1)S(1)}, f32[2,88,2048]{2,1,0:T(8,128)S(1)}, f32[2,1,2048]{2,1,0:T(1,128)S(1)}) custom-call(s32[2,2]{1,0:T(2,128)S(1)} %broadcast_select_fusion.7.ext_ref, bf16[16,2,3,88,128]{4,3,2,1,0:T(8,128)(2,1)S(1)} %all-to-all-done.1.qkv_ref, f32[88,2048]{1,0:T(8,128)S(1)} %copy-done.7, ...), custom_call_target="tpu_custom_call" | custom-call | flops 8858370048 | bytes 6291456 | tf_op jit(solution)/shard_map/pallas_call | solution.py:353
  319.6 14.9 %all-to-all-done.2 = bf16[16,2,88,128]{3,2,1,0:T(8,128)(2,1)S(1)} async-done(((bf16[16,2,88,128]{3,2,1,0:T(8,128)(2,1)}), bf16[16,2,88,128]{3,2,1,0:T(8,128)(2,1)S(1)}, u32[]{:S(2)}, u32[]{:S(2)}) %all-to-all-start.2) | async-done | bytes 720928 | tf_op jit(solution)/shard_map/all_to_all | solution.py:914
  339.3 35.2 %collective-permute-done.4 = bf16[1408,1408]{1,0:T(8,128)(2,1)} collective-permute-done((bf16[1408,1408]{1,0:T(8,128)(2,1)}, bf16[1408,1408]{1,0:T(8,128)(2,1)}, u32[]{:S(2)}, u32[]{:S(2)}) %collective-permute-start.4) | collective-permute-done | bytes 3964960 | tf_op jit(solution)/shard_map/ppermute | solution.py:143
  378.2 12.6 %shard_map.489 = (bf16[16,88,256]{2,1,0:T(8,128)(2,1)S(1)}, f32[16,1,256]{2,1,0:T(1,128)S(1)}) custom-call(s32[2,2]{1,0:T(2,128)S(1)} %copy-done.11, f32[16,88,256]{2,1,0:T(8,128)S(1)} %bitcast.325, bf16[2,16,88,768]{3,2,1,0:T(8,128)(2,1)S(1)} %bitcast.318, f32[88,256]{1,0:T(8,128)S(1)} %get-tuple-element.284.cos_ref, ...), custom_call_target="tpu_custom_call" | custom-call | flops 4294967296 | bytes 10485760 | tf_op jit(solution)/shard_map/pallas_call | solution.py:586
  406.6 7.7 slice.657
  414.3 7.8 pad_maximum_fusion
  422.1 9.4 fusion.49
  431.6 12.1 %convert_reduce_fusion = (bf16[3072]{0:T(1024)(128)(2,1)S(1)}, bf16[2,2,128,3072]{3,2,1,0:T(8,128)(2,1)}) fusion(f32[2,2,128,3072]{3,2,1,0:T(8,128)} %fusion.49, f32[3072]{0:T(1024)S(1)} %add.490, bf16[3072,1408,1,1]{1,0,3,2:T(8,128)(2,1)S(1)} %bitcast.346, bf16[1,2,128,1408]{3,2,1,0:T(8,128)(2,1)} %collective-permute-done.11, ...), kind=kOutput, calls=%fused_computation.30 | convolution fusion | flops 4466078720 | bytes 19548160 | tf_op jit(solution)/shard_map/dot_general | solution.py:45
  452.4 8.3 fusion.113
  473.5 10.8 %collective-permute-done.6 = bf16[1,2,128,1408]{3,2,1,0:T(8,128)(2,1)} collective-permute-done((bf16[1,2,128,1408]{3,2,1,0:T(8,128)(2,1)}, bf16[1,2,128,1408]{3,2,1,0:T(8,128)(2,1)}, u32[]{:S(2)}, u32[]{:S(2)}) %collective-permute-start.6) | collective-permute-done | bytes 720928 | tf_op jit(solution)/shard_map/ppermute | solution.py:113
  493.8 15.4 %shard_map.490 = (bf16[16,88,256]{2,1,0:T(8,128)(2,1)S(1)}, bf16[2,16,88,768]{3,2,1,0:T(8,128)(2,1)S(1)}, f32[8,88,2]{2,1,0:T(8,128)S(1)}) custom-call(s32[2,2]{1,0:T(2,128)S(1)} %copy-done.11, f32[16,88,256]{2,1,0:T(8,128)S(1)} %bitcast.326, bf16[2,16,88,768]{3,2,1,0:T(8,128)(2,1)S(1)} %bitcast.321, bf16[16,88,256]{2,1,0:T(8,128)(2,1)S(1)} %bitcast.327, ...), custom_call_target="tpu_custom_call" | custom-call | flops 8589934592 | bytes 16777216 | tf_op jit(solution)/shard_map/pallas_call | solution.py:606
  525.5 10.4 %bitcast_convert_fusion.1 = bf16[1408,3072]{1,0:T(8,128)(2,1)} fusion(bf16[2,2,128,3072]{3,2,1,0:T(8,128)(2,1)} %get-tuple-element.298, bf16[1,2,128,1408]{3,2,1,0:T(8,128)(2,1)} %collective-permute-done.5, bf16[1,2,128,1408]{3,2,1,0:T(8,128)(2,1)} %copy-done.76), kind=kOutput, calls=%fused_computation.2 | convolution fusion | flops 4434231296 | bytes 13238272 | tf_op jit(solution)/shard_map/dot_general | solution.py:45
  535.9 8.1 pad.24.refs_1_
  545.2 26.3 %shard_map.491 = (bf16[16,2,3,88,128]{4,3,2,1,0:T(8,128)(2,1)}, f32[2,88,4]{2,1,0:T(8,128)}) custom-call(s32[2,2]{1,0:T(2,128)} %copy-done.10, bf16[16,2,3,88,128]{4,3,2,1,0:T(8,128)(2,1)} %copy-done.5, bf16[16,2,88,128]{3,2,1,0:T(8,128)(2,1)} %all-to-all-done.3.dout_ref, f32[2,88,2048]{2,1,0:T(8,128)} %copy-done.12, f32[2,1,2048]{2,1,0:T(1,128)} %copy-done.13, ...), custom_call_target="tpu_custom_call" | custom-call | flops 22145925120 | bytes 8388608 | tf_op jit(solution)/shard_map/pallas_call | solution.py:457
  576.6 11.3 %bitcast_convert_fusion = bf16[3072,1408]{1,0:T(8,128)(2,1)} fusion(bf16[1,2,128,1408]{3,2,1,0:T(8,128)(2,1)} %collective-permute-done.11, bf16[1,2,128,1408]{3,2,1,0:T(8,128)(2,1)} %copy-done.77, f32[2,2,128,3072]{3,2,1,0:T(8,128)} %fusion.49, f32[3072]{0:T(1024)S(1)} %copy-done.133), kind=kOutput, calls=%fused_computation.1 | convolution fusion | flops 4449959936 | bytes 16396288 | tf_op jit(solution)/shard_map/dot_general | solution.py:45
  629.4 7.4 fusion.115
  682.1 7.1 constant_dynamic-update-slice_fusion.21
  730.1 209.1 %shard_map.492 = (bf16[704,1408]{1,0:T(8,128)(2,1)}, bf16[2,96,3072]{2,1,0:T(8,128)(2,1)}, bf16[2,192,1408]{2,1,0:T(8,128)(2,1)}) custom-call(bf16[16,704,1408]{2,1,0:T(8,128)(2,1)} %constant_dynamic-update-slice_fusion.18.refs_0_, bf16[16,96,3072]{2,1,0:T(8,128)(2,1)} %pad.24.refs_1_, bf16[16,192,1408]{2,1,0:T(8,128)(2,1)} %bitcast.353), custom_call_target="tpu_custom_call" | custom-call | flops 268435456 | bytes 268435456 | tf_op jit(solution)/shard_map/pallas_call | solution.py:896
  (766 shorter events, 361.2 us)
Async XLA Ops:
  7.3 131.6 %all-gather.4.cloned.1.call-start = ((), (), s32[]{:S(2)}) async-start(), calls=%async_computation.7 | async-start | bytes 21063680 | tf_op jit(solution)/shard_map/all_gather | solution.py:966
  13.1 38.2 %all-to-all-start = ((bf16[16,240,128]{2,1,0:T(8,128)(2,1)}), bf16[16,240,128]{2,1,0:T(8,128)(2,1)S(1)}, u32[]{:S(2)}, u32[]{:S(2)}) async-start(bf16[16,240,128]{2,1,0:T(8,128)(2,1)} %broadcast_in_dim.192), calls=%async_computation | async-start | bytes 1966080 | tf_op jit(solution)/shard_map/all_to_all | solution.py:914
  20.5 260.8 %all-gather.6.cloned.1.call-start = ((), (), s32[]{:S(2)}) async-start(), calls=%async_computation.8 | async-start | bytes 13021184 | tf_op jit(solution)/shard_map/all_gather | solution.py:1040
  56.4 344.2 %all-gather.8.cloned.1.call-start = ((), (), s32[]{:S(2)}) async-start(), calls=%async_computation.9 | async-start | bytes 19218432 | tf_op jit(solution)/shard_map/all_gather | solution.py:1059
  72.4 7.9 collective-permute-start.3
  170.6 116.6 %all-to-all-start.1 = ((bf16[16,2,3,88,128]{4,3,2,1,0:T(8,128)(2,1)}), bf16[16,2,3,88,128]{4,3,2,1,0:T(8,128)(2,1)S(1)}, u32[]{:S(2)}, u32[]{:S(2)}) async-start(bf16[16,2,3,88,128]{4,3,2,1,0:T(8,128)(2,1)} %bitcast.352), calls=%async_computation.1 | async-start | bytes 4325376 | tf_op jit(solution)/shard_map/all_to_all | solution.py:914
  285.7 88.8 %collective-permute-start.4 = (bf16[1408,1408]{1,0:T(8,128)(2,1)}, bf16[1408,1408]{1,0:T(8,128)(2,1)}, u32[]{:S(2)}, u32[]{:S(2)}) collective-permute-start(bf16[1408,1408]{1,0:T(8,128)(2,1)} %slice.646), channel_id=1, source_target_pairs={{0,16},{16,0},{1,17},{17,1},{2,18},{18,2},{3,19},{19,3},{4,20},{20... | collective-permute-start | bytes 11894792 | tf_op jit(solution)/shard_map/ppermute | solution.py:143
  306.6 28.0 %all-to-all-start.2 = ((bf16[16,2,88,128]{3,2,1,0:T(8,128)(2,1)}), bf16[16,2,88,128]{3,2,1,0:T(8,128)(2,1)S(1)}, u32[]{:S(2)}, u32[]{:S(2)}) async-start(bf16[16,2,88,128]{3,2,1,0:T(8,128)(2,1)} %copy-done.8), calls=%async_computation.2 | async-start | bytes 1441792 | tf_op jit(solution)/shard_map/all_to_all | solution.py:914
  314.1 117.5 %collective-permute-start.11 = (bf16[1,2,128,1408]{3,2,1,0:T(8,128)(2,1)S(1)}, bf16[1,2,128,1408]{3,2,1,0:T(8,128)(2,1)}, u32[]{:S(2)}, u32[]{:S(2)}) collective-permute-start(bf16[1,2,128,1408]{3,2,1,0:T(8,128)(2,1)S(1)} %convert_bitcast_fusion.1), channel_id=1, source_target_pairs={{0,16},{16,0},{1,17},{17,1},{2,18},{18,2},{3,19},{19,3},{4,20},{20... | collective-permute-start | bytes 2162696 | tf_op jit(solution)/shard_map/ppermute | solution.py:113
  399.0 23.1 %collective-permute-start.5 = (bf16[1,2,128,1408]{3,2,1,0:T(8,128)(2,1)S(1)}, bf16[1,2,128,1408]{3,2,1,0:T(8,128)(2,1)}, u32[]{:S(2)}, u32[]{:S(2)}) collective-permute-start(bf16[1,2,128,1408]{3,2,1,0:T(8,128)(2,1)S(1)} %fusion.50), channel_id=1, source_target_pairs={{0,16},{16,0},{1,17},{17,1},{2,18},{18,2},{3,19},{19,3},{4,20},{20... | collective-permute-start | bytes 2162696 | tf_op jit(solution)/shard_map/ppermute | solution.py:113
  452.0 19.5 %collective-permute-start.12 = (bf16[1,2,128,1408]{3,2,1,0:T(8,128)(2,1)}, bf16[1,2,128,1408]{3,2,1,0:T(8,128)(2,1)}, u32[]{:S(2)}, u32[]{:S(2)}) collective-permute-start(bf16[1,2,128,1408]{3,2,1,0:T(8,128)(2,1)} %slice.814), channel_id=1, source_target_pairs={{0,16},{16,0},{1,17},{17,1},{2,18},{18,2},{3,19},{19,3},{4,20},{20... | collective-permute-start | bytes 2162696 | tf_op jit(solution)/shard_map/ppermute | solution.py:113
  462.5 21.8 %collective-permute-start.6 = (bf16[1,2,128,1408]{3,2,1,0:T(8,128)(2,1)}, bf16[1,2,128,1408]{3,2,1,0:T(8,128)(2,1)}, u32[]{:S(2)}, u32[]{:S(2)}) collective-permute-start(bf16[1,2,128,1408]{3,2,1,0:T(8,128)(2,1)} %slice.815), channel_id=1, source_target_pairs={{0,16},{16,0},{1,17},{17,1},{2,18},{18,2},{3,19},{19,3},{4,20},{20... | collective-permute-start | bytes 2162696 | tf_op jit(solution)/shard_map/ppermute | solution.py:113
  520.8 24.4 %all-to-all-start.3 = ((bf16[16,2,88,128]{3,2,1,0:T(8,128)(2,1)}), bf16[16,2,88,128]{3,2,1,0:T(8,128)(2,1)}, u32[]{:S(2)}, u32[]{:S(2)}) async-start(bf16[16,2,88,128]{3,2,1,0:T(8,128)(2,1)} %bitcast.378), calls=%async_computation.3 | async-start | bytes 1441792 | tf_op jit(solution)/shard_map/all_to_all | solution.py:914
  571.6 55.8 %all-to-all-start.4 = ((bf16[16,2,3,88,128]{4,3,2,1,0:T(8,128)(2,1)}), bf16[16,2,3,88,128]{4,3,2,1,0:T(8,128)(2,1)}, u32[]{:S(2)}, u32[]{:S(2)}) async-start(bf16[16,2,3,88,128]{4,3,2,1,0:T(8,128)(2,1)} %get-tuple-element.48), calls=%async_computation.4 | async-start | bytes 4325376 | tf_op jit(solution)/shard_map/all_to_all | solution.py:914
  576.5 118.6 %reduce-scatter.2.cloned.1.call-start = ((), (), s32[]{:S(2)}) async-start(), calls=%async_computation.10 | async-start | bytes 4595712 | tf_op jit(solution)/shard_map/reduce_scatter | solution.py:141
  588.5 20.6 %collective-permute-start.8 = (f32[2,1,8,144]{3,2,1,0:T(8,128)S(1)}, f32[2,1,8,144]{3,2,1,0:T(8,128)S(1)}, u32[]{:S(2)}, u32[]{:S(2)}) collective-permute-start(f32[2,1,8,144]{3,2,1,0:T(8,128)S(1)} %get-tuple-element.247), channel_id=1, source_target_pairs={{4,0},{8,4},{12,8},{5,1},{9,5},{13,9},{6,2},{10,6},{14,10},{7,3},{... | collective-permute-start | bytes 27656 | tf_op jit(solution)/shard_map/ppermute | solution.py:39
  589.8 19.3 %collective-permute-start.7 = (f32[2,1,8,144]{3,2,1,0:T(8,128)S(1)}, f32[2,1,8,144]{3,2,1,0:T(8,128)S(1)}, u32[]{:S(2)}, u32[]{:S(2)}) collective-permute-start(f32[2,1,8,144]{3,2,1,0:T(8,128)S(1)} %get-tuple-element.246), channel_id=1, source_target_pairs={{0,4},{4,8},{8,12},{1,5},{5,9},{9,13},{2,6},{6,10},{10,14},{3,7},{... | collective-permute-start | bytes 27656 | tf_op jit(solution)/shard_map/ppermute | solution.py:36
  649.3 62.5 %collective-permute-start.14 = (f32[2,1,8,144]{3,2,1,0:T(8,128)S(1)}, f32[2,1,8,144]{3,2,1,0:T(8,128)S(1)}, u32[]{:S(2)}, u32[]{:S(2)}) collective-permute-start(f32[2,1,8,144]{3,2,1,0:T(8,128)S(1)} %get-tuple-element.245), channel_id=1, source_target_pairs={{4,0},{8,4},{12,8},{5,1},{9,5},{13,9},{6,2},{10,6},{14,10},{7,3},{... | collective-permute-start | bytes 27656 | tf_op jit(solution)/shard_map/ppermute | solution.py:39
  650.6 61.2 %collective-permute-start.13 = (f32[2,1,8,144]{3,2,1,0:T(8,128)S(1)}, f32[2,1,8,144]{3,2,1,0:T(8,128)S(1)}, u32[]{:S(2)}, u32[]{:S(2)}) collective-permute-start(f32[2,1,8,144]{3,2,1,0:T(8,128)S(1)} %get-tuple-element.244), channel_id=1, source_target_pairs={{0,4},{4,8},{8,12},{1,5},{5,9},{9,13},{2,6},{6,10},{10,14},{3,7},{... | collective-permute-start | bytes 27656 | tf_op jit(solution)/shard_map/ppermute | solution.py:36
  699.6 30.2 %all-to-all-start.5 = ((bf16[16,240,128]{2,1,0:T(8,128)(2,1)}), bf16[16,240,128]{2,1,0:T(8,128)(2,1)S(1)}, u32[]{:S(2)}, u32[]{:S(2)}) async-start(bf16[16,240,128]{2,1,0:T(8,128)(2,1)} %bitcast.143), calls=%async_computation.6 | async-start | bytes 1966080 | tf_op jit(solution)/shard_map/all_to_all | solution.py:914
  711.2 13.3 %collective-permute-start.19 = (bf16[1024,176]{0,1:T(8,128)(2,1)S(1)}, bf16[1024,176]{0,1:T(8,128)(2,1)S(1)}, u32[]{:S(2)}, u32[]{:S(2)}) collective-permute-start(bf16[1024,176]{0,1:T(8,128)(2,1)S(1)} %fusion.44), channel_id=1, source_target_pairs={{0,16},{16,0},{1,17},{17,1},{2,18},{18,2},{3,19},{19,3},{4,20},{20... | collective-permute-start | bytes 1081352 | tf_op jit(solution)/shard_map/ppermute | solution.py:113
  711.9 10.1 %collective-permute-start.16 = (f32[2,18,1,144]{3,2,1,0:T(1,128)S(1)}, f32[2,18,1,144]{3,2,1,0:T(1,128)S(1)}, u32[]{:S(2)}, u32[]{:S(2)}) collective-permute-start(f32[2,18,1,144]{3,2,1,0:T(1,128)S(1)} %get-tuple-element.230), channel_id=1, source_target_pairs={{0,1},{1,2},{2,3},{4,5},{5,6},{6,7},{8,9},{9,10},{10,11},{12,13},{... | collective-permute-start | bytes 62216 | tf_op jit(solution)/shard_map/ppermute | solution.py:36
  942.5 20.2 %collective-permute-start.17 = (f32[27532]{0:T(1024)S(1)}, f32[27532]{0:T(1024)}, u32[]{:S(2)}, u32[]{:S(2)}) collective-permute-start(f32[27532]{0:T(1024)S(1)} %slice.693), channel_id=1, source_target_pairs={{0,16},{16,0},{1,17},{17,1},{2,18},{18,2},{3,19},{19,3},{4,20},{20... | collective-permute-start | bytes 330392 | tf_op jit(solution)/shard_map/ppermute | solution.py:113
  945.7 23.5 %collective-permute-start.18 = (f32[88,1408]{1,0:T(8,128)}, f32[88,1408]{1,0:T(8,128)}, u32[]{:S(2)}, u32[]{:S(2)}) collective-permute-start(f32[88,1408]{1,0:T(8,128)} %fusion.105), channel_id=1, source_target_pairs={{0,16},{16,0},{1,17},{17,1},{2,18},{18,2},{3,19},{19,3},{4,20},{20... | collective-permute-start | bytes 1486856 | tf_op jit(solution)/shard_map/ppermute | solution.py:113
  (190 other events, 2594.7 us)
Sparse Core Ops, SparseCore 0:
  11.0 127.8 all-gather.3
  141.7 139.5 all-gather.5
  282.8 110.8 all-gather.7
  609.2 74.1 reduce-scatter.1

commit v6 on v5

--- a/solution.py
+++ b/solution.py
@@ -1184,7 +1184,6 @@
     grad_from_self, gain_self_grad, shift_self_grad = self_norm_pull(grad_normed)
     grad_resid_in = grad_resid_self + grad_from_self
     grad_merged = grad_resid_in.astype(BF)
-    whole_grads["skip"] = weight_grad(skip_in, grad_merged)
     bias_skip_grad = column_sum(grad_merged)
     grad_skip_normed = matmul_back(grad_merged, skip_full)
     grad_joined, skip_gain_grad, skip_shift_grad = skip_norm_pull(grad_skip_normed)
@@ -1256,6 +1255,8 @@
     shift_share = jnp.broadcast_to(grad_shift_rows.reshape(1, -1), (count, img_count * D))
     small_grads = jnp.concatenate([small_grads, shift_share], axis=1).astype(BF)
     small_grads = jnp.pad(small_grads, ((0, 0), (0, padded_len - small_grads.shape[1])))
+    skip_late, small_grads = lax.optimization_barrier((skip_in, small_grads))
+    whole_grads["skip"] = weight_grad(skip_late, grad_merged)
     small_got = all_to_all(small_grads.reshape(count, -1, 128))
     names = ("query", "key", "value", "skip", "out", "cross_q", "cross_o")
     packed = [whole_grads[name].astype(BF).reshape(count, -1, D) for name in names]

time: 994 us -> 995 us (level)
    unnamed x399 -> x410, local copies, waits for them, and re-layouts: 48.3 us -> 50.4 us
  transfers between devices with their start and end apart: 31 -> 31, of which waited for: 13 -> 13; matrix products, arithmetic and copies ran while one was open for 32% -> 31% of each run, Pallas kernels for 3% -> 3%
where the time goes in v6:
time: 995 us; the launch traced here: 982 us
  Pallas kernels  277 us (28%)
  waiting for transfers between devices  226 us (23%)
  local copies, waits for them, and re-layouts  177 us (18%)
  matrix products  143 us (14%)
  starting transfers between devices  78.9 us (8%)
  other arithmetic  62.3 us (6%)
  between operations  17.5 us (2%)
    pallas_call x1, Pallas kernels, sum_everywhere(): pl.pallas_call(functools.partial(sum_kernel, sizes, kinds), out_shape=[ja...  207 us
    dot_general x32, matrix products, dot(): lax.dot_general(former, latter, ((former_dims, latter_dims), ((), ())), p...  141 us
    all_gather x1, waiting for transfers between devices, body(): lax.all_gather(jnp.concatenate([out_weight, lax.select(jnp.broadcast_to(e...  79.3 us
    all_to_all x6, waiting for transfers between devices, all_to_all(): lax.all_to_all(values, GROUP, split_axis=0, concat_axis=0, tiled=True)  56.3 us
    unnamed x410, local copies, waits for them, and re-layouts  50.4 us
    all_gather x1, waiting for transfers between devices, body(): lax.all_gather(jnp.concatenate([beside(skip_weight, 2), qkv_weight], axis...  39.1 us
    ppermute x1, waiting for transfers between devices, exchange(): return lax.ppermute(values, axis, [(i, i ^ bit) for i in range(size)])  35.2 us
    all_to_all x6, starting transfers between devices, all_to_all(): lax.all_to_all(values, GROUP, split_axis=0, concat_axis=0, tiled=True)  32.9 us
  transfers between devices with their start and end apart: 31, of which 13 were waited for; matrix products, arithmetic and copies ran while one was open for 31% of the time, Pallas kernels for 3%

profile of v6, /device:TPU:0, one launch (start us, length us, event | category | flops | bytes accessed | tf_op | source)
XLA Modules:
  0.0 981.7 jit_solution(3862433926585462077)
XLA Ops:
  25.5 25.9 %all-to-all-done = bf16[16,240,128]{2,1,0:T(8,128)(2,1)S(1)} async-done(((bf16[16,240,128]{2,1,0:T(8,128)(2,1)}), bf16[16,240,128]{2,1,0:T(8,128)(2,1)S(1)}, u32[]{:S(2)}, u32[]{:S(2)}) %all-to-all-start) | async-done | bytes 983072 | tf_op jit(solution)/shard_map/all_to_all | solution.py:914
  99.8 39.1 %all-gather.4.cloned.1.call-done = bf16[1408,7040]{1,0:T(8,128)(2,1)} async-done(((bf16[88,7040]{1,0:T(8,128)(2,1)}), bf16[1408,7040]{1,0:T(8,128)(2,1)}) %all-gather.4.cloned.1.call-update) | async-done | bytes 19824656 | tf_op jit(solution)/shard_map/all_gather | solution.py:966
  160.8 8.1 fusion.7
  170.4 8.7 all-to-all-start.1
  201.6 79.3 %all-gather.6.cloned.1.call-done = bf16[1408,4352]{1,0:T(8,128)(2,1)} async-done(((bf16[88,4352]{1,0:T(8,128)(2,1)}), bf16[1408,4352]{1,0:T(8,128)(2,1)}) %all-gather.6.cloned.1.call-update) | async-done | bytes 12255248 | tf_op jit(solution)/shard_map/all_gather | solution.py:1040
  288.5 15.6 %shard_map.488 = (bf16[16,2,88,128]{3,2,1,0:T(8,128)(2,1)S(1)}, f32[2,88,2048]{2,1,0:T(8,128)S(1)}, f32[2,1,2048]{2,1,0:T(1,128)S(1)}) custom-call(s32[2,2]{1,0:T(2,128)S(1)} %broadcast_select_fusion.7.ext_ref, bf16[16,2,3,88,128]{4,3,2,1,0:T(8,128)(2,1)S(1)} %all-to-all-done.1.qkv_ref, f32[88,2048]{1,0:T(8,128)S(1)} %copy-done.7, ...), custom_call_target="tpu_custom_call" | custom-call | flops 8858370048 | bytes 6291456 | tf_op jit(solution)/shard_map/pallas_call | solution.py:353
  318.0 16.2 %all-to-all-done.2 = bf16[16,2,88,128]{3,2,1,0:T(8,128)(2,1)S(1)} async-done(((bf16[16,2,88,128]{3,2,1,0:T(8,128)(2,1)}), bf16[16,2,88,128]{3,2,1,0:T(8,128)(2,1)S(1)}, u32[]{:S(2)}, u32[]{:S(2)}) %all-to-all-start.2) | async-done | bytes 720928 | tf_op jit(solution)/shard_map/all_to_all | solution.py:914
  338.9 35.2 %collective-permute-done.4 = bf16[1408,1408]{1,0:T(8,128)(2,1)} collective-permute-done((bf16[1408,1408]{1,0:T(8,128)(2,1)}, bf16[1408,1408]{1,0:T(8,128)(2,1)}, u32[]{:S(2)}, u32[]{:S(2)}) %collective-permute-start.4) | collective-permute-done | bytes 3964960 | tf_op jit(solution)/shard_map/ppermute | solution.py:143
  377.8 12.6 %shard_map.489 = (bf16[16,88,256]{2,1,0:T(8,128)(2,1)S(1)}, f32[16,1,256]{2,1,0:T(1,128)S(1)}) custom-call(s32[2,2]{1,0:T(2,128)S(1)} %copy-done.11, f32[16,88,256]{2,1,0:T(8,128)S(1)} %bitcast.326, bf16[2,16,88,768]{3,2,1,0:T(8,128)(2,1)S(1)} %bitcast.319, f32[88,256]{1,0:T(8,128)S(1)} %get-tuple-element.288.cos_ref, ...), custom_call_target="tpu_custom_call" | custom-call | flops 4294967296 | bytes 10485760 | tf_op jit(solution)/shard_map/pallas_call | solution.py:586
  406.2 7.7 slice.657
  413.9 7.8 pad_maximum_fusion
  421.7 9.4 fusion.49
  431.2 13.0 %convert_reduce_fusion = (bf16[3072]{0:T(1024)(128)(2,1)}, bf16[2,2,128,3072]{3,2,1,0:T(8,128)(2,1)}) fusion(f32[2,2,128,3072]{3,2,1,0:T(8,128)} %fusion.49, f32[3072]{0:T(1024)S(1)} %add.490, bf16[3072,1408,1,1]{1,0,3,2:T(8,128)(2,1)S(1)} %bitcast.348, bf16[1,2,128,1408]{3,2,1,0:T(8,128)(2,1)} %collective-permute-done.11, ...), kind=kOutput, calls=%fused_computation.30 | convolution fusion | flops 4466078720 | bytes 19548160 | tf_op jit(solution)/shard_map/dot_general | solution.py:45
  452.9 8.1 fusion.113
  474.3 10.4 %collective-permute-done.6 = bf16[1,2,128,1408]{3,2,1,0:T(8,128)(2,1)} collective-permute-done((bf16[1,2,128,1408]{3,2,1,0:T(8,128)(2,1)S(1)}, bf16[1,2,128,1408]{3,2,1,0:T(8,128)(2,1)}, u32[]{:S(2)}, u32[]{:S(2)}) %collective-permute-start.6) | collective-permute-done | bytes 720928 | tf_op jit(solution)/shard_map/ppermute | solution.py:113
  494.4 15.4 %shard_map.490 = (bf16[16,88,256]{2,1,0:T(8,128)(2,1)S(1)}, bf16[2,16,88,768]{3,2,1,0:T(8,128)(2,1)S(1)}, f32[8,88,2]{2,1,0:T(8,128)S(1)}) custom-call(s32[2,2]{1,0:T(2,128)S(1)} %copy-done.11, f32[16,88,256]{2,1,0:T(8,128)S(1)} %bitcast.327, bf16[2,16,88,768]{3,2,1,0:T(8,128)(2,1)S(1)} %bitcast.322, bf16[16,88,256]{2,1,0:T(8,128)(2,1)S(1)} %bitcast.328, ...), custom_call_target="tpu_custom_call" | custom-call | flops 8589934592 | bytes 16777216 | tf_op jit(solution)/shard_map/pallas_call | solution.py:606
  525.7 10.2 %bitcast_convert_fusion.1 = bf16[1408,3072]{1,0:T(8,128)(2,1)} fusion(bf16[2,2,128,3072]{3,2,1,0:T(8,128)(2,1)} %get-tuple-element.302, bf16[1,2,128,1408]{3,2,1,0:T(8,128)(2,1)} %collective-permute-done.5, bf16[1,2,128,1408]{3,2,1,0:T(8,128)(2,1)S(1)} %copy-done.76), kind=kOutput, calls=%fused_computation.2 | convolution fusion | flops 4434231296 | bytes 13238272 | tf_op jit(solution)/shard_map/dot_general | solution.py:45
  535.9 8.2 pad.24.refs_1_
  546.2 26.3 %shard_map.491 = (bf16[16,2,3,88,128]{4,3,2,1,0:T(8,128)(2,1)}, f32[2,88,4]{2,1,0:T(8,128)}) custom-call(s32[2,2]{1,0:T(2,128)} %copy-done.10, bf16[16,2,3,88,128]{4,3,2,1,0:T(8,128)(2,1)} %copy-done.5, bf16[16,2,88,128]{3,2,1,0:T(8,128)(2,1)} %copy-done.78, f32[2,88,2048]{2,1,0:T(8,128)} %copy-done.12, f32[2,1,2048]{2,1,0:T(1,128)} %copy-done.13, ...), custom_call_target="tpu_custom_call" | custom-call | flops 22145925120 | bytes 8388608 | tf_op jit(solution)/shard_map/pallas_call | solution.py:457
  577.4 11.4 %bitcast_convert_fusion = bf16[3072,1408]{1,0:T(8,128)(2,1)} fusion(bf16[1,2,128,1408]{3,2,1,0:T(8,128)(2,1)} %collective-permute-done.11, bf16[1,2,128,1408]{3,2,1,0:T(8,128)(2,1)} %copy-done.77, f32[2,2,128,3072]{3,2,1,0:T(8,128)} %fusion.49, f32[3072]{0:T(1024)S(1)} %add.490), kind=kOutput, calls=%fused_computation.1 | convolution fusion | flops 4449959936 | bytes 16396288 | tf_op jit(solution)/shard_map/dot_general | solution.py:45
  620.3 8.1 all-to-all-done.4
  630.2 7.4 fusion.115
  677.8 9.0 collective-permute-start.16
  735.4 206.7 %shard_map.492 = (bf16[704,1408]{1,0:T(8,128)(2,1)}, bf16[2,96,3072]{2,1,0:T(8,128)(2,1)}, bf16[2,192,1408]{2,1,0:T(8,128)(2,1)}) custom-call(bf16[16,704,1408]{2,1,0:T(8,128)(2,1)} %constant_dynamic-update-slice_fusion.18.refs_0_, bf16[16,96,3072]{2,1,0:T(8,128)(2,1)} %pad.24.refs_1_, bf16[16,192,1408]{2,1,0:T(8,128)(2,1)} %bitcast.355), custom_call_target="tpu_custom_call" | custom-call | flops 268435456 | bytes 268435456 | tf_op jit(solution)/shard_map/pallas_call | solution.py:896
  (779 shorter events, 364.5 us)
Async XLA Ops:
  7.2 131.7 %all-gather.4.cloned.1.call-start = ((), (), s32[]{:S(2)}) async-start(), calls=%async_computation.7 | async-start | bytes 21063680 | tf_op jit(solution)/shard_map/all_gather | solution.py:966
  13.2 38.2 %all-to-all-start = ((bf16[16,240,128]{2,1,0:T(8,128)(2,1)}), bf16[16,240,128]{2,1,0:T(8,128)(2,1)S(1)}, u32[]{:S(2)}, u32[]{:S(2)}) async-start(bf16[16,240,128]{2,1,0:T(8,128)(2,1)} %broadcast_in_dim.192), calls=%async_computation | async-start | bytes 1966080 | tf_op jit(solution)/shard_map/all_to_all | solution.py:914
  20.6 260.3 %all-gather.6.cloned.1.call-start = ((), (), s32[]{:S(2)}) async-start(), calls=%async_computation.8 | async-start | bytes 13021184 | tf_op jit(solution)/shard_map/all_gather | solution.py:1040
  56.4 343.8 %all-gather.8.cloned.1.call-start = ((), (), s32[]{:S(2)}) async-start(), calls=%async_computation.9 | async-start | bytes 19218432 | tf_op jit(solution)/shard_map/all_gather | solution.py:1059
  170.4 116.4 %all-to-all-start.1 = ((bf16[16,2,3,88,128]{4,3,2,1,0:T(8,128)(2,1)}), bf16[16,2,3,88,128]{4,3,2,1,0:T(8,128)(2,1)S(1)}, u32[]{:S(2)}, u32[]{:S(2)}) async-start(bf16[16,2,3,88,128]{4,3,2,1,0:T(8,128)(2,1)} %bitcast.354), calls=%async_computation.1 | async-start | bytes 4325376 | tf_op jit(solution)/shard_map/all_to_all | solution.py:914
  285.3 88.8 %collective-permute-start.4 = (bf16[1408,1408]{1,0:T(8,128)(2,1)}, bf16[1408,1408]{1,0:T(8,128)(2,1)}, u32[]{:S(2)}, u32[]{:S(2)}) collective-permute-start(bf16[1408,1408]{1,0:T(8,128)(2,1)} %slice.646), channel_id=1, source_target_pairs={{0,16},{16,0},{1,17},{17,1},{2,18},{18,2},{3,19},{19,3},{4,20},{20... | collective-permute-start | bytes 11894792 | tf_op jit(solution)/shard_map/ppermute | solution.py:143
  306.2 28.1 %all-to-all-start.2 = ((bf16[16,2,88,128]{3,2,1,0:T(8,128)(2,1)}), bf16[16,2,88,128]{3,2,1,0:T(8,128)(2,1)S(1)}, u32[]{:S(2)}, u32[]{:S(2)}) async-start(bf16[16,2,88,128]{3,2,1,0:T(8,128)(2,1)} %copy-done.8), calls=%async_computation.2 | async-start | bytes 1441792 | tf_op jit(solution)/shard_map/all_to_all | solution.py:914
  312.4 118.8 %collective-permute-start.11 = (bf16[1,2,128,1408]{3,2,1,0:T(8,128)(2,1)S(1)}, bf16[1,2,128,1408]{3,2,1,0:T(8,128)(2,1)}, u32[]{:S(2)}, u32[]{:S(2)}) collective-permute-start(bf16[1,2,128,1408]{3,2,1,0:T(8,128)(2,1)S(1)} %convert_bitcast_fusion.1), channel_id=1, source_target_pairs={{0,16},{16,0},{1,17},{17,1},{2,18},{18,2},{3,19},{19,3},{4,20},{20... | collective-permute-start | bytes 2162696 | tf_op jit(solution)/shard_map/ppermute | solution.py:113
  398.6 23.1 %collective-permute-start.5 = (bf16[1,2,128,1408]{3,2,1,0:T(8,128)(2,1)S(1)}, bf16[1,2,128,1408]{3,2,1,0:T(8,128)(2,1)}, u32[]{:S(2)}, u32[]{:S(2)}) collective-permute-start(bf16[1,2,128,1408]{3,2,1,0:T(8,128)(2,1)S(1)} %fusion.50), channel_id=1, source_target_pairs={{0,16},{16,0},{1,17},{17,1},{2,18},{18,2},{3,19},{19,3},{4,20},{20... | collective-permute-start | bytes 2162696 | tf_op jit(solution)/shard_map/ppermute | solution.py:113
  452.4 19.4 %collective-permute-start.12 = (bf16[1,2,128,1408]{3,2,1,0:T(8,128)(2,1)}, bf16[1,2,128,1408]{3,2,1,0:T(8,128)(2,1)S(1)}, u32[]{:S(2)}, u32[]{:S(2)}) collective-permute-start(bf16[1,2,128,1408]{3,2,1,0:T(8,128)(2,1)} %slice.814), channel_id=1, source_target_pairs={{0,16},{16,0},{1,17},{17,1},{2,18},{18,2},{3,19},{19,3},{4,20},{20... | collective-permute-start | bytes 2162696 | tf_op jit(solution)/shard_map/ppermute | solution.py:113
  462.5 22.2 %collective-permute-start.6 = (bf16[1,2,128,1408]{3,2,1,0:T(8,128)(2,1)S(1)}, bf16[1,2,128,1408]{3,2,1,0:T(8,128)(2,1)}, u32[]{:S(2)}, u32[]{:S(2)}) collective-permute-start(bf16[1,2,128,1408]{3,2,1,0:T(8,128)(2,1)S(1)} %slice.815), channel_id=1, source_target_pairs={{0,16},{16,0},{1,17},{17,1},{2,18},{18,2},{3,19},{19,3},{4,20},{20... | collective-permute-start | bytes 2162696 | tf_op jit(solution)/shard_map/ppermute | solution.py:113
  521.5 23.9 %all-to-all-start.3 = ((bf16[16,2,88,128]{3,2,1,0:T(8,128)(2,1)}), bf16[16,2,88,128]{3,2,1,0:T(8,128)(2,1)S(1)}, u32[]{:S(2)}, u32[]{:S(2)}) async-start(bf16[16,2,88,128]{3,2,1,0:T(8,128)(2,1)} %bitcast.313), calls=%async_computation.3 | async-start | bytes 1441792 | tf_op jit(solution)/shard_map/all_to_all | solution.py:914
  572.6 55.8 %all-to-all-start.4 = ((bf16[16,2,3,88,128]{4,3,2,1,0:T(8,128)(2,1)}), bf16[16,2,3,88,128]{4,3,2,1,0:T(8,128)(2,1)}, u32[]{:S(2)}, u32[]{:S(2)}) async-start(bf16[16,2,3,88,128]{4,3,2,1,0:T(8,128)(2,1)} %get-tuple-element.50), calls=%async_computation.4 | async-start | bytes 4325376 | tf_op jit(solution)/shard_map/all_to_all | solution.py:914
  577.4 116.7 %reduce-scatter.2.cloned.1.call-start = ((), (), s32[]{:S(2)}) async-start(), calls=%async_computation.10 | async-start | bytes 4595712 | tf_op jit(solution)/shard_map/reduce_scatter | solution.py:141
  589.5 16.4 %collective-permute-start.8 = (f32[2,1,8,144]{3,2,1,0:T(8,128)S(1)}, f32[2,1,8,144]{3,2,1,0:T(8,128)S(1)}, u32[]{:S(2)}, u32[]{:S(2)}) collective-permute-start(f32[2,1,8,144]{3,2,1,0:T(8,128)S(1)} %get-tuple-element.251), channel_id=1, source_target_pairs={{4,0},{8,4},{12,8},{5,1},{9,5},{13,9},{6,2},{10,6},{14,10},{7,3},{... | collective-permute-start | bytes 27656 | tf_op jit(solution)/shard_map/ppermute | solution.py:39
  590.9 15.0 %collective-permute-start.7 = (f32[2,1,8,144]{3,2,1,0:T(8,128)S(1)}, f32[2,1,8,144]{3,2,1,0:T(8,128)S(1)}, u32[]{:S(2)}, u32[]{:S(2)}) collective-permute-start(f32[2,1,8,144]{3,2,1,0:T(8,128)S(1)} %get-tuple-element.250), channel_id=1, source_target_pairs={{0,4},{4,8},{8,12},{1,5},{5,9},{9,13},{2,6},{6,10},{10,14},{3,7},{... | collective-permute-start | bytes 27656 | tf_op jit(solution)/shard_map/ppermute | solution.py:36
  649.6 28.1 %collective-permute-start.14 = (f32[2,1,8,144]{3,2,1,0:T(8,128)S(1)}, f32[2,1,8,144]{3,2,1,0:T(8,128)S(1)}, u32[]{:S(2)}, u32[]{:S(2)}) collective-permute-start(f32[2,1,8,144]{3,2,1,0:T(8,128)S(1)} %get-tuple-element.249), channel_id=1, source_target_pairs={{4,0},{8,4},{12,8},{5,1},{9,5},{13,9},{6,2},{10,6},{14,10},{7,3},{... | collective-permute-start | bytes 27656 | tf_op jit(solution)/shard_map/ppermute | solution.py:39
  650.9 26.8 %collective-permute-start.13 = (f32[2,1,8,144]{3,2,1,0:T(8,128)S(1)}, f32[2,1,8,144]{3,2,1,0:T(8,128)S(1)}, u32[]{:S(2)}, u32[]{:S(2)}) collective-permute-start(f32[2,1,8,144]{3,2,1,0:T(8,128)S(1)} %get-tuple-element.248), channel_id=1, source_target_pairs={{0,4},{4,8},{8,12},{1,5},{5,9},{9,13},{2,6},{6,10},{10,14},{3,7},{... | collective-permute-start | bytes 27656 | tf_op jit(solution)/shard_map/ppermute | solution.py:36
  677.8 12.6 %collective-permute-start.16 = (f32[2,18,1,144]{3,2,1,0:T(1,128)S(1)}, f32[2,18,1,144]{3,2,1,0:T(1,128)S(1)}, u32[]{:S(2)}, u32[]{:S(2)}) collective-permute-start(f32[2,18,1,144]{3,2,1,0:T(1,128)S(1)} %get-tuple-element.234), channel_id=1, source_target_pairs={{0,1},{1,2},{2,3},{4,5},{5,6},{6,7},{8,9},{9,10},{10,11},{12,13},{... | collective-permute-start | bytes 62216 | tf_op jit(solution)/shard_map/ppermute | solution.py:36
  705.8 29.4 %all-to-all-start.5 = ((bf16[16,240,128]{2,1,0:T(8,128)(2,1)}), bf16[16,240,128]{2,1,0:T(8,128)(2,1)S(1)}, u32[]{:S(2)}, u32[]{:S(2)}) async-start(bf16[16,240,128]{2,1,0:T(8,128)(2,1)} %bitcast.370), calls=%async_computation.6 | async-start | bytes 1966080 | tf_op jit(solution)/shard_map/all_to_all | solution.py:914
  710.3 19.2 %collective-permute-start.19 = (bf16[1024,176]{0,1:T(8,128)(2,1)S(1)}, bf16[1024,176]{0,1:T(8,128)(2,1)S(1)}, u32[]{:S(2)}, u32[]{:S(2)}) collective-permute-start(bf16[1024,176]{0,1:T(8,128)(2,1)S(1)} %fusion.44), channel_id=1, source_target_pairs={{0,16},{16,0},{1,17},{17,1},{2,18},{18,2},{3,19},{19,3},{4,20},{20... | collective-permute-start | bytes 1081352 | tf_op jit(solution)/shard_map/ppermute | solution.py:113
  710.4 18.5 %collective-permute-start.20 = (f32[176]{0:T(256)S(1)}, f32[176]{0:T(256)S(1)}, u32[]{:S(2)}, u32[]{:S(2)}) collective-permute-start(f32[176]{0:T(256)S(1)} %convert_reduce_fusion.3), channel_id=1, source_target_pairs={{0,16},{16,0},{1,17},{17,1},{2,18},{18,2},{3,19},{19,3},{4,20},{20... | collective-permute-start | bytes 2120 | tf_op jit(solution)/shard_map/ppermute | solution.py:113
  945.4 20.7 %collective-permute-start.17 = (f32[27532]{0:T(1024)S(1)}, f32[27532]{0:T(1024)}, u32[]{:S(2)}, u32[]{:S(2)}) collective-permute-start(f32[27532]{0:T(1024)S(1)} %slice.693), channel_id=1, source_target_pairs={{0,16},{16,0},{1,17},{17,1},{2,18},{18,2},{3,19},{19,3},{4,20},{20... | collective-permute-start | bytes 330392 | tf_op jit(solution)/shard_map/ppermute | solution.py:113
  948.4 24.3 %collective-permute-start.18 = (f32[88,1408]{1,0:T(8,128)}, f32[88,1408]{1,0:T(8,128)}, u32[]{:S(2)}, u32[]{:S(2)}) collective-permute-start(f32[88,1408]{1,0:T(8,128)} %fusion.105), channel_id=1, source_target_pairs={{0,16},{16,0},{1,17},{17,1},{2,18},{18,2},{3,19},{19,3},{4,20},{20... | collective-permute-start | bytes 1486856 | tf_op jit(solution)/shard_map/ppermute | solution.py:113
  (196 other events, 2256.5 us)
Sparse Core Ops, SparseCore 0:
  11.1 127.8 all-gather.3
  141.7 139.1 all-gather.5
  282.5 110.9 all-gather.7
  594.4 73.7 reduce-scatter.1
